TPU v7x, 128 devices: a whole 4x4x4 slice. The times are simulated.
128 devices in a mesh: row: 8 (over x_hi, y), col: 16 (over z, x_lo, core).
Axes of the slice: x: 4 (x_hi: 2, x_lo: 2; x = x_hi * 2 + x_lo), y: 4, z: 4, core: 2. Of those that a mesh axis runs over, the one named last changes fastest.
Arguments:
- tokens: bfloat16 [768, 8192], P('row', 'col'), may hold values from -6 to 6
- cotangent: bfloat16 [768, 8192], P('row', 'col'), may hold values from -6 to 6
- gate_weight: bfloat16 [8192, 14336], P('col', 'row'), may hold values from -0.09375 to 0.09375
- up_weight: bfloat16 [8192, 14336], P('col', 'row'), may hold values from -0.09375 to 0.09375
- down_weight: bfloat16 [14336, 8192], P('row', 'col'), may hold values from -0.0625 to 0.0625
- gate_mask: int32 [64, 112], P('col', 'row'), may hold values from 0 to 1, as said below
- up_mask: int32 [64, 112], P('col', 'row'), may hold values from 0 to 1, as said below
- down_mask: int32 [112, 64], P('row', 'col'), may hold values from 0 to 1, as said below
Outputs:
- layer_out: bfloat16 [768, 8192], P('row', 'col')
- input_grad: bfloat16 [768, 8192], P('row', 'col')
- gate_weight_grad: bfloat16 [8192, 14336], P('col', 'row')
- up_weight_grad: bfloat16 [8192, 14336], P('col', 'row')
- down_weight_grad: bfloat16 [14336, 8192], P('row', 'col')
Inputs may be any that keep to these rules, and one draw needn't show every extreme that they name: `gate_mask`: 1 keeps a 128 x 128 block of the weight, 0 prunes it. `up_mask`: 1 keeps a 128 x 128 block of the weight, 0 prunes it. `down_mask`: 1 keeps a 128 x 128 block of the weight, 0 prunes it.
All inputs are finite; a program needn't handle non-finite values.
Results may differ from a plain program's by a relative error of at most 0.005.
Values may be sent and summed in bfloat16 or wider, within the bound.
No kernel may reach another device: no remote copies, remote signals or barrier semaphores. Data moves between devices by JAX's collectives and lax.ppermute only.
A program may use at most 128 MiB of HBM per device.

v0:
```python
import jax
import jax.numpy as jnp
from jax import lax
from jax.sharding import PartitionSpec as P

BLK = 128


def expand(block_mask):
    return jnp.repeat(jnp.repeat(block_mask, BLK, axis=0), BLK, axis=1)


def pointwise(summed, hidden_width):
    gate_proj = summed[:, :hidden_width]
    up_proj = summed[:, hidden_width : 2 * hidden_width]
    hidden_grad = summed[:, 2 * hidden_width :]
    sigmoid_gate = jax.nn.sigmoid(gate_proj)
    silu_gate = gate_proj * sigmoid_gate
    hidden = (silu_gate * up_proj).astype(jnp.bfloat16)
    gate_grad = (
        hidden_grad * up_proj * sigmoid_gate * (1.0 + gate_proj * (1.0 - sigmoid_gate))
    ).astype(jnp.bfloat16)
    up_grad = (hidden_grad * silu_gate).astype(jnp.bfloat16)
    return (hidden, gate_grad, up_grad)


def per_device(
    tokens, cotangent, gate_weight, up_weight, down_weight, gate_mask, up_mask, down_mask
):
    gate_full = expand(gate_mask)
    up_full = expand(up_mask)
    down_full = expand(down_mask)
    gate_eff = gate_weight * gate_full.astype(jnp.bfloat16)
    up_eff = up_weight * up_full.astype(jnp.bfloat16)
    down_eff = down_weight * down_full.astype(jnp.bfloat16)
    hidden_width = gate_eff.shape[1]
    token_panel, grad_panel = (
        lax.all_gather(tokens, "row", axis=0, tiled=True),
        lax.all_gather(cotangent, "row", axis=0, tiled=True),
    )
    trans_right = (((1,), (1,)), ((), ()))
    trans_left = (((0,), (0,)), ((), ()))
    gate_part = jnp.dot(token_panel, gate_eff, preferred_element_type=jnp.float32)
    up_part = jnp.dot(token_panel, up_eff, preferred_element_type=jnp.float32)
    hidden_part = lax.dot_general(
        grad_panel, down_eff, trans_right, preferred_element_type=jnp.float32
    )
    summed = lax.psum(jnp.concatenate([gate_part, up_part, hidden_part], axis=1), "col")
    hidden_all, gate_all, up_all = pointwise(summed, hidden_width)
    out_term = jnp.dot(hidden_all, down_eff, preferred_element_type=jnp.float32)
    input_term = lax.dot_general(
        gate_all, gate_eff, trans_right, preferred_element_type=jnp.float32
    )
    input_term = input_term + lax.dot_general(
        up_all, up_eff, trans_right, preferred_element_type=jnp.float32
    )
    out_sum, input_sum = (
        lax.psum_scatter(out_term, "row", scatter_dimension=0, tiled=True),
        lax.psum_scatter(input_term, "row", scatter_dimension=0, tiled=True),
    )
    gate_weight_grad = (
        lax.dot_general(token_panel, gate_all, trans_left, preferred_element_type=jnp.float32)
        * gate_full.astype(jnp.float32)
    ).astype(jnp.bfloat16)
    up_weight_grad = (
        lax.dot_general(token_panel, up_all, trans_left, preferred_element_type=jnp.float32)
        * up_full.astype(jnp.float32)
    ).astype(jnp.bfloat16)
    down_weight_grad = (
        lax.dot_general(hidden_all, grad_panel, trans_left, preferred_element_type=jnp.float32)
        * down_full.astype(jnp.float32)
    ).astype(jnp.bfloat16)
    return (
        out_sum.astype(jnp.bfloat16),
        input_sum.astype(jnp.bfloat16),
        gate_weight_grad,
        up_weight_grad,
        down_weight_grad,
    )


def solution(mesh):
    placed = (
        P("row", "col"),
        P("row", "col"),
        P("col", "row"),
        P("col", "row"),
        P("row", "col"),
        P("col", "row"),
        P("col", "row"),
        P("row", "col"),
    )
    return jax.shard_map(
        per_device,
        mesh=mesh,
        in_specs=placed,
        out_specs=(
            P("row", "col"),
            P("row", "col"),
            P("col", "row"),
            P("col", "row"),
            P("row", "col"),
        ),
        check_vma=False,
    )
```

profile of v0, /device:TPU:0, one launch (start us, length us, event | category | flops | bytes accessed | tf_op | source)
XLA Modules:
  0.0 642.8 jit_solution(16353552849639424666)
XLA Ops:
  7.2 36.5 %all_gather.6 = bf16[768,512]{1,0:T(8,128)(2,1)S(1)} all-gather(bf16[96,512]{1,0:T(8,128)(2,1)} %param.8), channel_id=1, replica_groups=mesh['row'=8,'col'=16] {'row'}, dimensions={0}, use_global_device_ids=true | all-gather | bytes 884736 | tf_op jit(solution)/shard_map/all_gather | solution.py:38
  43.7 0.8 fusion.6
  44.7 2.8 copy.22
  47.8 3.8 copy.20
  51.8 4.0 convolution_bitcast_fusion.1
  55.8 0.1 bitcast_multiply_fusion.5
  55.9 4.1 convolution_bitcast_fusion.2
  60.0 0.5 fusion.5
  60.7 35.8 %all_gather.7 = bf16[768,512]{1,0:T(8,128)(2,1)S(1)} all-gather(bf16[96,512]{1,0:T(8,128)(2,1)S(1)} %copy-done.10), channel_id=1, replica_groups=mesh['row'=8,'col'=16] {'row'}, dimensions={0}, use_global_device_ids=true | all-gather | bytes 884736 | tf_op jit(solution)/shard_map/all_gather | solution.py:39
  96.6 5.1 broadcast_in_dim.35
  101.7 1.2 copy-done
  102.9 1.7 convolution_bitcast_fusion
  104.7 6.5 %pad_maximum_fusion = f32[768,5376]{0,1:T(8,128)} fusion(f32[768,1792]{0,1:T(8,128)S(1)} %convolution_bitcast_fusion, f32[768,1792]{0,1:T(8,128)S(1)} %bitcast.75, f32[768,1792]{0,1:T(8,128)S(1)} %bitcast.77), kind=kLoop, calls=%fused_computation | loop fusion | flops 8257536 | bytes 33030144 | tf_op jit(solution)/shard_map/concatenate | solution.py:48
  111.3 360.3 %all-reduce.2.cloned.1.call-done = f32[768,5376]{0,1:T(8,128)} async-done(((f32[768,5376]{0,1:T(8,128)}), f32[768,5376]{0,1:T(8,128)}) %all-reduce.2.cloned.1.call-update) | async-done | bytes 16515088 | tf_op jit(solution)/shard_map/psum | solution.py:48
  471.6 7.3 %multiply_convert_fusion = (bf16[768,1792]{0,1:T(8,128)(2,1)S(1)}, bf16[768,1792]{0,1:T(8,128)(2,1)S(1)}, bf16[768,1792]{0,1:T(8,128)(2,1)S(1)}) fusion(f32[768,5376]{0,1:T(8,128)} %all-reduce.2.cloned.1.call-done), kind=kLoop, calls=%fused_computation.1 | loop fusion | flops 20643840 | bytes 24772608 | tf_op jit(solution)/shard_map/convert_element_type | solution.py:23
  478.9 4.6 fusion.8
  483.5 2.9 convolution_add_fusion
  486.4 0.2 reduce-scatter.3.cloned.1.call-start
  486.6 4.8 fusion.4
  491.7 0.6 copy.32
  492.5 0.6 copy.33
  493.1 0.7 copy.26
  493.8 4.7 fusion.3
  498.5 3.8 copy.27
  502.3 4.6 fusion.2
  506.9 3.8 copy.28
  510.8 2.2 broadcast_in_dim.41
  513.0 2.8 fusion.1
  515.8 42.8 %reduce-scatter.5.cloned.1.call-done = f32[96,512]{1,0:T(8,128)} async-done(((f32[768,512]{1,0:T(8,128)}), f32[96,512]{1,0:T(8,128)}) %reduce-scatter.5.cloned.1.call-update) | async-done | bytes 196624 | tf_op jit(solution)/shard_map/reduce_scatter | solution.py:59
  558.6 1.6 convert_element_type.103
  560.2 74.5 %reduce-scatter.3.cloned.1.call-done = f32[96,512]{1,0:T(8,128)} async-done(((f32[768,512]{1,0:T(8,128)}), f32[96,512]{1,0:T(8,128)}) %reduce-scatter.3.cloned.1.call-update) | async-done | bytes 196624 | tf_op jit(solution)/shard_map/reduce_scatter | solution.py:58
  634.7 1.6 convert_element_type.100
  (59 shorter events, 1.3 us)
Async XLA Ops:
  7.2 40.3 %copy-start.11 = (s32[4,14]{1,0:T(4,128)S(1)}, s32[4,14]{1,0:T(4,128)}, u32[]{:S(2)}) copy-start(s32[4,14]{1,0:T(4,128)} %param.13) | copy-start | bytes 676
  7.2 464.4 %all-reduce.2.cloned.1.call-start = ((), (), s32[]{:S(2)}) async-start(), calls=%async_computation.2 | async-start | bytes 33030144 | tf_op jit(solution)/shard_map/psum | solution.py:48
  51.7 4.0 copy-start.5
  51.7 4.0 copy-start.7
  55.9 4.1 copy-start.2
  55.9 4.1 copy-start.12
  55.9 4.8 copy-start.10
  60.0 42.9 %copy-start.3 = (bf16[1792,512]{1,0:T(8,128)(2,1)S(1)}, bf16[1792,512]{1,0:T(8,128)(2,1)}, u32[]{:S(2)}) copy-start(bf16[1792,512]{1,0:T(8,128)(2,1)} %param.12) | copy-start | bytes 5505028
  96.5 5.2 copy-start.8
  96.5 8.1 %slice-start = ((s8[5505024]{0:T(1024)(128)(4,1)}), s8[4194304]{0:T(1024)(128)(4,1)S(1)}, s32[]{:S(2)}) async-start(s8[5505024]{0:T(1024)(128)(4,1)} %bitcast.74), calls=%async_computation.5 | async-start | bytes 8388608
  96.6 8.1 %slice-start.2 = ((s8[5505024]{0:T(1024)(128)(4,1)}), s8[4194304]{0:T(1024)(128)(4,1)S(1)}, s32[]{:S(2)}) async-start(s8[5505024]{0:T(1024)(128)(4,1)} %bitcast.76), calls=%async_computation.7 | async-start | bytes 8388608
  101.7 1.2 copy-start
  102.9 1.7 slice-start.1
  102.9 1.7 slice-start.3
  111.2 447.4 %reduce-scatter.5.cloned.1.call-start = ((), (), s32[]{:S(2)}) async-start(), calls=%async_computation.4 | async-start | bytes 1769472 | tf_op jit(solution)/shard_map/reduce_scatter | solution.py:59
  478.8 4.7 copy-start.1
  478.8 4.7 copy-start.4
  478.8 4.7 copy-start.6
  486.4 148.2 %reduce-scatter.3.cloned.1.call-start = ((), (), s32[]{:S(2)}) async-start(), calls=%async_computation.3 | async-start | bytes 1769472 | tf_op jit(solution)/shard_map/reduce_scatter | solution.py:58
  510.7 2.3 copy-start.9
Sparse Core Ops, SparseCore 0:
  111.3 360.1 all-reduce.1
  486.5 72.0 reduce-scatter.4
  562.3 72.3 reduce-scatter.2
where the time goes:
time: 643 us
  waiting for transfers between devices  478 us (74%)
  blocking collectives  72.3 us (11%)
  matrix products  34.2 us (5%)
  local copies, waits for them, and re-layouts  25.8 us (4%)
  other arithmetic  18.5 us (3%)
  between operations  14.1 us (2%)
    psum x1, waiting for transfers between devices, per_device(): lax.psum(jnp.concatenate([gate_part, up_part, hidden_part], axis=1), 'col')  360 us
    reduce_scatter x1, waiting for transfers between devices, per_device(): lax.psum_scatter(out_term, 'row', scatter_dimension=0, tiled=True)  74.5 us
    reduce_scatter x1, waiting for transfers between devices, per_device(): lax.psum_scatter(input_term, 'row', scatter_dimension=0, tiled=True)  42.8 us
    all_gather x1, blocking collectives, per_device(): lax.all_gather(tokens, 'row', axis=0, tiled=True)  36.5 us
    all_gather x1, blocking collectives, per_device(): lax.all_gather(cotangent, 'row', axis=0, tiled=True)  35.8 us
    unnamed x50, local copies, waits for them, and re-layouts  17.2 us
  transfers between devices with their start and end apart: 3, of which 3 were waited for; matrix products, arithmetic and copies ran while one was open for 5% of the time, Pallas kernels for 0%

commit v1 on v0

v1 whole, which is shorter than its diff:
```python
import jax
import jax.numpy as jnp
from jax import lax
from jax.sharding import PartitionSpec as P

BLK = 128
BF = jnp.bfloat16
F32 = jnp.float32

GRAY = ((0, 0), (1, 0), (1, 1), (0, 1))
RING = {bits: pos for pos, bits in enumerate(GRAY)}
AXIS = {"A": 0, "B": 1, "X": 2}
ORDERS = ("ABX", "BXA", "XAB")


def flip_ring(pos, dim):
    bits = list(GRAY[pos])
    bits[dim] ^= 1
    return RING[tuple(bits)]


def col_perm(dim):
    pairs = []
    for i in range(16):
        z, x, c = i // 4, (i // 2) % 2, i % 2
        if dim in "AB":
            z = flip_ring(z, AXIS[dim])
        elif dim == "X":
            x ^= 1
        else:
            c ^= 1
        pairs.append((i, (z * 2 + x) * 2 + c))
    return pairs


def row_perm(dim):
    pairs = []
    for i in range(8):
        x, y = i // 4, i % 4
        if dim in "AB":
            y = flip_ring(y, AXIS[dim])
        else:
            x ^= 1
        pairs.append((i, x * 4 + y))
    return pairs


def swap_col(value, dim):
    return lax.ppermute(value, "col", col_perm(dim))


def swap_row(value, dim):
    return lax.ppermute(value, "row", row_perm(dim))


def ring_bits(pos):
    return ((pos == 1) | (pos == 2)).astype(jnp.int32), (pos >= 2).astype(jnp.int32)


def place(row):
    bit_a, bit_b = ring_bits(row % 4)
    return bit_a * 4 + bit_b * 2 + row // 4


def take(value, axis, index):
    return lax.dynamic_index_in_dim(value, index, axis, keepdims=True)


def halve(parts, bits, swap, types):
    parts = list(parts)
    for step in range(3):
        got = []
        for i, part in enumerate(parts):
            dim = ORDERS[i][step]
            got.append(swap(take(part, AXIS[dim], 1 - bits[dim]).astype(types[step]), dim))
        for i, part in enumerate(parts):
            dim = ORDERS[i][step]
            parts[i] = take(part, AXIS[dim], bits[dim]) + got[i].astype(F32)
    return [part[0, 0, 0] for part in parts]


def double(parts, bits, swap):
    rows = parts[0].shape[0]
    parts = [part[None, None, None] for part in parts]
    for step in range(3):
        got = [swap(part, ORDERS[i][step]) for i, part in enumerate(parts)]
        for i, part in enumerate(parts):
            dim = ORDERS[i][step]
            first = jnp.where(bits[dim] == 0, part, got[i])
            second = jnp.where(bits[dim] == 0, got[i], part)
            parts[i] = jnp.concatenate([first, second], axis=AXIS[dim])
    return [part.reshape(8 * rows, -1) for part in parts]


def pointwise(gate_proj, up_proj, hidden_grad):
    sigmoid_gate = jax.nn.sigmoid(gate_proj)
    silu_gate = gate_proj * sigmoid_gate
    hidden = (silu_gate * up_proj).astype(BF)
    gate_grad = (
        hidden_grad * up_proj * sigmoid_gate * (1.0 + gate_proj * (1.0 - sigmoid_gate))
    ).astype(BF)
    up_grad = (hidden_grad * silu_gate).astype(BF)
    return hidden, gate_grad, up_grad


def expand(block_mask):
    return jnp.repeat(jnp.repeat(block_mask, BLK, axis=0), BLK, axis=1)


def dot(a, b, dims):
    return lax.dot_general(a, b, (dims, ((), ())), preferred_element_type=F32)


NN = ((1,), (0,))
NT = ((1,), (1,))
TN = ((0,), (0,))


def per_device(
    tokens, cotangent, gate_weight, up_weight, down_weight, gate_mask, up_mask, down_mask
):
    col, row = lax.axis_index("col"), lax.axis_index("row")
    core = col % 2
    bit_a, bit_b = ring_bits(col // 4)
    col_bits = {"A": bit_a, "B": bit_b, "X": (col // 2) % 2}
    bit_a, bit_b = ring_bits(row % 4)
    row_bits = {"A": bit_a, "B": bit_b, "X": row // 4}

    gate_full = expand(gate_mask).astype(BF)
    up_full = expand(up_mask).astype(BF)
    down_full = expand(down_mask).astype(BF)
    gate_eff = gate_weight * gate_full
    up_eff = up_weight * up_full
    down_eff = down_weight * down_full
    half = gate_eff.shape[1] // 2
    width = tokens.shape[1]

    def trade(weight, axis):
        kept = lax.dynamic_slice_in_dim(weight, core * half, half, axis)
        sent = lax.dynamic_slice_in_dim(weight, (1 - core) * half, half, axis)
        return jnp.concatenate([kept, swap_col(sent, "C")], axis=1 - axis)

    both = jnp.concatenate([tokens, cotangent], axis=1)
    row_of = [swap_to(both, k) for k in range(1, 8)]
    panel = jnp.zeros((8,) + both.shape, BF)
    panel = lax.dynamic_update_index_in_dim(panel, both, place(row), 0)
    for k in range(1, 8):
        panel = lax.dynamic_update_index_in_dim(panel, row_of[k - 1], place(row ^ k), 0)
    panel = panel.reshape(-1, 2 * width)
    other = swap_col(panel, "C")
    token_panel = jnp.concatenate([panel[:, :width], other[:, :width]], axis=1)
    grad_panel = jnp.concatenate([panel[:, width:], other[:, width:]], axis=1)

    gate_eff = trade(gate_eff, 1)
    up_eff = trade(up_eff, 1)
    down_eff = trade(down_eff, 0)

    gate_part = dot(token_panel, gate_eff, NN)
    up_part = dot(token_panel, up_eff, NN)
    hidden_part = dot(grad_panel, down_eff, NT)
    cube = (2, 2, 2, gate_part.shape[0] // 8, half)
    sums = halve(
        [part.reshape(cube) for part in (gate_part, up_part, hidden_part)],
        col_bits,
        swap_col,
        (BF, BF, F32),
    )
    hidden_all, gate_all, up_all = double(pointwise(*sums), col_bits, swap_col)

    out_term = dot(hidden_all, down_eff, NN)
    input_term = dot(gate_all, gate_eff, NT) + dot(up_all, up_eff, NT)
    out_term = out_term[:, :width] + swap_col(out_term[:, width:].astype(BF), "C").astype(F32)
    input_term = input_term[:, :width] + swap_col(input_term[:, width:].astype(BF), "C").astype(F32)
    terms = jnp.concatenate([out_term, input_term], axis=1)
    cuts = (0, 3 * width // 4, 6 * width // 4, 2 * width)
    cube = (2, 2, 2, terms.shape[0] // 8)
    sums = halve(
        [terms[:, a:b].reshape(cube + (b - a,)) for a, b in zip(cuts, cuts[1:])],
        row_bits,
        swap_row,
        (BF, BF, F32),
    )
    sums = jnp.concatenate(sums, axis=1)

    def give_back(grad, axis):
        kept = lax.slice_in_dim(grad, 0, width, axis=1 - axis)
        got = swap_col(lax.slice_in_dim(grad, width, 2 * width, axis=1 - axis), "C")
        first = jnp.where(core == 0, kept, got)
        second = jnp.where(core == 0, got, kept)
        return jnp.concatenate([first, second], axis=axis)

    gate_weight_grad = give_back(dot(token_panel, gate_all, TN).astype(BF), 1) * gate_full
    up_weight_grad = give_back(dot(token_panel, up_all, TN).astype(BF), 1) * up_full
    down_weight_grad = give_back(dot(hidden_all, grad_panel, TN).astype(BF), 0) * down_full
    return (
        sums[:, :width].astype(BF),
        sums[:, width:].astype(BF),
        gate_weight_grad,
        up_weight_grad,
        down_weight_grad,
    )


def swap_to(value, k):
    return lax.ppermute(value, "row", [(i, i ^ k) for i in range(8)])


def solution(mesh):
    placed = (
        P("row", "col"),
        P("row", "col"),
        P("col", "row"),
        P("col", "row"),
        P("row", "col"),
        P("col", "row"),
        P("col", "row"),
        P("row", "col"),
    )
    return jax.shard_map(
        per_device,
        mesh=mesh,
        in_specs=placed,
        out_specs=(
            P("row", "col"),
            P("row", "col"),
            P("col", "row"),
            P("col", "row"),
            P("row", "col"),
        ),
        check_vma=False,
    )
```

time: 643 us -> 198 us (0.31)
  waiting for transfers between devices: 478 us -> 68.5 us
  blocking collectives: 72.3 us -> 0 us
  starting transfers between devices: 0.3 us -> 48.3 us
  between operations: 14.1 us -> 1.56 us
  local copies, waits for them, and re-layouts: 25.8 us -> 37.4 us
  matrix products: 34.2 us -> 23.2 us
    psum x1 -> x0, waiting for transfers between devices: 360 us -> none  [per_device(): lax.psum(jnp.concatenate([gate_part, up_part, hidden_part], axis=1), 'col')]
    reduce_scatter x2 -> x0, waiting for transfers between devices: 117 us -> none  [the longest x1 74.5 us: per_device(): lax.psum_scatter(out_term, 'row', scatter_dimension=0, tiled=True)]
    all_gather x2 -> x0, blocking collectives: 72.3 us -> none  [the longest x1 36.5 us: per_device(): lax.all_gather(tokens, 'row', axis=0, tiled=True)]
    ppermute x0 -> x43, waiting for transfers between devices: none -> 68.5 us  [the longest x27 51.5 us: swap_col(): return lax.ppermute(value, 'col', col_perm(dim))]
    ppermute x0 -> x43, starting transfers between devices: none -> 48.3 us  [the longest x27 22.3 us: swap_col(): return lax.ppermute(value, 'col', col_perm(dim))]
    dot_general x9, matrix products: 34.2 us -> 23.2 us  [dot(): return lax.dot_general(a, b, (dims, ((), ())), preferred_element_type=F32)]
    convert_element_type x6 -> x4, other arithmetic: 11.7 us -> 1.02 us  [the longest x1 1 us: pointwise(): hidden = (silu_gate * up_proj).astype(BF)]
    mul x2 -> x6, other arithmetic: 0.25 us -> 6.93 us  [the longest x1 1.75 us: per_device(): give_back(dot(hidden_all, grad_panel, TN).astype(BF), 0) * down_full]
  transfers between devices with their start and end apart: 3 -> 43, of which waited for: 3 -> 20; matrix products, arithmetic and copies ran while one was open for 5% -> 36% of each run, Pallas kernels for 0% -> 0%
where the time goes in v1:
time: 198 us; the launch traced here: 197 us
  waiting for transfers between devices  68.5 us (35%)
  starting transfers between devices  48.3 us (24%)
  local copies, waits for them, and re-layouts  37.4 us (19%)
  matrix products  23.2 us (12%)
  other arithmetic  18.1 us (9%)
    ppermute x27, waiting for transfers between devices, swap_col(): return lax.ppermute(value, 'col', col_perm(dim))  51.5 us
    dot_general x9, matrix products, dot(): return lax.dot_general(a, b, (dims, ((), ())), preferred_element_type=F32)  23.2 us
    ppermute x27, starting transfers between devices, swap_col(): return lax.ppermute(value, 'col', col_perm(dim))  22.3 us
    unnamed x53, local copies, waits for them, and re-layouts  15.4 us
    ppermute x7, starting transfers between devices, swap_to(): return lax.ppermute(value, 'row', [(i, i ^ k) for i in range(8)])  14.9 us
    ppermute x9, waiting for transfers between devices, swap_row(): return lax.ppermute(value, 'row', row_perm(dim))  11.5 us
    ppermute x9, starting transfers between devices, swap_row(): return lax.ppermute(value, 'row', row_perm(dim))  11.1 us
    ppermute x7, waiting for transfers between devices, swap_to(): return lax.ppermute(value, 'row', [(i, i ^ k) for i in range(8)])  5.58 us
  transfers between devices with their start and end apart: 43, of which 20 were waited for; matrix products, arithmetic and copies ran while one was open for 36% of the time, Pallas kernels for 0%

profile of v1, /device:TPU:0, one launch (start us, length us, event | category | flops | bytes accessed | tf_op | source)
XLA Modules:
  0.0 197.1 jit_solution(9210113396418794900)
XLA Ops:
  5.4 2.9 %collective-permute-start.1 = (bf16[96,1024]{1,0:T(8,128)(2,1)}, bf16[96,1024]{1,0:T(8,128)(2,1)}, u32[]{:S(2)}, u32[]{:S(2)}) collective-permute-start(bf16[96,1024]{1,0:T(8,128)(2,1)} %constant_dynamic-update-slice_fusion), channel_id=1, source_target_pairs={{0,32},{16,48},{32,0},{48,16},{64,96},{80,112},{96,64},{112,80},{1... | collective-permute-start | bytes 589832 | tf_op jit(solution)/shard_map/ppermute | solution.py:205
  8.4 3.1 %collective-permute-start.3 = (bf16[96,1024]{1,0:T(8,128)(2,1)}, bf16[96,1024]{1,0:T(8,128)(2,1)}, u32[]{:S(2)}, u32[]{:S(2)}) collective-permute-start(bf16[96,1024]{1,0:T(8,128)(2,1)} %constant_dynamic-update-slice_fusion), channel_id=1, source_target_pairs={{0,64},{16,80},{32,96},{48,112},{64,0},{80,16},{96,32},{112,48},{1... | collective-permute-start | bytes 589832 | tf_op jit(solution)/shard_map/ppermute | solution.py:205
  11.8 2.8 %copy.16 = bf16[512,1792]{0,1:T(8,128)(2,1)S(1)} copy(bf16[512,1792]{1,0:T(8,128)(2,1)} %param.11) | data formatting | bytes 3670016 | tf_op args[3]
  17.6 6.7 %collective-permute-start.5 = (bf16[96,1024]{1,0:T(8,128)(2,1)}, bf16[96,1024]{1,0:T(8,128)(2,1)S(1)}, u32[]{:S(2)}, u32[]{:S(2)}) collective-permute-start(bf16[96,1024]{1,0:T(8,128)(2,1)} %constant_dynamic-update-slice_fusion), channel_id=1, source_target_pairs={{0,96},{16,112},{32,64},{48,80},{64,32},{80,48},{96,0},{112,16},{1... | collective-permute-start | bytes 589832 | tf_op jit(solution)/shard_map/ppermute | solution.py:205
  29.4 5.3 %collective-permute-done.6 = bf16[96,1024]{1,0:T(8,128)(2,1)S(1)} collective-permute-done((bf16[96,1024]{1,0:T(8,128)(2,1)}, bf16[96,1024]{1,0:T(8,128)(2,1)S(1)}, u32[]{:S(2)}, u32[]{:S(2)}) %collective-permute-start.6) | collective-permute-done | bytes 196640 | tf_op jit(solution)/shard_map/ppermute | solution.py:205
  36.7 2.8 %copy.14 = bf16[512,1792]{0,1:T(8,128)(2,1)S(1)} copy(bf16[512,1792]{1,0:T(8,128)(2,1)} %param.10) | data formatting | bytes 3670016 | tf_op args[2]
  42.0 5.1 %broadcast_in_dim.63 = bf16[1792,4,128]{2,1,0:T(4,128)(2,1)S(1)} broadcast(bf16[1792,4]{1,0:T(8,128)(2,1)S(1)} %bitcast.71), dimensions={0,1} | broadcast | bytes 1849344 | tf_op jit(solution)/shard_map/broadcast_in_dim | solution.py:107
  53.0 3.2 %fusion.3 = f32[768,896]{1,0:T(8,128)S(1)} fusion(bf16[512,896]{0,1:T(8,128)(2,1)} %collective-permute-done.12, bf16[512,896]{0,1:T(8,128)(2,1)S(1)} %copy-done.5, bf16[768,512]{1,0:T(8,128)(2,1)S(1)} %get-tuple-element.29, bf16[768,512]{1,0:T(8,128)(2,1)S(1)} %get-tuple-element.27), kind=kOutput, calls=%fused_computation.31 | convolution fusion | flops 1416101888 | bytes 6160384 | tf_op jit(solution)/shard_map/dot_general | solution.py:111
  56.3 4.1 %collective-permute-start.13 = (bf16[2,1,2,96,896]{4,3,2,1,0:T(8,128)(2,1)S(1)}, bf16[2,1,2,96,896]{4,3,2,1,0:T(8,128)(2,1)S(1)}, u32[]{:S(2)}, u32[]{:S(2)}) collective-permute-start(bf16[2,1,2,96,896]{4,3,2,1,0:T(8,128)(2,1)S(1)} %dynamic-slice_convert_fusion.1), channel_id=1, source_target_pairs={{0,12},{1,13},{2,14},{3,15},{4,8},{5,9},{6,10},{7,11},{8,4},{9,5},... | collective-permute-start | bytes 2064392 | tf_op jit(solution)/shard_map/ppermute | solution.py:49
  60.5 3.1 %fusion.4 = f32[768,896]{1,0:T(8,128)S(1)} fusion(bf16[512,896]{0,1:T(8,128)(2,1)} %collective-permute-done.8, bf16[512,896]{0,1:T(8,128)(2,1)S(1)} %copy-done.7, bf16[768,512]{1,0:T(8,128)(2,1)S(1)} %get-tuple-element.29, bf16[768,512]{1,0:T(8,128)(2,1)S(1)} %get-tuple-element.27), kind=kOutput, calls=%fused_computation.32 | convolution fusion | flops 1416101888 | bytes 6160384 | tf_op jit(solution)/shard_map/dot_general | solution.py:111
  63.8 3.0 %fusion = f32[768,896]{1,0:T(8,128)S(1)} fusion(bf16[896,512]{1,0:T(8,128)(2,1)} %collective-permute-done.19, bf16[896,512]{1,0:T(8,128)(2,1)S(1)} %copy-done.4, bf16[768,512]{1,0:T(8,128)(2,1)S(1)} %get-tuple-element.30, bf16[768,512]{1,0:T(8,128)(2,1)S(1)} %get-tuple-element.28), kind=kOutput, calls=%fused_computation.28 | convolution fusion | flops 1416101888 | bytes 6160384 | tf_op jit(solution)/shard_map/dot_general | solution.py:111
  67.5 8.5 %collective-permute-done.13 = bf16[2,1,2,96,896]{4,3,2,1,0:T(8,128)(2,1)S(1)} collective-permute-done((bf16[2,1,2,96,896]{4,3,2,1,0:T(8,128)(2,1)S(1)}, bf16[2,1,2,96,896]{4,3,2,1,0:T(8,128)(2,1)S(1)}, u32[]{:S(2)}, u32[]{:S(2)}) %collective-permute-start.13) | collective-permute-done | bytes 688160 | tf_op jit(solution)/shard_map/ppermute | solution.py:49
  77.1 3.7 %collective-permute-done.9 = bf16[1,2,2,96,896]{4,3,2,1,0:T(8,128)(2,1)S(1)} collective-permute-done((bf16[1,2,2,96,896]{4,3,2,1,0:T(8,128)(2,1)S(1)}, bf16[1,2,2,96,896]{4,3,2,1,0:T(8,128)(2,1)S(1)}, u32[]{:S(2)}, u32[]{:S(2)}) %collective-permute-start.9) | collective-permute-done | bytes 688160 | tf_op jit(solution)/shard_map/ppermute | solution.py:49
  81.4 3.9 %collective-permute-done.24 = bf16[2,2,1,96,896]{4,3,2,1,0:T(8,128)(2,1)S(1)} collective-permute-done((bf16[2,2,1,96,896]{4,3,2,1,0:T(8,128)(2,1)S(1)}, bf16[2,2,1,96,896]{4,3,2,1,0:T(8,128)(2,1)S(1)}, u32[]{:S(2)}, u32[]{:S(2)}) %collective-permute-start.24) | collective-permute-done | bytes 688160 | tf_op jit(solution)/shard_map/ppermute | solution.py:49
  85.4 2.1 %collective-permute-start.25 = (bf16[1,2,1,96,896]{4,3,2,1,0:T(8,128)(2,1)S(1)}, bf16[1,2,1,96,896]{4,3,2,1,0:T(8,128)(2,1)S(1)}, u32[]{:S(2)}, u32[]{:S(2)}) collective-permute-start(bf16[1,2,1,96,896]{4,3,2,1,0:T(8,128)(2,1)S(1)} %dynamic-slice_convert_fusion.3), channel_id=1, source_target_pairs={{0,4},{1,5},{2,6},{3,7},{4,0},{5,1},{6,2},{7,3},{8,12},{9,13},{10,... | collective-permute-start | bytes 1032200 | tf_op jit(solution)/shard_map/ppermute | solution.py:49
  87.6 3.8 %collective-permute-done.14 = bf16[2,1,1,96,896]{4,3,2,1,0:T(8,128)(2,1)S(1)} collective-permute-done((bf16[2,1,1,96,896]{4,3,2,1,0:T(8,128)(2,1)S(1)}, bf16[2,1,1,96,896]{4,3,2,1,0:T(8,128)(2,1)S(1)}, u32[]{:S(2)}, u32[]{:S(2)}) %collective-permute-start.14) | collective-permute-done | bytes 344096 | tf_op jit(solution)/shard_map/ppermute | solution.py:49
  94.6 5.9 %collective-permute-done.15 = f32[1,1,1,96,896]{4,3,2,1,0:T(8,128)S(1)} collective-permute-done((f32[1,1,1,96,896]{4,3,2,1,0:T(8,128)S(1)}, f32[1,1,1,96,896]{4,3,2,1,0:T(8,128)S(1)}, u32[]{:S(2)}, u32[]{:S(2)}) %collective-permute-start.15) | collective-permute-done | bytes 344096 | tf_op jit(solution)/shard_map/ppermute | solution.py:49
  106.5 3.7 %collective-permute-done.30 = bf16[1,1,1,96,896]{4,3,2,1,0:T(8,128)(2,1)} collective-permute-done((bf16[1,1,1,96,896]{4,3,2,1,0:T(8,128)(2,1)}, bf16[1,1,1,96,896]{4,3,2,1,0:T(8,128)(2,1)}, u32[]{:S(2)}, u32[]{:S(2)}) %collective-permute-start.30) | collective-permute-done | bytes 172064 | tf_op jit(solution)/shard_map/ppermute | solution.py:49
  116.5 2.6 %collective-permute-done.31 = bf16[1,1,2,96,896]{4,3,2,1,0:T(8,128)(2,1)S(1)} collective-permute-done((bf16[1,1,2,96,896]{4,3,2,1,0:T(8,128)(2,1)S(1)}, bf16[1,1,2,96,896]{4,3,2,1,0:T(8,128)(2,1)S(1)}, u32[]{:S(2)}, u32[]{:S(2)}) %collective-permute-start.31) | collective-permute-done | bytes 344096 | tf_op jit(solution)/shard_map/ppermute | solution.py:49
  122.2 4.0 %collective-permute-done.17 = bf16[2,1,1,96,896]{4,3,2,1,0:T(8,128)(2,1)S(1)} collective-permute-done((bf16[2,1,1,96,896]{4,3,2,1,0:T(8,128)(2,1)S(1)}, bf16[2,1,1,96,896]{4,3,2,1,0:T(8,128)(2,1)S(1)}, u32[]{:S(2)}, u32[]{:S(2)}) %collective-permute-start.17) | collective-permute-done | bytes 344096 | tf_op jit(solution)/shard_map/ppermute | solution.py:49
  126.3 2.1 %collective-permute-start.18 = (bf16[2,2,1,96,896]{4,3,2,1,0:T(8,128)(2,1)S(1)}, bf16[2,2,1,96,896]{4,3,2,1,0:T(8,128)(2,1)S(1)}, u32[]{:S(2)}, u32[]{:S(2)}) collective-permute-start(bf16[2,2,1,96,896]{4,3,2,1,0:T(8,128)(2,1)S(1)} %pad_maximum_fusion.17), channel_id=1, source_target_pairs={{0,2},{1,3},{2,0},{3,1},{4,6},{5,7},{6,4},{7,5},{8,10},{9,11},{10,... | collective-permute-start | bytes 2064392 | tf_op jit(solution)/shard_map/ppermute | solution.py:49
  128.4 9.4 %collective-permute-done.32 = bf16[2,1,2,96,896]{4,3,2,1,0:T(8,128)(2,1)S(1)} collective-permute-done((bf16[2,1,2,96,896]{4,3,2,1,0:T(8,128)(2,1)S(1)}, bf16[2,1,2,96,896]{4,3,2,1,0:T(8,128)(2,1)S(1)}, u32[]{:S(2)}, u32[]{:S(2)}) %collective-permute-start.32) | collective-permute-done | bytes 688160 | tf_op jit(solution)/shard_map/ppermute | solution.py:49
  139.1 3.0 %fusion.2 = f32[768,1024]{1,0:T(8,128)S(1)} fusion(bf16[768,896]{1,0:T(8,128)(2,1)S(1)} %bitcast.78, bf16[512,896]{0,1:T(8,128)(2,1)} %collective-permute-done.12, bf16[512,896]{0,1:T(8,128)(2,1)S(1)} %copy-done.6), kind=kOutput, calls=%fused_computation.30 | convolution fusion | flops 1412956160 | bytes 6356992 | tf_op jit(solution)/shard_map/dot_general | solution.py:111
  143.5 3.0 %convolution_add_fusion = f32[768,1024]{1,0:T(8,128)S(1)} fusion(f32[768,1024]{1,0:T(8,128)S(1)} %fusion.2, bf16[768,896]{1,0:T(8,128)(2,1)S(1)} %bitcast.80, bf16[512,896]{0,1:T(8,128)(2,1)} %collective-permute-done.8, bf16[512,896]{0,1:T(8,128)(2,1)S(1)} %copy-done.8), kind=kOutput, calls=%fused_computation.12 | convolution fusion | flops 1413742592 | bytes 9502720 | tf_op jit(solution)/shard_map/dot_general | solution.py:111
  147.0 3.1 %fusion.1 = f32[768,1024]{1,0:T(8,128)S(1)} fusion(bf16[768,896]{1,0:T(8,128)(2,1)S(1)} %bitcast.82, bf16[896,512]{1,0:T(8,128)(2,1)} %collective-permute-done.19, bf16[896,512]{1,0:T(8,128)(2,1)S(1)} %copy-done.4), kind=kOutput, calls=%fused_computation.29 | convolution fusion | flops 1412956160 | bytes 6356992 | tf_op jit(solution)/shard_map/dot_general | solution.py:111
  161.1 2.5 %collective-permute-start.34 = (bf16[2,1,2,96,384]{4,3,2,1,0:T(8,128)(2,1)}, bf16[2,1,2,96,384]{4,3,2,1,0:T(8,128)(2,1)}, u32[]{:S(2)}, u32[]{:S(2)}) collective-permute-start(bf16[2,1,2,96,384]{4,3,2,1,0:T(8,128)(2,1)} %dynamic-slice_convert_fusion.6), channel_id=1, source_target_pairs={{0,48},{16,32},{32,16},{48,0},{64,112},{80,96},{96,80},{112,64},{1... | collective-permute-start | bytes 884744 | tf_op jit(solution)/shard_map/ppermute | solution.py:53
  170.0 2.4 %copy.18 = bf16[512,1792]{1,0:T(8,128)(2,1)} copy(bf16[512,1792]{0,1:T(8,128)(2,1)S(1)} %bitcast_multiply_fusion.2) | data formatting | bytes 3670016
  174.0 2.4 %copy.19 = bf16[512,1792]{1,0:T(8,128)(2,1)} copy(bf16[512,1792]{0,1:T(8,128)(2,1)S(1)} %bitcast_multiply_fusion) | data formatting | bytes 3670016
  179.4 2.7 %collective-permute-start.35 = (bf16[2,1,1,96,384]{4,3,2,1,0:T(8,128)(2,1)S(1)}, bf16[2,1,1,96,384]{4,3,2,1,0:T(8,128)(2,1)S(1)}, u32[]{:S(2)}, u32[]{:S(2)}) collective-permute-start(bf16[2,1,1,96,384]{4,3,2,1,0:T(8,128)(2,1)S(1)} %dynamic-slice_convert_fusion.9), channel_id=1, source_target_pairs={{0,64},{16,80},{32,96},{48,112},{64,0},{80,16},{96,32},{112,48},{1... | collective-permute-start | bytes 442376 | tf_op jit(solution)/shard_map/ppermute | solution.py:53
  183.9 2.2 %collective-permute-done.35 = bf16[2,1,1,96,384]{4,3,2,1,0:T(8,128)(2,1)S(1)} collective-permute-done((bf16[2,1,1,96,384]{4,3,2,1,0:T(8,128)(2,1)S(1)}, bf16[2,1,1,96,384]{4,3,2,1,0:T(8,128)(2,1)S(1)}, u32[]{:S(2)}, u32[]{:S(2)}) %collective-permute-start.35) | collective-permute-done | bytes 147488 | tf_op jit(solution)/shard_map/ppermute | solution.py:53
  187.0 2.6 %collective-permute-done.22 = bf16[1,1,2,96,384]{4,3,2,1,0:T(8,128)(2,1)S(1)} collective-permute-done((bf16[1,1,2,96,384]{4,3,2,1,0:T(8,128)(2,1)S(1)}, bf16[1,1,2,96,384]{4,3,2,1,0:T(8,128)(2,1)S(1)}, u32[]{:S(2)}, u32[]{:S(2)}) %collective-permute-start.22) | collective-permute-done | bytes 147488 | tf_op jit(solution)/shard_map/ppermute | solution.py:53
  191.5 4.9 %collective-permute-done.23 = f32[1,1,1,96,384]{4,3,2,1,0:T(8,128)S(1)} collective-permute-done((f32[1,1,1,96,384]{4,3,2,1,0:T(8,128)S(1)}, f32[1,1,1,96,384]{4,3,2,1,0:T(8,128)S(1)}, u32[]{:S(2)}, u32[]{:S(2)}) %collective-permute-start.23) | collective-permute-done | bytes 147488 | tf_op jit(solution)/shard_map/ppermute | solution.py:53
  (210 shorter events, 75.0 us)
Async XLA Ops:
  3.7 13.8 %collective-permute-start = (bf16[96,1024]{1,0:T(8,128)(2,1)}, bf16[96,1024]{1,0:T(8,128)(2,1)}, u32[]{:S(2)}, u32[]{:S(2)}) collective-permute-start(bf16[96,1024]{1,0:T(8,128)(2,1)} %constant_dynamic-update-slice_fusion), channel_id=1, source_target_pairs={{0,16},{16,0},{32,48},{48,32},{64,80},{80,64},{96,112},{112,96},{1... | collective-permute-start | bytes 589832 | tf_op jit(solution)/shard_map/ppermute | solution.py:205
  5.4 19.8 %collective-permute-start.1 = (bf16[96,1024]{1,0:T(8,128)(2,1)}, bf16[96,1024]{1,0:T(8,128)(2,1)}, u32[]{:S(2)}, u32[]{:S(2)}) collective-permute-start(bf16[96,1024]{1,0:T(8,128)(2,1)} %constant_dynamic-update-slice_fusion), channel_id=1, source_target_pairs={{0,32},{16,48},{32,0},{48,16},{64,96},{80,112},{96,64},{112,80},{1... | collective-permute-start | bytes 589832 | tf_op jit(solution)/shard_map/ppermute | solution.py:205
  8.3 18.0 %collective-permute-start.2 = (bf16[96,1024]{1,0:T(8,128)(2,1)}, bf16[96,1024]{1,0:T(8,128)(2,1)}, u32[]{:S(2)}, u32[]{:S(2)}) collective-permute-start(bf16[96,1024]{1,0:T(8,128)(2,1)} %constant_dynamic-update-slice_fusion), channel_id=1, source_target_pairs={{0,48},{16,32},{32,16},{48,0},{64,112},{80,96},{96,80},{112,64},{1... | collective-permute-start | bytes 589832 | tf_op jit(solution)/shard_map/ppermute | solution.py:205
  8.4 18.8 %collective-permute-start.3 = (bf16[96,1024]{1,0:T(8,128)(2,1)}, bf16[96,1024]{1,0:T(8,128)(2,1)}, u32[]{:S(2)}, u32[]{:S(2)}) collective-permute-start(bf16[96,1024]{1,0:T(8,128)(2,1)} %constant_dynamic-update-slice_fusion), channel_id=1, source_target_pairs={{0,64},{16,80},{32,96},{48,112},{64,0},{80,16},{96,32},{112,48},{1... | collective-permute-start | bytes 589832 | tf_op jit(solution)/shard_map/ppermute | solution.py:205
  11.5 16.7 %collective-permute-start.4 = (bf16[96,1024]{1,0:T(8,128)(2,1)}, bf16[96,1024]{1,0:T(8,128)(2,1)}, u32[]{:S(2)}, u32[]{:S(2)}) collective-permute-start(bf16[96,1024]{1,0:T(8,128)(2,1)} %constant_dynamic-update-slice_fusion), channel_id=1, source_target_pairs={{0,80},{16,64},{32,112},{48,96},{64,16},{80,0},{96,48},{112,32},{1... | collective-permute-start | bytes 589832 | tf_op jit(solution)/shard_map/ppermute | solution.py:205
  17.6 11.8 %collective-permute-start.5 = (bf16[96,1024]{1,0:T(8,128)(2,1)}, bf16[96,1024]{1,0:T(8,128)(2,1)S(1)}, u32[]{:S(2)}, u32[]{:S(2)}) collective-permute-start(bf16[96,1024]{1,0:T(8,128)(2,1)} %constant_dynamic-update-slice_fusion), channel_id=1, source_target_pairs={{0,96},{16,112},{32,64},{48,80},{64,32},{80,48},{96,0},{112,16},{1... | collective-permute-start | bytes 589832 | tf_op jit(solution)/shard_map/ppermute | solution.py:205
  25.2 9.6 %collective-permute-start.6 = (bf16[96,1024]{1,0:T(8,128)(2,1)}, bf16[96,1024]{1,0:T(8,128)(2,1)S(1)}, u32[]{:S(2)}, u32[]{:S(2)}) collective-permute-start(bf16[96,1024]{1,0:T(8,128)(2,1)} %constant_dynamic-update-slice_fusion), channel_id=1, source_target_pairs={{0,112},{16,96},{32,80},{48,64},{64,48},{80,32},{96,16},{112,0},{1... | collective-permute-start | bytes 589832 | tf_op jit(solution)/shard_map/ppermute | solution.py:205
  34.8 16.1 %collective-permute-start.7 = (bf16[768,1024]{1,0:T(8,128)(2,1)S(1)}, bf16[768,1024]{1,0:T(8,128)(2,1)}, u32[]{:S(2)}, u32[]{:S(2)}) collective-permute-start(bf16[768,1024]{1,0:T(8,128)(2,1)S(1)} %bitcast.63), channel_id=1, source_target_pairs={{0,1},{1,0},{2,3},{3,2},{4,5},{5,4},{6,7},{7,6},{8,9},{9,8},{10,11... | collective-permute-start | bytes 4718600 | tf_op jit(solution)/shard_map/ppermute | solution.py:49
  36.2 16.7 %collective-permute-start.12 = (bf16[512,896]{0,1:T(8,128)(2,1)}, bf16[512,896]{0,1:T(8,128)(2,1)}, u32[]{:S(2)}, u32[]{:S(2)}) collective-permute-start(bf16[512,896]{0,1:T(8,128)(2,1)} %get-tuple-element.20), channel_id=1, source_target_pairs={{0,1},{1,0},{2,3},{3,2},{4,5},{5,4},{6,7},{7,6},{8,9},{9,8},{10,11... | collective-permute-start | bytes 2752520 | tf_op jit(solution)/shard_map/ppermute | solution.py:49
  41.7 18.7 %collective-permute-start.8 = (bf16[512,896]{0,1:T(8,128)(2,1)}, bf16[512,896]{0,1:T(8,128)(2,1)}, u32[]{:S(2)}, u32[]{:S(2)}) collective-permute-start(bf16[512,896]{0,1:T(8,128)(2,1)} %get-tuple-element.22), channel_id=1, source_target_pairs={{0,1},{1,0},{2,3},{3,2},{4,5},{5,4},{6,7},{7,6},{8,9},{9,8},{10,11... | collective-permute-start | bytes 2752520 | tf_op jit(solution)/shard_map/ppermute | solution.py:49
  50.2 13.5 %collective-permute-start.19 = (bf16[896,512]{1,0:T(8,128)(2,1)}, bf16[896,512]{1,0:T(8,128)(2,1)}, u32[]{:S(2)}, u32[]{:S(2)}) collective-permute-start(bf16[896,512]{1,0:T(8,128)(2,1)} %get-tuple-element.24), channel_id=1, source_target_pairs={{0,1},{1,0},{2,3},{3,2},{4,5},{5,4},{6,7},{7,6},{8,9},{9,8},{10,11... | collective-permute-start | bytes 2752520 | tf_op jit(solution)/shard_map/ppermute | solution.py:49
  56.3 19.7 %collective-permute-start.13 = (bf16[2,1,2,96,896]{4,3,2,1,0:T(8,128)(2,1)S(1)}, bf16[2,1,2,96,896]{4,3,2,1,0:T(8,128)(2,1)S(1)}, u32[]{:S(2)}, u32[]{:S(2)}) collective-permute-start(bf16[2,1,2,96,896]{4,3,2,1,0:T(8,128)(2,1)S(1)} %dynamic-slice_convert_fusion.1), channel_id=1, source_target_pairs={{0,12},{1,13},{2,14},{3,15},{4,8},{5,9},{6,10},{7,11},{8,4},{9,5},... | collective-permute-start | bytes 2064392 | tf_op jit(solution)/shard_map/ppermute | solution.py:49
  63.6 17.2 %collective-permute-start.9 = (bf16[1,2,2,96,896]{4,3,2,1,0:T(8,128)(2,1)S(1)}, bf16[1,2,2,96,896]{4,3,2,1,0:T(8,128)(2,1)S(1)}, u32[]{:S(2)}, u32[]{:S(2)}) collective-permute-start(bf16[1,2,2,96,896]{4,3,2,1,0:T(8,128)(2,1)S(1)} %dynamic-slice_convert_fusion.2), channel_id=1, source_target_pairs={{0,4},{1,5},{2,6},{3,7},{4,0},{5,1},{6,2},{7,3},{8,12},{9,13},{10,... | collective-permute-start | bytes 2064392 | tf_op jit(solution)/shard_map/ppermute | solution.py:49
  66.9 18.4 %collective-permute-start.24 = (bf16[2,2,1,96,896]{4,3,2,1,0:T(8,128)(2,1)S(1)}, bf16[2,2,1,96,896]{4,3,2,1,0:T(8,128)(2,1)S(1)}, u32[]{:S(2)}, u32[]{:S(2)}) collective-permute-start(bf16[2,2,1,96,896]{4,3,2,1,0:T(8,128)(2,1)S(1)} %dynamic-slice_convert_fusion), channel_id=1, source_target_pairs={{0,2},{1,3},{2,0},{3,1},{4,6},{5,7},{6,4},{7,5},{8,10},{9,11},{10,... | collective-permute-start | bytes 2064392 | tf_op jit(solution)/shard_map/ppermute | solution.py:49
  76.2 15.2 %collective-permute-start.14 = (bf16[2,1,1,96,896]{4,3,2,1,0:T(8,128)(2,1)S(1)}, bf16[2,1,1,96,896]{4,3,2,1,0:T(8,128)(2,1)S(1)}, u32[]{:S(2)}, u32[]{:S(2)}) collective-permute-start(bf16[2,1,1,96,896]{4,3,2,1,0:T(8,128)(2,1)S(1)} %dynamic-slice_convert_fusion.4), channel_id=1, source_target_pairs={{0,2},{1,3},{2,0},{3,1},{4,6},{5,7},{6,4},{7,5},{8,10},{9,11},{10,... | collective-permute-start | bytes 1032200 | tf_op jit(solution)/shard_map/ppermute | solution.py:49
  81.0 12.3 %collective-permute-start.10 = (bf16[1,1,2,96,896]{4,3,2,1,0:T(8,128)(2,1)S(1)}, bf16[1,1,2,96,896]{4,3,2,1,0:T(8,128)(2,1)S(1)}, u32[]{:S(2)}, u32[]{:S(2)}) collective-permute-start(bf16[1,1,2,96,896]{4,3,2,1,0:T(8,128)(2,1)S(1)} %dynamic-slice_convert_fusion.5), channel_id=1, source_target_pairs={{0,12},{1,13},{2,14},{3,15},{4,8},{5,9},{6,10},{7,11},{8,4},{9,5},... | collective-permute-start | bytes 1032200 | tf_op jit(solution)/shard_map/ppermute | solution.py:49
  85.4 8.6 %collective-permute-start.25 = (bf16[1,2,1,96,896]{4,3,2,1,0:T(8,128)(2,1)S(1)}, bf16[1,2,1,96,896]{4,3,2,1,0:T(8,128)(2,1)S(1)}, u32[]{:S(2)}, u32[]{:S(2)}) collective-permute-start(bf16[1,2,1,96,896]{4,3,2,1,0:T(8,128)(2,1)S(1)} %dynamic-slice_convert_fusion.3), channel_id=1, source_target_pairs={{0,4},{1,5},{2,6},{3,7},{4,0},{5,1},{6,2},{7,3},{8,12},{9,13},{10,... | collective-permute-start | bytes 1032200 | tf_op jit(solution)/shard_map/ppermute | solution.py:49
  91.5 9.0 %collective-permute-start.15 = (f32[1,1,1,96,896]{4,3,2,1,0:T(8,128)S(1)}, f32[1,1,1,96,896]{4,3,2,1,0:T(8,128)S(1)}, u32[]{:S(2)}, u32[]{:S(2)}) collective-permute-start(f32[1,1,1,96,896]{4,3,2,1,0:T(8,128)S(1)} %constant_dynamic-slice_fusion.6), channel_id=1, source_target_pairs={{0,4},{1,5},{2,6},{3,7},{4,0},{5,1},{6,2},{7,3},{8,12},{9,13},{10,... | collective-permute-start | bytes 1032200 | tf_op jit(solution)/shard_map/ppermute | solution.py:49
  93.4 8.3 %collective-permute-start.11 = (f32[1,1,1,96,896]{4,3,2,1,0:T(8,128)S(1)}, f32[1,1,1,96,896]{4,3,2,1,0:T(8,128)S(1)}, u32[]{:S(2)}, u32[]{:S(2)}) collective-permute-start(f32[1,1,1,96,896]{4,3,2,1,0:T(8,128)S(1)} %constant_dynamic-slice_fusion.9), channel_id=1, source_target_pairs={{0,2},{1,3},{2,0},{3,1},{4,6},{5,7},{6,4},{7,5},{8,10},{9,11},{10,... | collective-permute-start | bytes 1032200 | tf_op jit(solution)/shard_map/ppermute | solution.py:49
  94.2 9.3 %collective-permute-start.26 = (f32[1,1,1,96,896]{4,3,2,1,0:T(8,128)S(1)}, f32[1,1,1,96,896]{4,3,2,1,0:T(8,128)S(1)}, u32[]{:S(2)}, u32[]{:S(2)}) collective-permute-start(f32[1,1,1,96,896]{4,3,2,1,0:T(8,128)S(1)} %constant_dynamic-slice_fusion.2), channel_id=1, source_target_pairs={{0,12},{1,13},{2,14},{3,15},{4,8},{5,9},{6,10},{7,11},{8,4},{9,5},... | collective-permute-start | bytes 1032200 | tf_op jit(solution)/shard_map/ppermute | solution.py:49
  113.7 8.2 %collective-permute-start.28 = (bf16[1,2,1,96,896]{4,3,2,1,0:T(8,128)(2,1)S(1)}, bf16[1,2,1,96,896]{4,3,2,1,0:T(8,128)(2,1)S(1)}, u32[]{:S(2)}, u32[]{:S(2)}) collective-permute-start(bf16[1,2,1,96,896]{4,3,2,1,0:T(8,128)(2,1)S(1)} %pad_maximum_fusion.21), channel_id=1, source_target_pairs={{0,2},{1,3},{2,0},{3,1},{4,6},{5,7},{6,4},{7,5},{8,10},{9,11},{10,... | collective-permute-start | bytes 1032200 | tf_op jit(solution)/shard_map/ppermute | solution.py:49
  114.5 11.7 %collective-permute-start.17 = (bf16[2,1,1,96,896]{4,3,2,1,0:T(8,128)(2,1)S(1)}, bf16[2,1,1,96,896]{4,3,2,1,0:T(8,128)(2,1)S(1)}, u32[]{:S(2)}, u32[]{:S(2)}) collective-permute-start(bf16[2,1,1,96,896]{4,3,2,1,0:T(8,128)(2,1)S(1)} %pad_maximum_fusion.20), channel_id=1, source_target_pairs={{0,12},{1,13},{2,14},{3,15},{4,8},{5,9},{6,10},{7,11},{8,4},{9,5},... | collective-permute-start | bytes 1032200 | tf_op jit(solution)/shard_map/ppermute | solution.py:49
  119.3 18.5 %collective-permute-start.32 = (bf16[2,1,2,96,896]{4,3,2,1,0:T(8,128)(2,1)S(1)}, bf16[2,1,2,96,896]{4,3,2,1,0:T(8,128)(2,1)S(1)}, u32[]{:S(2)}, u32[]{:S(2)}) collective-permute-start(bf16[2,1,2,96,896]{4,3,2,1,0:T(8,128)(2,1)S(1)} %pad_maximum_fusion.19), channel_id=1, source_target_pairs={{0,12},{1,13},{2,14},{3,15},{4,8},{5,9},{6,10},{7,11},{8,4},{9,5},... | collective-permute-start | bytes 2064392 | tf_op jit(solution)/shard_map/ppermute | solution.py:49
  122.1 20.0 %collective-permute-start.29 = (bf16[1,2,2,96,896]{4,3,2,1,0:T(8,128)(2,1)S(1)}, bf16[1,2,2,96,896]{4,3,2,1,0:T(8,128)(2,1)S(1)}, u32[]{:S(2)}, u32[]{:S(2)}) collective-permute-start(bf16[1,2,2,96,896]{4,3,2,1,0:T(8,128)(2,1)S(1)} %pad_maximum_fusion.18), channel_id=1, source_target_pairs={{0,4},{1,5},{2,6},{3,7},{4,0},{5,1},{6,2},{7,3},{8,12},{9,13},{10,... | collective-permute-start | bytes 2064392 | tf_op jit(solution)/shard_map/ppermute | solution.py:49
  126.3 20.3 %collective-permute-start.18 = (bf16[2,2,1,96,896]{4,3,2,1,0:T(8,128)(2,1)S(1)}, bf16[2,2,1,96,896]{4,3,2,1,0:T(8,128)(2,1)S(1)}, u32[]{:S(2)}, u32[]{:S(2)}) collective-permute-start(bf16[2,2,1,96,896]{4,3,2,1,0:T(8,128)(2,1)S(1)} %pad_maximum_fusion.17), channel_id=1, source_target_pairs={{0,2},{1,3},{2,0},{3,1},{4,6},{5,7},{6,4},{7,5},{8,10},{9,11},{10,... | collective-permute-start | bytes 2064392 | tf_op jit(solution)/shard_map/ppermute | solution.py:49
  146.6 11.4 %collective-permute-start.33 = (bf16[768,512]{1,0:T(8,128)(2,1)S(1)}, bf16[768,512]{1,0:T(8,128)(2,1)S(1)}, u32[]{:S(2)}, u32[]{:S(2)}) collective-permute-start(bf16[768,512]{1,0:T(8,128)(2,1)S(1)} %slice.108), channel_id=1, source_target_pairs={{0,1},{1,0},{2,3},{3,2},{4,5},{5,4},{6,7},{7,6},{8,9},{9,8},{10,11... | collective-permute-start | bytes 2359304 | tf_op jit(solution)/shard_map/ppermute | solution.py:49
  152.5 13.2 %collective-permute-start.40 = (bf16[512,896]{0,1:T(8,128)(2,1)S(1)}, bf16[512,896]{0,1:T(8,128)(2,1)S(1)}, u32[]{:S(2)}, u32[]{:S(2)}) collective-permute-start(bf16[512,896]{0,1:T(8,128)(2,1)S(1)} %slice.93), channel_id=1, source_target_pairs={{0,1},{1,0},{2,3},{3,2},{4,5},{5,4},{6,7},{7,6},{8,9},{9,8},{10,11... | collective-permute-start | bytes 2752520 | tf_op jit(solution)/shard_map/ppermute | solution.py:49
  154.6 13.9 %collective-permute-start.41 = (bf16[512,896]{0,1:T(8,128)(2,1)S(1)}, bf16[512,896]{0,1:T(8,128)(2,1)S(1)}, u32[]{:S(2)}, u32[]{:S(2)}) collective-permute-start(bf16[512,896]{0,1:T(8,128)(2,1)S(1)} %slice.95), channel_id=1, source_target_pairs={{0,1},{1,0},{2,3},{3,2},{4,5},{5,4},{6,7},{7,6},{8,9},{9,8},{10,11... | collective-permute-start | bytes 2752520 | tf_op jit(solution)/shard_map/ppermute | solution.py:49
  158.3 8.4 %collective-permute-start.37 = (bf16[2,2,1,96,256]{4,3,2,1,0:T(8,128)(2,1)S(1)}, bf16[2,2,1,96,256]{4,3,2,1,0:T(8,128)(2,1)S(1)}, u32[]{:S(2)}, u32[]{:S(2)}) collective-permute-start(bf16[2,2,1,96,256]{4,3,2,1,0:T(8,128)(2,1)S(1)} %dynamic-slice_convert_fusion.8), channel_id=1, source_target_pairs={{0,64},{16,80},{32,96},{48,112},{64,0},{80,16},{96,32},{112,48},{1... | collective-permute-start | bytes 589832 | tf_op jit(solution)/shard_map/ppermute | solution.py:53
  161.1 17.1 %collective-permute-start.34 = (bf16[2,1,2,96,384]{4,3,2,1,0:T(8,128)(2,1)}, bf16[2,1,2,96,384]{4,3,2,1,0:T(8,128)(2,1)}, u32[]{:S(2)}, u32[]{:S(2)}) collective-permute-start(bf16[2,1,2,96,384]{4,3,2,1,0:T(8,128)(2,1)} %dynamic-slice_convert_fusion.6), channel_id=1, source_target_pairs={{0,48},{16,32},{32,16},{48,0},{64,112},{80,96},{96,80},{112,64},{1... | collective-permute-start | bytes 884744 | tf_op jit(solution)/shard_map/ppermute | solution.py:53
  163.7 18.4 %collective-permute-start.21 = (bf16[1,2,2,96,384]{4,3,2,1,0:T(8,128)(2,1)S(1)}, bf16[1,2,2,96,384]{4,3,2,1,0:T(8,128)(2,1)}, u32[]{:S(2)}, u32[]{:S(2)}) collective-permute-start(bf16[1,2,2,96,384]{4,3,2,1,0:T(8,128)(2,1)S(1)} %dynamic-slice_convert_fusion.7), channel_id=1, source_target_pairs={{0,16},{16,0},{32,48},{48,32},{64,80},{80,64},{96,112},{112,96},{1... | collective-permute-start | bytes 884744 | tf_op jit(solution)/shard_map/ppermute | solution.py:53
  167.5 8.9 %collective-permute-start.38 = (bf16[1,2,1,96,256]{4,3,2,1,0:T(8,128)(2,1)}, bf16[1,2,1,96,256]{4,3,2,1,0:T(8,128)(2,1)}, u32[]{:S(2)}, u32[]{:S(2)}) collective-permute-start(bf16[1,2,1,96,256]{4,3,2,1,0:T(8,128)(2,1)} %dynamic-slice_convert_fusion.11), channel_id=1, source_target_pairs={{0,16},{16,0},{32,48},{48,32},{64,80},{80,64},{96,112},{112,96},{1... | collective-permute-start | bytes 294920 | tf_op jit(solution)/shard_map/ppermute | solution.py:53
  (32 other events, 177.0 us)

commit v2 on v0

v2 whole, which is shorter than its diff:
```python
import functools

import jax
import jax.numpy as jnp
import numpy as np
from jax import lax
from jax.experimental import pallas as pl
from jax.experimental.pallas import tpu as pltpu
from jax.sharding import PartitionSpec as P

BLK = 128
BF = jnp.bfloat16
F32 = jnp.float32

GRAY = ((0, 0), (1, 0), (1, 1), (0, 1))
RING = {bits: pos for pos, bits in enumerate(GRAY)}
MASK = {"A": 4, "B": 2, "X": 1}
ORDERS = ("ABX", "BXA", "XAB")
NEAR = ("", "A", "B", "X")
FAR = ("AB", "AX", "BX", "ABX")


def flip_ring(pos, dims):
    bit_a, bit_b = GRAY[pos]
    return RING[(bit_a ^ ("A" in dims), bit_b ^ ("B" in dims))]


def flip_col(i, dims):
    z, x, c = i // 4, (i // 2) % 2, i % 2
    return (flip_ring(z, dims) * 2 + (x ^ ("X" in dims))) * 2 + c


def flip_row(i, dims):
    return (i // 4 ^ ("X" in dims)) * 4 + flip_ring(i % 4, dims)


def swap_core(value):
    return lax.ppermute(value, "col", [(i, i ^ 1) for i in range(16)])


def swap_cube(parts, step):
    return [
        lax.ppermute(part, "col", [(i, flip_col(i, order[step])) for i in range(16)])
        for part, order in zip(parts, ORDERS)
    ]


def swap_row(value, dims):
    return lax.ppermute(value, "row", [(i, flip_row(i, dims)) for i in range(8)])


def make_table():
    rows = []
    for i in range(16):
        bit_a, bit_b = GRAY[i // 4]
        own = bit_a * 4 + bit_b * 2 + (i // 2) % 2
        row = [i % 2]
        for order in ORDERS:
            for place in range(8):
                bits = (place >> 2, (place >> 1) & 1, place & 1)
                row.append(own ^ sum(MASK[d] * b for d, b in zip(order, bits)))
        rows.append(row)
    return np.array(rows, np.int32)


def dot(a, b, dims=((1,), (0,))):
    return lax.dot_general(a, b, (dims, ((), ())), preferred_element_type=F32)


NT = ((1,), (1,))
PARAMS = pltpu.CompilerParams(vmem_limit_bytes=24 * 1024 * 1024)


def call(kernel, prefetch, grid, in_specs, out_specs, out_shape, scratch=(), flops=0, size=0, **more):
    return pl.pallas_call(
        kernel,
        grid_spec=pltpu.PrefetchScalarGridSpec(
            num_scalar_prefetch=prefetch,
            grid=grid,
            in_specs=in_specs,
            out_specs=out_specs,
            scratch_shapes=list(scratch),
        ),
        out_shape=out_shape,
        compiler_params=PARAMS,
        cost_estimate=pl.CostEstimate(flops=flops, bytes_accessed=size, transcendentals=0),
        **more,
    )


def shape(dims, dtype):
    return jax.ShapeDtypeStruct(dims, dtype)


def whole(dims):
    return pl.BlockSpec(dims, lambda *_: (0,) * len(dims))


def times(block, keep):
    return (block.astype(F32) * keep.astype(F32)).astype(BF)


def prepare_kernel(info, gm, um, dm, gk, gs, uk, us, dk, ds, gu_keep, gu_send, d_keep, d_send):
    j = pl.program_id(0)
    blocks, halves = gk.shape[0] // BLK, pl.num_programs(0)
    for side, (g, u, d, gu_out, d_out) in enumerate(
        ((gk, uk, dk, gu_keep, d_keep), (gs, us, ds, gu_send, d_send))
    ):
        core = info[0] if side == 0 else 1 - info[0]
        at = core * halves + j
        for f in range(blocks):
            rows = slice(f * BLK, (f + 1) * BLK)
            gu_out[0, rows, :] = times(g[rows, :], gm[f, at])
            gu_out[1, rows, :] = times(u[rows, :], um[f, at])
            d_out[:, rows] = times(d[:, rows], dm[at, f])


def prepare(info, gm, um, dm, gate_weight, up_weight, down_weight):
    width, hidden = gate_weight.shape
    half, n = hidden // 2, hidden // 2 // BLK

    def wide(side):
        return pl.BlockSpec(
            (width, BLK), lambda j, info, *_: (0, (info[0] if side == 0 else 1 - info[0]) * n + j)
        )

    def tall(side):
        return pl.BlockSpec(
            (BLK, width), lambda j, info, *_: ((info[0] if side == 0 else 1 - info[0]) * n + j, 0)
        )

    gu_spec = pl.BlockSpec((2, width, BLK), lambda j, *_: (0, 0, j))
    d_spec = pl.BlockSpec((BLK, width), lambda j, *_: (j, 0))
    return call(
        prepare_kernel,
        4,
        (n,),
        [wide(0), wide(1), wide(0), wide(1), tall(0), tall(1)],
        [gu_spec, gu_spec, d_spec, d_spec],
        [shape((2, width, half), BF)] * 2 + [shape((half, width), BF)] * 2,
        size=12 * width * hidden,
    )(info, gm, um, dm, gate_weight, gate_weight, up_weight, up_weight, down_weight, down_weight)


def project_kernel(info, own_a, own_b, oth_a, oth_b, gu_own, gu_oth, d_own, d_oth, *refs, base):
    outs, panel = refs[:3], refs[3]
    rows, width = own_a.shape[0], own_a.shape[1] // 2
    r = rows // 4
    for q in range(3):
        cols = slice(0, width) if q < 2 else slice(width, 2 * width)
        for k in range(4):
            at = info[1 + 8 * q + base + k]
            to = slice(k * r, (k + 1) * r)
            row = pl.ds(pl.multiple_of((at % 4) * r, 16), r)

            @pl.when(at < 4)
            def _():
                panel[q, to, :width] = own_a[row, cols]
                panel[q, to, width:] = oth_a[row, cols]

            @pl.when(at >= 4)
            def _():
                panel[q, to, :width] = own_b[row, cols]
                panel[q, to, width:] = oth_b[row, cols]

    for q in range(2):
        w = jnp.concatenate([gu_own[q], gu_oth[q]], axis=0)
        outs[q][...] = dot(panel[q], w).astype(outs[q].dtype)
    w = jnp.concatenate([d_own[...], d_oth[...]], axis=1)
    outs[2][...] = dot(panel[2], w, NT).astype(outs[2].dtype)


def project(info, panels, weights, base, kind):
    rows, width = panels[0].shape[0], panels[0].shape[1] // 2
    count = weights[2].shape[0]
    return call(
        functools.partial(project_kernel, base=base),
        1,
        (1,),
        [whole(v.shape) for v in (*panels, *weights)],
        [whole((rows, count))] * 3,
        [shape((rows, count), kind)] * 3,
        [pltpu.VMEM((3, rows, 2 * width), BF)],
        flops=12 * rows * width * count,
        size=12 * rows * count + 12 * width * count + 8 * rows * width,
    )(info, *panels, *weights)


def pointwise(gate_proj, up_proj, hidden_grad):
    sigmoid_gate = jax.nn.sigmoid(gate_proj)
    silu_gate = gate_proj * sigmoid_gate
    hidden = (silu_gate * up_proj).astype(BF)
    gate_grad = (
        hidden_grad * up_proj * sigmoid_gate * (1.0 + gate_proj * (1.0 - sigmoid_gate))
    ).astype(BF)
    up_grad = (hidden_grad * silu_gate).astype(BF)
    return hidden, gate_grad, up_grad


def exchange(sends, keeps):
    for step in range(3):
        got = swap_cube(sends, step)
        sums = [keep + g.astype(F32) for keep, g in zip(keeps, got)]
        if step < 2:
            n = sums[0].shape[0] // 2
            keeps = [v[:n] for v in sums]
            sends = [v[n:].astype(BF) for v in sums]
    hidden, gate_grad, up_grad = pointwise(*sums)
    parts = [gate_grad, up_grad, hidden]
    for step in (2, 1, 0):
        got = swap_cube(parts, step)
        if step == 0:
            return parts + got
        parts = [jnp.concatenate([part, g], axis=0) for part, g in zip(parts, got)]


def gather_kernel(info, *refs):
    halves, acts = (refs[:3], refs[3:6]), refs[6]
    r = acts.shape[0] // 8
    n = acts.shape[1] // 3
    for q in range(3):
        for k in range(8):
            at = pl.ds(pl.multiple_of(info[1 + 8 * q + k] * r, 16), r)
            acts[at, q * n : (q + 1) * n] = halves[k // 4][q][k % 4 * r : (k % 4 + 1) * r, :]


def gather(info, pieces):
    rows, count = 2 * pieces[0].shape[0], 3 * pieces[0].shape[1]
    return call(
        gather_kernel,
        1,
        (1,),
        [whole(v.shape) for v in pieces],
        whole((rows, count)),
        shape((rows, count), BF),
        size=4 * rows * count,
    )(info, *pieces)


def backward_kernel(acts, gu, d, terms):
    n = acts.shape[1] // 3
    terms[0] = dot(acts[:, 2 * n :], d[...]).astype(terms.dtype)
    inp = dot(acts[:, :n], gu[0], NT) + dot(acts[:, n : 2 * n], gu[1], NT)
    terms[1] = inp.astype(terms.dtype)


def backward(acts, gu, d, kind):
    rows, count, width = acts.shape[0], acts.shape[1], d.shape[1]
    step = 2 * BLK
    return call(
        backward_kernel,
        0,
        (width // step,),
        [
            whole(acts.shape),
            pl.BlockSpec((2, step, d.shape[0]), lambda i: (0, i, 0)),
            pl.BlockSpec((d.shape[0], step), lambda i: (0, i)),
        ],
        pl.BlockSpec((2, rows, step), lambda i: (0, 0, i)),
        shape((2, rows, width), kind),
        flops=2 * rows * width * count,
        size=2 * width * count + 2 * rows * count,
    )(acts, gu, d)


def grads_kernel(info, gm, um, dm, own_a, own_b, gg, ug, hid, *refs, mine):
    outs, tok_t, cot = refs[-5:-2], refs[-2], refs[-1]
    j = pl.program_id(0)
    rows, width = own_a.shape[0], own_a.shape[1] // 2

    @pl.when(j == 0)
    def _():
        tok_t[:, :rows] = own_a[:, :width].T
        tok_t[:, rows:] = own_b[:, :width].T
        cot[:rows, :] = own_a[:, width:]
        cot[rows:, :] = own_b[:, width:]

    gu = dot(tok_t[...], jnp.concatenate([gg[...], ug[...]], axis=1))
    d = dot(hid[...].T, cot[...])
    at = (info[0] if mine else 1 - info[0]) * pl.num_programs(0) + j
    g_out, u_out, d_out = outs
    for f in range(width // BLK):
        block = slice(f * BLK, (f + 1) * BLK)
        g_out[block, :] = (gu[block, :BLK] * gm[f, at].astype(F32)).astype(BF)
        u_out[block, :] = (gu[block, BLK:] * um[f, at].astype(F32)).astype(BF)
        d_out[:, block] = (d[:, block] * dm[at, f].astype(F32)).astype(BF)


def grads(info, masks, panels, acts, into=()):
    rows, width = panels[0].shape[0], panels[0].shape[1] // 2
    n = acts.shape[1] // 3 // BLK
    hidden = 2 * n * BLK

    def half(info):
        return (1 - info[0] if into else info[0]) * n

    wide = pl.BlockSpec((width, BLK), lambda j, info, *_: (0, half(info) + j))
    tall = pl.BlockSpec((BLK, width), lambda j, info, *_: (half(info) + j, 0))
    wide_shape = shape((width, hidden), BF)
    return call(
        functools.partial(grads_kernel, mine=not into),
        4,
        (n,),
        [whole(v.shape) for v in panels]
        + [
            pl.BlockSpec((2 * rows, BLK), lambda j, *_, q=q: (0, q * n + j))
            for q in range(3)
        ]
        + [pl.BlockSpec(memory_space=pl.ANY)] * len(into),
        [wide, wide, tall],
        [wide_shape, wide_shape, shape((hidden, width), BF)],
        [pltpu.VMEM((width, 2 * rows), BF), pltpu.VMEM((2 * rows, width), BF)],
        flops=6 * rows * width * hidden,
        size=3 * width * hidden + 6 * rows * hidden,
        **({"input_output_aliases": {9: 0, 10: 1, 11: 2}} if into else {}),
    )(info, *masks, *panels, acts, acts, acts, *into)


def per_device(
    tokens, cotangent, gate_weight, up_weight, down_weight, gate_mask, up_mask, down_mask
):
    masks = (gate_mask, up_mask, down_mask)
    info = lax.dynamic_index_in_dim(jnp.asarray(make_table()), lax.axis_index("col"), 0, keepdims=False)
    names = NEAR[1:] + FAR
    both = jnp.concatenate([tokens, cotangent], axis=1)
    got = [swap_row(both, d) for d in names[:5]]
    gu_own, gu_send, d_own, d_send = prepare(info, *masks, gate_weight, up_weight, down_weight)
    late, gu_send, d_send, *got = lax.optimization_barrier((both, gu_send, d_send, *got))
    gu_oth, d_oth = swap_core(gu_send), swap_core(d_send)
    got += [swap_row(late, d) for d in names[5:]]
    own = [jnp.concatenate(blocks, axis=0) for blocks in ([both, *got[:3]], got[3:])]
    oth = [swap_core(panel) for panel in own]

    panels, weights = (*own, *oth), (gu_own, gu_oth, d_own, d_oth)
    sends = project(info, panels, weights, 4, BF)
    keeps = project(info, panels, weights, 0, F32)
    acts = gather(info, exchange(sends, keeps))

    got = swap_core(backward(acts, gu_oth, d_oth, F32))
    part = backward(acts, gu_own, d_own, F32) + got
    parts = jnp.split(part, 8, axis=1)
    acts, *blocks = lax.optimization_barrier([acts] + [p.astype(BF) for p in parts[1:]])
    got = [swap_row(block, d) for block, d in zip(blocks[:4], names[:4])]
    sib = swap_core(acts)
    partial = grads(info, masks, own, acts)
    sib, *rest = lax.optimization_barrier([sib] + got + blocks[4:])
    got = rest[:4] + [swap_row(block, d) for block, d in zip(rest[4:], names[4:])]
    weight_grads = grads(info, masks, own, sib, partial)
    total = parts[0]
    for block in got:
        total = total + block.astype(F32)
    total = total.astype(BF)
    return (total[0], total[1], *weight_grads)


def solution(mesh):
    placed = (
        P("row", "col"),
        P("row", "col"),
        P("col", "row"),
        P("col", "row"),
        P("row", "col"),
        P("col", "row"),
        P("col", "row"),
        P("row", "col"),
    )
    return jax.shard_map(
        per_device,
        mesh=mesh,
        in_specs=placed,
        out_specs=(
            P("row", "col"),
            P("row", "col"),
            P("col", "row"),
            P("col", "row"),
            P("row", "col"),
        ),
        check_vma=False,
    )
```

time: 643 us -> 163 us (0.25)
  waiting for transfers between devices: 478 us -> 51.8 us
  blocking collectives: 72.3 us -> 0 us
  starting transfers between devices: 0.3 us -> 67.2 us
  matrix products: 34.2 us -> 0 us
  Pallas kernels: 0 us -> 30.6 us
  other arithmetic: 18.5 us -> 2.17 us
  local copies, waits for them, and re-layouts: 25.8 us -> 10.2 us
  between operations: 14.1 us -> 0.98 us
    psum x1 -> x0, waiting for transfers between devices: 360 us -> none  [per_device(): lax.psum(jnp.concatenate([gate_part, up_part, hidden_part], axis=1), 'col')]
    reduce_scatter x2 -> x0, waiting for transfers between devices: 117 us -> none  [the longest x1 74.5 us: per_device(): lax.psum_scatter(out_term, 'row', scatter_dimension=0, tiled=True)]
    all_gather x2 -> x0, blocking collectives: 72.3 us -> none  [the longest x1 36.5 us: per_device(): lax.all_gather(tokens, 'row', axis=0, tiled=True)]
    ppermute x0 -> x38, starting transfers between devices: none -> 67.2 us  [the longest x18 35.5 us: swap_cube(): lax.ppermute(part, 'col', [(i, flip_col(i, order[step])) for i in range(1...]
    ppermute x0 -> x38, waiting for transfers between devices: none -> 51.8 us  [the longest x18 32.9 us: swap_cube(): lax.ppermute(part, 'col', [(i, flip_col(i, order[step])) for i in range(1...]
    dot_general x9 -> x0, matrix products: 34.2 us -> none  [the longest x1 4.85 us: per_device(): out_term = jnp.dot(hidden_all, down_eff, preferred_element_type=jnp.float32)]
    pallas_call x0 -> x8, Pallas kernels: none -> 30.6 us  [the longest x2 12.9 us: grads(): call(functools.partial(grads_kernel, mine=not into), 4, (n,), [whole(v.sh...]
    convert_element_type x6 -> x2, other arithmetic: 11.7 us -> 0.49 us  [the longest x1 0.26 us: pointwise(): hidden = (silu_gate * up_proj).astype(BF)]
  transfers between devices with their start and end apart: 3 -> 38, of which waited for: 3 -> 20; matrix products, arithmetic and copies ran while one was open for 5% -> 2% of each run, Pallas kernels for 0% -> 14%
where the time goes in v2:
time: 163 us
  starting transfers between devices  67.2 us (41%)
  waiting for transfers between devices  51.8 us (32%)
  Pallas kernels  30.6 us (19%)
  local copies, waits for them, and re-layouts  10.2 us (6%)
  other arithmetic  2.17 us (1%)
    ppermute x18, starting transfers between devices, swap_cube(): lax.ppermute(part, 'col', [(i, flip_col(i, order[step])) for i in range(1...  35.5 us
    ppermute x18, waiting for transfers between devices, swap_cube(): lax.ppermute(part, 'col', [(i, flip_col(i, order[step])) for i in range(1...  32.9 us
    ppermute x14, starting transfers between devices, swap_row(): lax.ppermute(value, 'row', [(i, flip_row(i, dims)) for i in range(8)])  30.6 us
    ppermute x14, waiting for transfers between devices, swap_row(): lax.ppermute(value, 'row', [(i, flip_row(i, dims)) for i in range(8)])  14.4 us
    pallas_call x2, Pallas kernels, grads(): call(functools.partial(grads_kernel, mine=not into), 4, (n,), [whole(v.sh...  12.9 us
    unnamed x19, local copies, waits for them, and re-layouts  7.58 us
    pallas_call x2, Pallas kernels, project(): call(functools.partial(project_kernel, base=base), 1, (1,), [whole(v.shap...  6.91 us
    pallas_call x2, Pallas kernels, backward(): call(backward_kernel, 0, (width // step,), [whole(acts.shape), pl.BlockSp...  6.57 us
  transfers between devices with their start and end apart: 38, of which 20 were waited for; matrix products, arithmetic and copies ran while one was open for 2% of the time, Pallas kernels for 14%

profile of v2, /device:TPU:0, one launch (start us, length us, event | category | flops | bytes accessed | tf_op | source)
XLA Modules:
  0.0 162.9 jit_solution(15275135971285937095)
XLA Ops:
  2.4 4.1 %collective-permute-start.4 = (bf16[96,1024]{1,0:T(8,128)(2,1)S(1)}, bf16[96,1024]{1,0:T(8,128)(2,1)S(1)}, u32[]{:S(2)}, u32[]{:S(2)}) collective-permute-start(bf16[96,1024]{1,0:T(8,128)(2,1)S(1)} %constant_dynamic-update-slice_fusion), channel_id=1, source_target_pairs={{0,80},{16,64},{32,112},{48,96},{64,16},{80,0},{96,48},{112,32},{1... | collective-permute-start | bytes 589832 | tf_op jit(solution)/shard_map/ppermute | solution.py:49
  6.6 2.9 %collective-permute-start.3 = (bf16[96,1024]{1,0:T(8,128)(2,1)S(1)}, bf16[96,1024]{1,0:T(8,128)(2,1)S(1)}, u32[]{:S(2)}, u32[]{:S(2)}) collective-permute-start(bf16[96,1024]{1,0:T(8,128)(2,1)S(1)} %constant_dynamic-update-slice_fusion), channel_id=1, source_target_pairs={{0,32},{16,48},{32,0},{48,16},{64,96},{80,112},{96,64},{112,80},{1... | collective-permute-start | bytes 589832 | tf_op jit(solution)/shard_map/ppermute | solution.py:49
  17.9 3.4 %shard_map.128 = (bf16[2,512,896]{2,1,0:T(8,128)(2,1)S(1)}, bf16[2,512,896]{2,1,0:T(8,128)(2,1)S(1)}, bf16[896,512]{1,0:T(8,128)(2,1)S(1)}, bf16[896,512]{1,0:T(8,128)(2,1)S(1)}) custom-call(s32[25]{0:T(128)S(1)} %dynamic-slice_bitcast_fusion.info, s32[4,14]{1,0:T(4,128)S(1)} %copy-done.3, s32[4,14]{1,0:T(4,128)S(1)} %copy-done.5, s32[14,4]{1,0:T(8,128)S(1)} %copy.17.dm, ...), custom_call_target="tpu_custom_call" | custom-call | bytes 11010048 | tf_op jit(solution)/shard_map/pallas_call | solution.py:134
  21.4 6.7 %collective-permute-start.6 = (bf16[96,1024]{1,0:T(8,128)(2,1)S(1)}, bf16[96,1024]{1,0:T(8,128)(2,1)S(1)}, u32[]{:S(2)}, u32[]{:S(2)}) collective-permute-start(bf16[96,1024]{1,0:T(8,128)(2,1)S(1)} %constant_dynamic-update-slice_fusion), channel_id=1, source_target_pairs={{0,96},{16,112},{32,64},{48,80},{64,32},{80,48},{96,0},{112,16},{1... | collective-permute-start | bytes 589832 | tf_op jit(solution)/shard_map/ppermute | solution.py:49
  28.8 9.8 %collective-permute-done.5 = bf16[96,1024]{1,0:T(8,128)(2,1)S(1)} collective-permute-done((bf16[96,1024]{1,0:T(8,128)(2,1)S(1)}, bf16[96,1024]{1,0:T(8,128)(2,1)S(1)}, u32[]{:S(2)}, u32[]{:S(2)}) %collective-permute-start.5) | collective-permute-done | bytes 196640 | tf_op jit(solution)/shard_map/ppermute | solution.py:49
  38.8 2.3 %collective-permute-done.8.oth_b = bf16[384,1024]{1,0:T(8,128)(2,1)S(1)} collective-permute-done((bf16[384,1024]{1,0:T(8,128)(2,1)S(1)}, bf16[384,1024]{1,0:T(8,128)(2,1)S(1)}, u32[]{:S(2)}, u32[]{:S(2)}) %collective-permute-start.8) | collective-permute-done | bytes 786464 | tf_op jit(solution)/shard_map/ppermute | solution.py:38
  41.1 3.5 %shard_map.130 = (bf16[384,896]{1,0:T(8,128)(2,1)S(1)}, bf16[384,896]{1,0:T(8,128)(2,1)S(1)}, bf16[384,896]{1,0:T(8,128)(2,1)S(1)}) custom-call(s32[25]{0:T(128)S(1)} %dynamic-slice_bitcast_fusion.info, bf16[384,1024]{1,0:T(8,128)(2,1)S(1)} %pad_maximum_fusion.own_a, bf16[384,1024]{1,0:T(8,128)(2,1)S(1)} %constant_dynamic-update-slice_fusion.2.own_b, ...), custom_call_target="tpu_custom_call" | custom-call | flops 2113929216 | bytes 11206656 | tf_op jit(solution)/shard_map/pallas_call | solution.py:176
  45.2 4.0 %collective-permute-start.14 = (bf16[384,896]{1,0:T(8,128)(2,1)S(1)}, bf16[384,896]{1,0:T(8,128)(2,1)S(1)}, u32[]{:S(2)}, u32[]{:S(2)}) collective-permute-start(bf16[384,896]{1,0:T(8,128)(2,1)S(1)} %get-tuple-element.60), channel_id=1, source_target_pairs={{0,12},{1,13},{2,14},{3,15},{4,8},{5,9},{6,10},{7,11},{8,4},{9,5},... | collective-permute-start | bytes 2064392 | tf_op jit(solution)/shard_map/ppermute | solution.py:43
  49.2 3.5 %shard_map.129 = (f32[384,896]{1,0:T(8,128)S(1)}, f32[384,896]{1,0:T(8,128)S(1)}, f32[384,896]{1,0:T(8,128)S(1)}) custom-call(s32[25]{0:T(128)S(1)} %dynamic-slice_bitcast_fusion.info, bf16[384,1024]{1,0:T(8,128)(2,1)S(1)} %pad_maximum_fusion.own_a, bf16[384,1024]{1,0:T(8,128)(2,1)S(1)} %constant_dynamic-update-slice_fusion.2.own_b, ...), custom_call_target="tpu_custom_call" | custom-call | flops 2113929216 | bytes 11206656 | tf_op jit(solution)/shard_map/pallas_call | solution.py:176
  52.7 9.4 %collective-permute-done.11 = bf16[384,896]{1,0:T(8,128)(2,1)S(1)} collective-permute-done((bf16[384,896]{1,0:T(8,128)(2,1)S(1)}, bf16[384,896]{1,0:T(8,128)(2,1)S(1)}, u32[]{:S(2)}, u32[]{:S(2)}) %collective-permute-start.11) | collective-permute-done | bytes 688160 | tf_op jit(solution)/shard_map/ppermute | solution.py:43
  62.3 2.0 %collective-permute-start.12 = (bf16[192,896]{1,0:T(8,128)(2,1)S(1)}, bf16[192,896]{1,0:T(8,128)(2,1)S(1)}, u32[]{:S(2)}, u32[]{:S(2)}) collective-permute-start(bf16[192,896]{1,0:T(8,128)(2,1)S(1)} %slice.108), channel_id=1, source_target_pairs={{0,4},{1,5},{2,6},{3,7},{4,0},{5,1},{6,2},{7,3},{8,12},{9,13},{10,... | collective-permute-start | bytes 1032200 | tf_op jit(solution)/shard_map/ppermute | solution.py:43
  67.8 1.8 %collective-permute-start.18 = (bf16[192,896]{1,0:T(8,128)(2,1)S(1)}, bf16[192,896]{1,0:T(8,128)(2,1)S(1)}, u32[]{:S(2)}, u32[]{:S(2)}) collective-permute-start(bf16[192,896]{1,0:T(8,128)(2,1)S(1)} %slice.106), channel_id=1, source_target_pairs={{0,12},{1,13},{2,14},{3,15},{4,8},{5,9},{6,10},{7,11},{8,4},{9,5},... | collective-permute-start | bytes 1032200 | tf_op jit(solution)/shard_map/ppermute | solution.py:43
  69.6 3.9 %collective-permute-done.12 = bf16[192,896]{1,0:T(8,128)(2,1)S(1)} collective-permute-done((bf16[192,896]{1,0:T(8,128)(2,1)S(1)}, bf16[192,896]{1,0:T(8,128)(2,1)S(1)}, u32[]{:S(2)}, u32[]{:S(2)}) %collective-permute-start.12) | collective-permute-done | bytes 344096 | tf_op jit(solution)/shard_map/ppermute | solution.py:43
  73.6 2.2 %collective-permute-start.13 = (bf16[96,896]{1,0:T(8,128)(2,1)S(1)}, bf16[96,896]{1,0:T(8,128)(2,1)S(1)}, u32[]{:S(2)}, u32[]{:S(2)}) collective-permute-start(bf16[96,896]{1,0:T(8,128)(2,1)S(1)} %slice.111), channel_id=1, source_target_pairs={{0,12},{1,13},{2,14},{3,15},{4,8},{5,9},{6,10},{7,11},{8,4},{9,5},... | collective-permute-start | bytes 516104 | tf_op jit(solution)/shard_map/ppermute | solution.py:43
  78.0 2.5 %collective-permute-done.13 = bf16[96,896]{1,0:T(8,128)(2,1)S(1)} collective-permute-done((bf16[96,896]{1,0:T(8,128)(2,1)S(1)}, bf16[96,896]{1,0:T(8,128)(2,1)S(1)}, u32[]{:S(2)}, u32[]{:S(2)}) %collective-permute-start.13) | collective-permute-done | bytes 172064 | tf_op jit(solution)/shard_map/ppermute | solution.py:43
  84.6 4.2 %collective-permute-start.24 = (bf16[96,896]{1,0:T(8,128)(2,1)S(1)}, bf16[96,896]{1,0:T(8,128)(2,1)S(1)}, u32[]{:S(2)}, u32[]{:S(2)}) collective-permute-start(bf16[96,896]{1,0:T(8,128)(2,1)S(1)} %get-tuple-element.87), channel_id=1, source_target_pairs={{0,12},{1,13},{2,14},{3,15},{4,8},{5,9},{6,10},{7,11},{8,4},{9,5},... | collective-permute-start | bytes 516104 | tf_op jit(solution)/shard_map/ppermute | solution.py:43
  91.3 4.3 %collective-permute-start.21 = (bf16[192,896]{1,0:T(8,128)(2,1)S(1)}, bf16[192,896]{1,0:T(8,128)(2,1)S(1)}, u32[]{:S(2)}, u32[]{:S(2)}) collective-permute-start(bf16[192,896]{1,0:T(8,128)(2,1)S(1)} %pad_maximum_fusion.4), channel_id=1, source_target_pairs={{0,12},{1,13},{2,14},{3,15},{4,8},{5,9},{6,10},{7,11},{8,4},{9,5},... | collective-permute-start | bytes 1032200 | tf_op jit(solution)/shard_map/ppermute | solution.py:43
  96.3 8.9 %collective-permute-start.27 = (bf16[384,896]{1,0:T(8,128)(2,1)S(1)}, bf16[384,896]{1,0:T(8,128)(2,1)S(1)}, u32[]{:S(2)}, u32[]{:S(2)}) collective-permute-start(bf16[384,896]{1,0:T(8,128)(2,1)S(1)} %pad_maximum_fusion.2.refs_1_), channel_id=1, source_target_pairs={{0,12},{1,13},{2,14},{3,15},{4,8},{5,9},{6,10},{7,11},{8,4},{9,5},... | collective-permute-start | bytes 2064392 | tf_op jit(solution)/shard_map/ppermute | solution.py:43
  106.8 2.1 %collective-permute-start.28 = (bf16[384,896]{1,0:T(8,128)(2,1)S(1)}, bf16[384,896]{1,0:T(8,128)(2,1)S(1)}, u32[]{:S(2)}, u32[]{:S(2)}) collective-permute-start(bf16[384,896]{1,0:T(8,128)(2,1)S(1)} %pad_maximum_fusion.3.refs_2_), channel_id=1, source_target_pairs={{0,2},{1,3},{2,0},{3,1},{4,6},{5,7},{6,4},{7,5},{8,10},{9,11},{10,... | collective-permute-start | bytes 2064392 | tf_op jit(solution)/shard_map/ppermute | solution.py:43
  108.9 5.5 %collective-permute-done.27.refs_4_ = bf16[384,896]{1,0:T(8,128)(2,1)S(1)} collective-permute-done((bf16[384,896]{1,0:T(8,128)(2,1)S(1)}, bf16[384,896]{1,0:T(8,128)(2,1)S(1)}, u32[]{:S(2)}, u32[]{:S(2)}) %collective-permute-start.27) | collective-permute-done | bytes 688160 | tf_op jit(solution)/shard_map/ppermute | solution.py:43
  114.3 1.9 %collective-permute-done.26.refs_3_ = bf16[384,896]{1,0:T(8,128)(2,1)S(1)} collective-permute-done((bf16[384,896]{1,0:T(8,128)(2,1)S(1)}, bf16[384,896]{1,0:T(8,128)(2,1)S(1)}, u32[]{:S(2)}, u32[]{:S(2)}) %collective-permute-start.26) | collective-permute-done | bytes 688160 | tf_op jit(solution)/shard_map/ppermute | solution.py:43
  118.7 3.3 %shard_map.133 = f32[2,768,512]{2,1,0:T(8,128)S(1)} custom-call(bf16[768,2688]{1,0:T(8,128)(2,1)S(1)} %shard_map.131.acts.gg.ug.hid, bf16[2,512,896]{2,1,0:T(8,128)(2,1)S(1)} %collective-permute-done.9.gu_oth.gu, bf16[896,512]{1,0:T(8,128)(2,1)S(1)} %collective-permute-done.10.d_oth.d), custom_call_target="tpu_custom_call" | custom-call | flops 2113929216 | bytes 6881280 | tf_op jit(solution)/shard_map/pallas_call | solution.py:250
  122.0 3.3 %shard_map.132 = f32[2,768,512]{2,1,0:T(8,128)S(1)} custom-call(bf16[768,2688]{1,0:T(8,128)(2,1)S(1)} %shard_map.131.acts.gg.ug.hid, bf16[2,512,896]{2,1,0:T(8,128)(2,1)S(1)} %get-tuple-element.53.gu_own.gu, bf16[896,512]{1,0:T(8,128)(2,1)S(1)} %get-tuple-element.55.d_own.d), custom_call_target="tpu_custom_call" | custom-call | flops 2113929216 | bytes 6881280 | tf_op jit(solution)/shard_map/pallas_call | solution.py:250
  125.3 2.4 %collective-permute-done.29 = f32[2,768,512]{2,1,0:T(8,128)S(1)} collective-permute-done((f32[2,768,512]{2,1,0:T(8,128)S(1)}, f32[2,768,512]{2,1,0:T(8,128)S(1)}, u32[]{:S(2)}, u32[]{:S(2)}) %collective-permute-start.29) | collective-permute-done | bytes 3145760 | tf_op jit(solution)/shard_map/ppermute | solution.py:38
  130.1 3.0 %collective-permute-start.32 = (bf16[2,96,512]{2,1,0:T(8,128)(2,1)S(1)}, bf16[2,96,512]{2,1,0:T(8,128)(2,1)S(1)}, u32[]{:S(2)}, u32[]{:S(2)}) collective-permute-start(bf16[2,96,512]{2,1,0:T(8,128)(2,1)S(1)} %get-tuple-element.65), channel_id=1, source_target_pairs={{0,48},{16,32},{32,16},{48,0},{64,112},{80,96},{96,80},{112,64},{1... | collective-permute-start | bytes 589832 | tf_op jit(solution)/shard_map/ppermute | solution.py:49
  133.2 2.7 %collective-permute-start.33 = (bf16[2,96,512]{2,1,0:T(8,128)(2,1)S(1)}, bf16[2,96,512]{2,1,0:T(8,128)(2,1)S(1)}, u32[]{:S(2)}, u32[]{:S(2)}) collective-permute-start(bf16[2,96,512]{2,1,0:T(8,128)(2,1)S(1)} %get-tuple-element.66), channel_id=1, source_target_pairs={{0,64},{16,80},{32,96},{48,112},{64,0},{80,16},{96,32},{112,48},{1... | collective-permute-start | bytes 589832 | tf_op jit(solution)/shard_map/ppermute | solution.py:49
  136.5 6.5 %shard_map.134 = (bf16[512,1792]{1,0:T(8,128)(2,1)}, bf16[512,1792]{1,0:T(8,128)(2,1)}, bf16[1792,512]{1,0:T(8,128)(2,1)}) custom-call(s32[25]{0:T(128)S(1)} %dynamic-slice_bitcast_fusion.info, s32[4,14]{1,0:T(4,128)S(1)} %copy-done.4, s32[4,14]{1,0:T(4,128)S(1)} %copy-done.6, s32[14,4]{1,0:T(8,128)S(1)} %copy.17.dm, ...), custom_call_target="tpu_custom_call" | custom-call | flops 2113929216 | bytes 6881280 | tf_op jit(solution)/shard_map/pallas_call | solution.py:300
  143.7 1.8 %collective-permute-start.35 = (bf16[2,96,512]{2,1,0:T(8,128)(2,1)S(1)}, bf16[2,96,512]{2,1,0:T(8,128)(2,1)S(1)}, u32[]{:S(2)}, u32[]{:S(2)}) collective-permute-start(bf16[2,96,512]{2,1,0:T(8,128)(2,1)S(1)} %get-tuple-element.75), channel_id=1, source_target_pairs={{0,80},{16,64},{32,112},{48,96},{64,16},{80,0},{96,48},{112,32},{1... | collective-permute-start | bytes 589832 | tf_op jit(solution)/shard_map/ppermute | solution.py:49
  145.5 3.4 %collective-permute-start.36 = (bf16[2,96,512]{2,1,0:T(8,128)(2,1)S(1)}, bf16[2,96,512]{2,1,0:T(8,128)(2,1)S(1)}, u32[]{:S(2)}, u32[]{:S(2)}) collective-permute-start(bf16[2,96,512]{2,1,0:T(8,128)(2,1)S(1)} %get-tuple-element.76), channel_id=1, source_target_pairs={{0,112},{16,96},{32,80},{48,64},{64,48},{80,32},{96,16},{112,0},{1... | collective-permute-start | bytes 589832 | tf_op jit(solution)/shard_map/ppermute | solution.py:49
  149.0 2.8 %collective-permute-start.37 = (bf16[2,96,512]{2,1,0:T(8,128)(2,1)S(1)}, bf16[2,96,512]{2,1,0:T(8,128)(2,1)S(1)}, u32[]{:S(2)}, u32[]{:S(2)}) collective-permute-start(bf16[2,96,512]{2,1,0:T(8,128)(2,1)S(1)} %get-tuple-element.77), channel_id=1, source_target_pairs={{0,96},{16,112},{32,64},{48,80},{64,32},{80,48},{96,0},{112,16},{1... | collective-permute-start | bytes 589832 | tf_op jit(solution)/shard_map/ppermute | solution.py:49
  151.8 6.5 %shard_map.135 = (bf16[512,1792]{1,0:T(8,128)(2,1)}, bf16[512,1792]{1,0:T(8,128)(2,1)}, bf16[1792,512]{1,0:T(8,128)(2,1)}) custom-call(s32[25]{0:T(128)S(1)} %dynamic-slice_bitcast_fusion.info, s32[4,14]{1,0:T(4,128)S(1)} %copy-done.4, s32[4,14]{1,0:T(4,128)S(1)} %copy-done.6, ...), custom_call_target="tpu_custom_call", output_to_operand_aliasing={{0}: (9, {}), {1}: (10, {}), {2}: (11, {})} | custom-call | flops 2113929216 | bytes 6881280 | tf_op jit(solution)/shard_map/pallas_call | solution.py:300
  159.0 3.0 %collective-permute-done.37 = bf16[2,96,512]{2,1,0:T(8,128)(2,1)S(1)} collective-permute-done((bf16[2,96,512]{2,1,0:T(8,128)(2,1)S(1)}, bf16[2,96,512]{2,1,0:T(8,128)(2,1)S(1)}, u32[]{:S(2)}, u32[]{:S(2)}) %collective-permute-start.37) | collective-permute-done | bytes 196640 | tf_op jit(solution)/shard_map/ppermute | solution.py:49
  (98 shorter events, 34.4 us)
Async XLA Ops:
  2.4 18.8 %collective-permute-start.4 = (bf16[96,1024]{1,0:T(8,128)(2,1)S(1)}, bf16[96,1024]{1,0:T(8,128)(2,1)S(1)}, u32[]{:S(2)}, u32[]{:S(2)}) collective-permute-start(bf16[96,1024]{1,0:T(8,128)(2,1)S(1)} %constant_dynamic-update-slice_fusion), channel_id=1, source_target_pairs={{0,80},{16,64},{32,112},{48,96},{64,16},{80,0},{96,48},{112,32},{1... | collective-permute-start | bytes 589832 | tf_op jit(solution)/shard_map/ppermute | solution.py:49
  6.6 14.7 %collective-permute-start.3 = (bf16[96,1024]{1,0:T(8,128)(2,1)S(1)}, bf16[96,1024]{1,0:T(8,128)(2,1)S(1)}, u32[]{:S(2)}, u32[]{:S(2)}) collective-permute-start(bf16[96,1024]{1,0:T(8,128)(2,1)S(1)} %constant_dynamic-update-slice_fusion), channel_id=1, source_target_pairs={{0,32},{16,48},{32,0},{48,16},{64,96},{80,112},{96,64},{112,80},{1... | collective-permute-start | bytes 589832 | tf_op jit(solution)/shard_map/ppermute | solution.py:49
  9.5 11.8 %collective-permute-start.2 = (bf16[96,1024]{1,0:T(8,128)(2,1)S(1)}, bf16[96,1024]{1,0:T(8,128)(2,1)S(1)}, u32[]{:S(2)}, u32[]{:S(2)}) collective-permute-start(bf16[96,1024]{1,0:T(8,128)(2,1)S(1)} %constant_dynamic-update-slice_fusion), channel_id=1, source_target_pairs={{0,64},{16,80},{32,96},{48,112},{64,0},{80,16},{96,32},{112,48},{1... | collective-permute-start | bytes 589832 | tf_op jit(solution)/shard_map/ppermute | solution.py:49
  10.0 11.3 %collective-permute-start.1 = (bf16[96,1024]{1,0:T(8,128)(2,1)S(1)}, bf16[96,1024]{1,0:T(8,128)(2,1)S(1)}, u32[]{:S(2)}, u32[]{:S(2)}) collective-permute-start(bf16[96,1024]{1,0:T(8,128)(2,1)S(1)} %constant_dynamic-update-slice_fusion), channel_id=1, source_target_pairs={{0,48},{16,32},{32,16},{48,0},{64,112},{80,96},{96,80},{112,64},{1... | collective-permute-start | bytes 589832 | tf_op jit(solution)/shard_map/ppermute | solution.py:49
  10.1 11.2 %collective-permute-start = (bf16[96,1024]{1,0:T(8,128)(2,1)S(1)}, bf16[96,1024]{1,0:T(8,128)(2,1)S(1)}, u32[]{:S(2)}, u32[]{:S(2)}) collective-permute-start(bf16[96,1024]{1,0:T(8,128)(2,1)S(1)} %constant_dynamic-update-slice_fusion), channel_id=1, source_target_pairs={{0,16},{16,0},{32,48},{48,32},{64,80},{80,64},{96,112},{112,96},{1... | collective-permute-start | bytes 589832 | tf_op jit(solution)/shard_map/ppermute | solution.py:49
  21.3 19.7 %collective-permute-start.9 = (bf16[2,512,896]{2,1,0:T(8,128)(2,1)S(1)}, bf16[2,512,896]{2,1,0:T(8,128)(2,1)S(1)}, u32[]{:S(2)}, u32[]{:S(2)}) collective-permute-start(bf16[2,512,896]{2,1,0:T(8,128)(2,1)S(1)} %get-tuple-element.54), channel_id=1, source_target_pairs={{0,1},{1,0},{2,3},{3,2},{4,5},{5,4},{6,7},{7,6},{8,9},{9,8},{10,11... | collective-permute-start | bytes 5505032 | tf_op jit(solution)/shard_map/ppermute | solution.py:38
  21.4 17.2 %collective-permute-start.6 = (bf16[96,1024]{1,0:T(8,128)(2,1)S(1)}, bf16[96,1024]{1,0:T(8,128)(2,1)S(1)}, u32[]{:S(2)}, u32[]{:S(2)}) collective-permute-start(bf16[96,1024]{1,0:T(8,128)(2,1)S(1)} %constant_dynamic-update-slice_fusion), channel_id=1, source_target_pairs={{0,96},{16,112},{32,64},{48,80},{64,32},{80,48},{96,0},{112,16},{1... | collective-permute-start | bytes 589832 | tf_op jit(solution)/shard_map/ppermute | solution.py:49
  28.1 10.6 %collective-permute-start.5 = (bf16[96,1024]{1,0:T(8,128)(2,1)S(1)}, bf16[96,1024]{1,0:T(8,128)(2,1)S(1)}, u32[]{:S(2)}, u32[]{:S(2)}) collective-permute-start(bf16[96,1024]{1,0:T(8,128)(2,1)S(1)} %constant_dynamic-update-slice_fusion), channel_id=1, source_target_pairs={{0,112},{16,96},{32,80},{48,64},{64,48},{80,32},{96,16},{112,0},{1... | collective-permute-start | bytes 589832 | tf_op jit(solution)/shard_map/ppermute | solution.py:49
  28.2 10.6 %collective-permute-start.7 = (bf16[384,1024]{1,0:T(8,128)(2,1)S(1)}, bf16[384,1024]{1,0:T(8,128)(2,1)S(1)}, u32[]{:S(2)}, u32[]{:S(2)}) collective-permute-start(bf16[384,1024]{1,0:T(8,128)(2,1)S(1)} %pad_maximum_fusion.own_a), channel_id=1, source_target_pairs={{0,1},{1,0},{2,3},{3,2},{4,5},{5,4},{6,7},{7,6},{8,9},{9,8},{10,11... | collective-permute-start | bytes 2359304 | tf_op jit(solution)/shard_map/ppermute | solution.py:38
  28.4 10.4 %collective-permute-start.10 = (bf16[896,512]{1,0:T(8,128)(2,1)S(1)}, bf16[896,512]{1,0:T(8,128)(2,1)S(1)}, u32[]{:S(2)}, u32[]{:S(2)}) collective-permute-start(bf16[896,512]{1,0:T(8,128)(2,1)S(1)} %get-tuple-element.56), channel_id=1, source_target_pairs={{0,1},{1,0},{2,3},{3,2},{4,5},{5,4},{6,7},{7,6},{8,9},{9,8},{10,11... | collective-permute-start | bytes 2752520 | tf_op jit(solution)/shard_map/ppermute | solution.py:38
  44.5 17.6 %collective-permute-start.11 = (bf16[384,896]{1,0:T(8,128)(2,1)S(1)}, bf16[384,896]{1,0:T(8,128)(2,1)S(1)}, u32[]{:S(2)}, u32[]{:S(2)}) collective-permute-start(bf16[384,896]{1,0:T(8,128)(2,1)S(1)} %get-tuple-element.58), channel_id=1, source_target_pairs={{0,2},{1,3},{2,0},{3,1},{4,6},{5,7},{6,4},{7,5},{8,10},{9,11},{10,... | collective-permute-start | bytes 2064392 | tf_op jit(solution)/shard_map/ppermute | solution.py:43
  45.2 19.5 %collective-permute-start.14 = (bf16[384,896]{1,0:T(8,128)(2,1)S(1)}, bf16[384,896]{1,0:T(8,128)(2,1)S(1)}, u32[]{:S(2)}, u32[]{:S(2)}) collective-permute-start(bf16[384,896]{1,0:T(8,128)(2,1)S(1)} %get-tuple-element.60), channel_id=1, source_target_pairs={{0,12},{1,13},{2,14},{3,15},{4,8},{5,9},{6,10},{7,11},{8,4},{9,5},... | collective-permute-start | bytes 2064392 | tf_op jit(solution)/shard_map/ppermute | solution.py:43
  49.2 18.4 %collective-permute-start.17 = (bf16[384,896]{1,0:T(8,128)(2,1)S(1)}, bf16[384,896]{1,0:T(8,128)(2,1)S(1)}, u32[]{:S(2)}, u32[]{:S(2)}) collective-permute-start(bf16[384,896]{1,0:T(8,128)(2,1)S(1)} %get-tuple-element.62), channel_id=1, source_target_pairs={{0,4},{1,5},{2,6},{3,7},{4,0},{5,1},{6,2},{7,3},{8,12},{9,13},{10,... | collective-permute-start | bytes 2064392 | tf_op jit(solution)/shard_map/ppermute | solution.py:43
  62.3 11.2 %collective-permute-start.12 = (bf16[192,896]{1,0:T(8,128)(2,1)S(1)}, bf16[192,896]{1,0:T(8,128)(2,1)S(1)}, u32[]{:S(2)}, u32[]{:S(2)}) collective-permute-start(bf16[192,896]{1,0:T(8,128)(2,1)S(1)} %slice.108), channel_id=1, source_target_pairs={{0,4},{1,5},{2,6},{3,7},{4,0},{5,1},{6,2},{7,3},{8,12},{9,13},{10,... | collective-permute-start | bytes 1032200 | tf_op jit(solution)/shard_map/ppermute | solution.py:43
  64.9 11.0 %collective-permute-start.15 = (bf16[192,896]{1,0:T(8,128)(2,1)S(1)}, bf16[192,896]{1,0:T(8,128)(2,1)S(1)}, u32[]{:S(2)}, u32[]{:S(2)}) collective-permute-start(bf16[192,896]{1,0:T(8,128)(2,1)S(1)} %slice.107), channel_id=1, source_target_pairs={{0,2},{1,3},{2,0},{3,1},{4,6},{5,7},{6,4},{7,5},{8,10},{9,11},{10,... | collective-permute-start | bytes 1032200 | tf_op jit(solution)/shard_map/ppermute | solution.py:43
  67.8 9.7 %collective-permute-start.18 = (bf16[192,896]{1,0:T(8,128)(2,1)S(1)}, bf16[192,896]{1,0:T(8,128)(2,1)S(1)}, u32[]{:S(2)}, u32[]{:S(2)}) collective-permute-start(bf16[192,896]{1,0:T(8,128)(2,1)S(1)} %slice.106), channel_id=1, source_target_pairs={{0,12},{1,13},{2,14},{3,15},{4,8},{5,9},{6,10},{7,11},{8,4},{9,5},... | collective-permute-start | bytes 1032200 | tf_op jit(solution)/shard_map/ppermute | solution.py:43
  84.0 7.3 %collective-permute-start.20 = (bf16[96,896]{1,0:T(8,128)(2,1)S(1)}, bf16[96,896]{1,0:T(8,128)(2,1)S(1)}, u32[]{:S(2)}, u32[]{:S(2)}) collective-permute-start(bf16[96,896]{1,0:T(8,128)(2,1)S(1)} %get-tuple-element.88), channel_id=1, source_target_pairs={{0,2},{1,3},{2,0},{3,1},{4,6},{5,7},{6,4},{7,5},{8,10},{9,11},{10,... | collective-permute-start | bytes 516104 | tf_op jit(solution)/shard_map/ppermute | solution.py:43
  84.6 11.1 %collective-permute-start.24 = (bf16[96,896]{1,0:T(8,128)(2,1)S(1)}, bf16[96,896]{1,0:T(8,128)(2,1)S(1)}, u32[]{:S(2)}, u32[]{:S(2)}) collective-permute-start(bf16[96,896]{1,0:T(8,128)(2,1)S(1)} %get-tuple-element.87), channel_id=1, source_target_pairs={{0,12},{1,13},{2,14},{3,15},{4,8},{5,9},{6,10},{7,11},{8,4},{9,5},... | collective-permute-start | bytes 516104 | tf_op jit(solution)/shard_map/ppermute | solution.py:43
  88.9 7.3 %collective-permute-start.23 = (bf16[192,896]{1,0:T(8,128)(2,1)S(1)}, bf16[192,896]{1,0:T(8,128)(2,1)S(1)}, u32[]{:S(2)}, u32[]{:S(2)}) collective-permute-start(bf16[192,896]{1,0:T(8,128)(2,1)S(1)} %pad_maximum_fusion.5), channel_id=1, source_target_pairs={{0,2},{1,3},{2,0},{3,1},{4,6},{5,7},{6,4},{7,5},{8,10},{9,11},{10,... | collective-permute-start | bytes 1032200 | tf_op jit(solution)/shard_map/ppermute | solution.py:43
  91.3 13.9 %collective-permute-start.21 = (bf16[192,896]{1,0:T(8,128)(2,1)S(1)}, bf16[192,896]{1,0:T(8,128)(2,1)S(1)}, u32[]{:S(2)}, u32[]{:S(2)}) collective-permute-start(bf16[192,896]{1,0:T(8,128)(2,1)S(1)} %pad_maximum_fusion.4), channel_id=1, source_target_pairs={{0,12},{1,13},{2,14},{3,15},{4,8},{5,9},{6,10},{7,11},{8,4},{9,5},... | collective-permute-start | bytes 1032200 | tf_op jit(solution)/shard_map/ppermute | solution.py:43
  95.6 11.1 %collective-permute-start.25 = (bf16[192,896]{1,0:T(8,128)(2,1)S(1)}, bf16[192,896]{1,0:T(8,128)(2,1)S(1)}, u32[]{:S(2)}, u32[]{:S(2)}) collective-permute-start(bf16[192,896]{1,0:T(8,128)(2,1)S(1)} %pad_maximum_fusion.6), channel_id=1, source_target_pairs={{0,4},{1,5},{2,6},{3,7},{4,0},{5,1},{6,2},{7,3},{8,12},{9,13},{10,... | collective-permute-start | bytes 1032200 | tf_op jit(solution)/shard_map/ppermute | solution.py:43
  96.3 18.1 %collective-permute-start.27 = (bf16[384,896]{1,0:T(8,128)(2,1)S(1)}, bf16[384,896]{1,0:T(8,128)(2,1)S(1)}, u32[]{:S(2)}, u32[]{:S(2)}) collective-permute-start(bf16[384,896]{1,0:T(8,128)(2,1)S(1)} %pad_maximum_fusion.2.refs_1_), channel_id=1, source_target_pairs={{0,12},{1,13},{2,14},{3,15},{4,8},{5,9},{6,10},{7,11},{8,4},{9,5},... | collective-permute-start | bytes 2064392 | tf_op jit(solution)/shard_map/ppermute | solution.py:43
  105.3 11.0 %collective-permute-start.26 = (bf16[384,896]{1,0:T(8,128)(2,1)S(1)}, bf16[384,896]{1,0:T(8,128)(2,1)S(1)}, u32[]{:S(2)}, u32[]{:S(2)}) collective-permute-start(bf16[384,896]{1,0:T(8,128)(2,1)S(1)} %pad_maximum_fusion.1.refs_0_), channel_id=1, source_target_pairs={{0,4},{1,5},{2,6},{3,7},{4,0},{5,1},{6,2},{7,3},{8,12},{9,13},{10,... | collective-permute-start | bytes 2064392 | tf_op jit(solution)/shard_map/ppermute | solution.py:43
  106.8 11.0 %collective-permute-start.28 = (bf16[384,896]{1,0:T(8,128)(2,1)S(1)}, bf16[384,896]{1,0:T(8,128)(2,1)S(1)}, u32[]{:S(2)}, u32[]{:S(2)}) collective-permute-start(bf16[384,896]{1,0:T(8,128)(2,1)S(1)} %pad_maximum_fusion.3.refs_2_), channel_id=1, source_target_pairs={{0,2},{1,3},{2,0},{3,1},{4,6},{5,7},{6,4},{7,5},{8,10},{9,11},{10,... | collective-permute-start | bytes 2064392 | tf_op jit(solution)/shard_map/ppermute | solution.py:43
  128.6 15.1 %collective-permute-start.30 = (bf16[768,2688]{1,0:T(8,128)(2,1)S(1)}, bf16[768,2688]{1,0:T(8,128)(2,1)S(1)}, u32[]{:S(2)}, u32[]{:S(2)}) collective-permute-start(bf16[768,2688]{1,0:T(8,128)(2,1)S(1)} %shard_map.131.acts.gg.ug.hid), channel_id=1, source_target_pairs={{0,1},{1,0},{2,3},{3,2},{4,5},{5,4},{6,7},{7,6},{8,9},{9,8},{10,11... | collective-permute-start | bytes 12386312 | tf_op jit(solution)/shard_map/ppermute | solution.py:38
  128.8 14.1 %collective-permute-start.31 = (bf16[2,96,512]{2,1,0:T(8,128)(2,1)S(1)}, bf16[2,96,512]{2,1,0:T(8,128)(2,1)S(1)}, u32[]{:S(2)}, u32[]{:S(2)}) collective-permute-start(bf16[2,96,512]{2,1,0:T(8,128)(2,1)S(1)} %get-tuple-element.64), channel_id=1, source_target_pairs={{0,16},{16,0},{32,48},{48,32},{64,80},{80,64},{96,112},{112,96},{1... | collective-permute-start | bytes 589832 | tf_op jit(solution)/shard_map/ppermute | solution.py:49
  130.1 12.8 %collective-permute-start.32 = (bf16[2,96,512]{2,1,0:T(8,128)(2,1)S(1)}, bf16[2,96,512]{2,1,0:T(8,128)(2,1)S(1)}, u32[]{:S(2)}, u32[]{:S(2)}) collective-permute-start(bf16[2,96,512]{2,1,0:T(8,128)(2,1)S(1)} %get-tuple-element.65), channel_id=1, source_target_pairs={{0,48},{16,32},{32,16},{48,0},{64,112},{80,96},{96,80},{112,64},{1... | collective-permute-start | bytes 589832 | tf_op jit(solution)/shard_map/ppermute | solution.py:49
  133.2 9.8 %collective-permute-start.33 = (bf16[2,96,512]{2,1,0:T(8,128)(2,1)S(1)}, bf16[2,96,512]{2,1,0:T(8,128)(2,1)S(1)}, u32[]{:S(2)}, u32[]{:S(2)}) collective-permute-start(bf16[2,96,512]{2,1,0:T(8,128)(2,1)S(1)} %get-tuple-element.66), channel_id=1, source_target_pairs={{0,64},{16,80},{32,96},{48,112},{64,0},{80,16},{96,32},{112,48},{1... | collective-permute-start | bytes 589832 | tf_op jit(solution)/shard_map/ppermute | solution.py:49
  135.9 7.8 %collective-permute-start.34 = (bf16[2,96,512]{2,1,0:T(8,128)(2,1)S(1)}, bf16[2,96,512]{2,1,0:T(8,128)(2,1)S(1)}, u32[]{:S(2)}, u32[]{:S(2)}) collective-permute-start(bf16[2,96,512]{2,1,0:T(8,128)(2,1)S(1)} %get-tuple-element.67), channel_id=1, source_target_pairs={{0,32},{16,48},{32,0},{48,16},{64,96},{80,112},{96,64},{112,80},{1... | collective-permute-start | bytes 589832 | tf_op jit(solution)/shard_map/ppermute | solution.py:49
  143.7 14.5 %collective-permute-start.35 = (bf16[2,96,512]{2,1,0:T(8,128)(2,1)S(1)}, bf16[2,96,512]{2,1,0:T(8,128)(2,1)S(1)}, u32[]{:S(2)}, u32[]{:S(2)}) collective-permute-start(bf16[2,96,512]{2,1,0:T(8,128)(2,1)S(1)} %get-tuple-element.75), channel_id=1, source_target_pairs={{0,80},{16,64},{32,112},{48,96},{64,16},{80,0},{96,48},{112,32},{1... | collective-permute-start | bytes 589832 | tf_op jit(solution)/shard_map/ppermute | solution.py:49
  145.5 13.5 %collective-permute-start.36 = (bf16[2,96,512]{2,1,0:T(8,128)(2,1)S(1)}, bf16[2,96,512]{2,1,0:T(8,128)(2,1)S(1)}, u32[]{:S(2)}, u32[]{:S(2)}) collective-permute-start(bf16[2,96,512]{2,1,0:T(8,128)(2,1)S(1)} %get-tuple-element.76), channel_id=1, source_target_pairs={{0,112},{16,96},{32,80},{48,64},{64,48},{80,32},{96,16},{112,0},{1... | collective-permute-start | bytes 589832 | tf_op jit(solution)/shard_map/ppermute | solution.py:49
  149.0 13.0 %collective-permute-start.37 = (bf16[2,96,512]{2,1,0:T(8,128)(2,1)S(1)}, bf16[2,96,512]{2,1,0:T(8,128)(2,1)S(1)}, u32[]{:S(2)}, u32[]{:S(2)}) collective-permute-start(bf16[2,96,512]{2,1,0:T(8,128)(2,1)S(1)} %get-tuple-element.77), channel_id=1, source_target_pairs={{0,96},{16,112},{32,64},{48,80},{64,32},{80,48},{96,0},{112,16},{1... | collective-permute-start | bytes 589832 | tf_op jit(solution)/shard_map/ppermute | solution.py:49
  (13 other events, 53.4 us)

commit v3 on v2

--- a/solution.py
+++ b/solution.py
@@ -16,9 +16,6 @@
 RING = {bits: pos for pos, bits in enumerate(GRAY)}
 MASK = {"A": 4, "B": 2, "X": 1}
 ORDERS = ("ABX", "BXA", "XAB")
-NEAR = ("", "A", "B", "X")
-FAR = ("AB", "AX", "BX", "ABX")
-
 
 def flip_ring(pos, dims):
     bit_a, bit_b = GRAY[pos]
@@ -71,7 +68,7 @@
 PARAMS = pltpu.CompilerParams(vmem_limit_bytes=24 * 1024 * 1024)
 
 
-def call(kernel, prefetch, grid, in_specs, out_specs, out_shape, scratch=(), flops=0, size=0, **more):
+def call(kernel, prefetch, grid, in_specs, out_specs, out_shape, scratch=(), flops=0, size=0, params=PARAMS, **more):
     return pl.pallas_call(
         kernel,
         grid_spec=pltpu.PrefetchScalarGridSpec(
@@ -82,7 +79,7 @@
             scratch_shapes=list(scratch),
         ),
         out_shape=out_shape,
-        compiler_params=PARAMS,
+        compiler_params=params,
         cost_estimate=pl.CostEstimate(flops=flops, bytes_accessed=size, transcendentals=0),
         **more,
     )
@@ -101,52 +98,48 @@
 
 
 def prepare_kernel(info, gm, um, dm, gk, gs, uk, us, dk, ds, gu_keep, gu_send, d_keep, d_send):
-    j = pl.program_id(0)
-    blocks, halves = gk.shape[0] // BLK, pl.num_programs(0)
+    f = pl.program_id(0)
+    n = gk.shape[1] // BLK
     for side, (g, u, d, gu_out, d_out) in enumerate(
         ((gk, uk, dk, gu_keep, d_keep), (gs, us, ds, gu_send, d_send))
     ):
-        core = info[0] if side == 0 else 1 - info[0]
-        at = core * halves + j
-        for f in range(blocks):
-            rows = slice(f * BLK, (f + 1) * BLK)
-            gu_out[0, rows, :] = times(g[rows, :], gm[f, at])
-            gu_out[1, rows, :] = times(u[rows, :], um[f, at])
-            d_out[:, rows] = times(d[:, rows], dm[at, f])
+        first = (info[0] if side == 0 else 1 - info[0]) * n
+        for j in range(n):
+            at = slice(j * BLK, (j + 1) * BLK)
+            gu_out[0, :, at] = times(g[:, at], gm[f, first + j])
+            gu_out[1, :, at] = times(u[:, at], um[f, first + j])
+            d_out[at, :] = times(d[at, :], dm[first + j, f])
 
 
 def prepare(info, gm, um, dm, gate_weight, up_weight, down_weight):
     width, hidden = gate_weight.shape
-    half, n = hidden // 2, hidden // 2 // BLK
+    half = hidden // 2
 
     def wide(side):
-        return pl.BlockSpec(
-            (width, BLK), lambda j, info, *_: (0, (info[0] if side == 0 else 1 - info[0]) * n + j)
-        )
+        return pl.BlockSpec((BLK, half), lambda f, info, *_: (f, info[0] if side == 0 else 1 - info[0]))
 
     def tall(side):
-        return pl.BlockSpec(
-            (BLK, width), lambda j, info, *_: ((info[0] if side == 0 else 1 - info[0]) * n + j, 0)
-        )
-
-    gu_spec = pl.BlockSpec((2, width, BLK), lambda j, *_: (0, 0, j))
-    d_spec = pl.BlockSpec((BLK, width), lambda j, *_: (j, 0))
+        return pl.BlockSpec((half, BLK), lambda f, info, *_: (info[0] if side == 0 else 1 - info[0], f))
+
+    gu_spec = pl.BlockSpec((2, BLK, half), lambda f, *_: (0, f, 0))
+    d_spec = pl.BlockSpec((half, BLK), lambda f, *_: (0, f))
     return call(
         prepare_kernel,
         4,
-        (n,),
+        (width // BLK,),
         [wide(0), wide(1), wide(0), wide(1), tall(0), tall(1)],
         [gu_spec, gu_spec, d_spec, d_spec],
         [shape((2, width, half), BF)] * 2 + [shape((half, width), BF)] * 2,
         size=12 * width * hidden,
+        params=pltpu.CompilerParams(vmem_limit_bytes=52 * 1024 * 1024),
     )(info, gm, um, dm, gate_weight, gate_weight, up_weight, up_weight, down_weight, down_weight)
 
 
-def project_kernel(info, own_a, own_b, oth_a, oth_b, gu_own, gu_oth, d_own, d_oth, *refs, base):
-    outs, panel = refs[:3], refs[3]
+def project_kernel(info, own_a, own_b, oth_a, oth_b, *refs, base, parts):
+    outs, panel = refs[-1 - len(parts) : -1], refs[-1]
     rows, width = own_a.shape[0], own_a.shape[1] // 2
     r = rows // 4
-    for q in range(3):
+    for n, q in enumerate(parts):
         cols = slice(0, width) if q < 2 else slice(width, 2 * width)
         for k in range(4):
             at = info[1 + 8 * q + base + k]
@@ -155,35 +148,46 @@
 
             @pl.when(at < 4)
             def _():
-                panel[q, to, :width] = own_a[row, cols]
-                panel[q, to, width:] = oth_a[row, cols]
+                panel[n, to, :width] = own_a[row, cols]
+                panel[n, to, width:] = oth_a[row, cols]
 
             @pl.when(at >= 4)
             def _():
-                panel[q, to, :width] = own_b[row, cols]
-                panel[q, to, width:] = oth_b[row, cols]
-
-    for q in range(2):
-        w = jnp.concatenate([gu_own[q], gu_oth[q]], axis=0)
-        outs[q][...] = dot(panel[q], w).astype(outs[q].dtype)
-    w = jnp.concatenate([d_own[...], d_oth[...]], axis=1)
-    outs[2][...] = dot(panel[2], w, NT).astype(outs[2].dtype)
-
-
-def project(info, panels, weights, base, kind):
+                panel[n, to, :width] = own_b[row, cols]
+                panel[n, to, width:] = oth_b[row, cols]
+
+    for n, q in enumerate(parts):
+        w_own, w_oth = refs[2 * n], refs[2 * n + 1]
+        if q < 2:
+            w, dims = jnp.concatenate([w_own[0], w_oth[0]], axis=0), ((1,), (0,))
+        else:
+            w, dims = jnp.concatenate([w_own[...], w_oth[...]], axis=1), NT
+        outs[n][...] = dot(panel[n], w, dims).astype(outs[n].dtype)
+
+
+def project(info, panels, weights, base, parts, kind):
     rows, width = panels[0].shape[0], panels[0].shape[1] // 2
-    count = weights[2].shape[0]
-    return call(
-        functools.partial(project_kernel, base=base),
+    gu_own, gu_oth, d_own, d_oth = weights
+    count = d_own.shape[0]
+    args, specs = [], []
+    for q in parts:
+        if q < 2:
+            args += [gu_own, gu_oth]
+            specs += [pl.BlockSpec((1, width, count), lambda i, *_, q=q: (q, 0, 0))] * 2
+        else:
+            args += [d_own, d_oth]
+            specs += [whole(d_own.shape)] * 2
+    return call(
+        functools.partial(project_kernel, base=base, parts=parts),
         1,
         (1,),
-        [whole(v.shape) for v in (*panels, *weights)],
-        [whole((rows, count))] * 3,
-        [shape((rows, count), kind)] * 3,
-        [pltpu.VMEM((3, rows, 2 * width), BF)],
-        flops=12 * rows * width * count,
-        size=12 * rows * count + 12 * width * count + 8 * rows * width,
-    )(info, *panels, *weights)
+        [whole(v.shape) for v in panels] + specs,
+        [whole((rows, count))] * len(parts),
+        [shape((rows, count), kind)] * len(parts),
+        [pltpu.VMEM((len(parts), rows, 2 * width), BF)],
+        flops=4 * rows * width * count * len(parts),
+        size=4 * (rows + width) * count * len(parts) + 8 * rows * width,
+    )(info, *panels, *args)
 
 
 def pointwise(gate_proj, up_proj, hidden_grad):
@@ -321,32 +325,35 @@
 ):
     masks = (gate_mask, up_mask, down_mask)
     info = lax.dynamic_index_in_dim(jnp.asarray(make_table()), lax.axis_index("col"), 0, keepdims=False)
-    names = NEAR[1:] + FAR
     both = jnp.concatenate([tokens, cotangent], axis=1)
-    got = [swap_row(both, d) for d in names[:5]]
+    x, a, b, ab = (swap_row(both, d) for d in ("X", "A", "B", "AB"))
     gu_own, gu_send, d_own, d_send = prepare(info, *masks, gate_weight, up_weight, down_weight)
-    late, gu_send, d_send, *got = lax.optimization_barrier((both, gu_send, d_send, *got))
+    gu_send, d_send, x, a, b, ab = lax.optimization_barrier((gu_send, d_send, x, a, b, ab))
+    ax, bx, abx = swap_row(x, "A"), swap_row(x, "B"), swap_row(ab, "X")
     gu_oth, d_oth = swap_core(gu_send), swap_core(d_send)
-    got += [swap_row(late, d) for d in names[5:]]
-    own = [jnp.concatenate(blocks, axis=0) for blocks in ([both, *got[:3]], got[3:])]
+    own = [jnp.concatenate(blocks, axis=0) for blocks in ([both, x, ax, bx], [abx, ab, a, b])]
     oth = [swap_core(panel) for panel in own]
 
     panels, weights = (*own, *oth), (gu_own, gu_oth, d_own, d_oth)
-    sends = project(info, panels, weights, 4, BF)
-    keeps = project(info, panels, weights, 0, F32)
+    sends = [project(info, panels, weights, 4, (q,), BF)[0] for q in range(3)]
+    keeps = project(info, panels, weights, 0, (0, 1, 2), F32)
     acts = gather(info, exchange(sends, keeps))
 
     got = swap_core(backward(acts, gu_oth, d_oth, F32))
     part = backward(acts, gu_own, d_own, F32) + got
     parts = jnp.split(part, 8, axis=1)
-    acts, *blocks = lax.optimization_barrier([acts] + [p.astype(BF) for p in parts[1:]])
-    got = [swap_row(block, d) for block, d in zip(blocks[:4], names[:4])]
+    own_part, x, ax, bx, abx, ab, a, b = parts
+    acts, ax, bx, abx, a, b = lax.optimization_barrier([acts] + [v.astype(BF) for v in (ax, bx, abx, a, b)])
+    ax, bx, abx = swap_row(ax, "A"), swap_row(bx, "B"), swap_row(abx, "X")
     sib = swap_core(acts)
     partial = grads(info, masks, own, acts)
-    sib, *rest = lax.optimization_barrier([sib] + got + blocks[4:])
-    got = rest[:4] + [swap_row(block, d) for block, d in zip(rest[4:], names[4:])]
+    x = x + ax.astype(F32) + bx.astype(F32)
+    ab = (ab + abx.astype(F32)).astype(BF)
+    sib, x, ab, a, b, *partial = lax.optimization_barrier((sib, x, ab, a, b, *partial))
+    got = [swap_row(v, d) for v, d in ((ab, "AB"), (x, "X"), (a, "A"), (b, "B"))]
     weight_grads = grads(info, masks, own, sib, partial)
-    total = parts[0]
+    *weight_grads, got = lax.optimization_barrier((*weight_grads, got))
+    total = own_part
     for block in got:
         total = total + block.astype(F32)
     total = total.astype(BF)

time: 163 us -> 144 us (0.88)
  starting transfers between devices: 67.2 us -> 43.2 us
  waiting for transfers between devices: 51.8 us -> 57.1 us
  local copies, waits for them, and re-layouts: 10.2 us -> 5.63 us
  Pallas kernels: 30.6 us -> 34.8 us
    ppermute x18, starting transfers between devices: 35.5 us -> 20.2 us  [swap_cube(): lax.ppermute(part, 'col', [(i, flip_col(i, order[step])) for i in range(1...]
    ppermute x18, waiting for transfers between devices: 32.9 us -> 46.2 us  [swap_cube(): lax.ppermute(part, 'col', [(i, flip_col(i, order[step])) for i in range(1...]
    ppermute x14, waiting for transfers between devices: 14.4 us -> 6.22 us  [swap_row(): lax.ppermute(value, 'row', [(i, flip_row(i, dims)) for i in range(8)])]
    ppermute x14, starting transfers between devices: 30.6 us -> 22.5 us  [swap_row(): lax.ppermute(value, 'row', [(i, flip_row(i, dims)) for i in range(8)])]
    unnamed x19 -> x11, local copies, waits for them, and re-layouts: 7.58 us -> 3.08 us
    pallas_call x3 -> x5, Pallas kernels: 10.3 us -> 14.5 us  [the longest x4 8.34 us: project(): call(functools.partial(project_kernel, base=base, parts=parts), 1, (1,),...]
  transfers between devices with their start and end apart: 38 -> 38, of which waited for: 20 -> 21; matrix products, arithmetic and copies ran while one was open for 2% -> 2% of each run, Pallas kernels for 14% -> 21%
where the time goes in v3:
time: 144 us
  waiting for transfers between devices  57.1 us (40%)
  starting transfers between devices  43.2 us (30%)
  Pallas kernels  34.8 us (24%)
  local copies, waits for them, and re-layouts  5.63 us (4%)
  other arithmetic  2.36 us (2%)
    ppermute x18, waiting for transfers between devices, swap_cube(): lax.ppermute(part, 'col', [(i, flip_col(i, order[step])) for i in range(1...  46.2 us
    ppermute x14, starting transfers between devices, swap_row(): lax.ppermute(value, 'row', [(i, flip_row(i, dims)) for i in range(8)])  22.5 us
    ppermute x18, starting transfers between devices, swap_cube(): lax.ppermute(part, 'col', [(i, flip_col(i, order[step])) for i in range(1...  20.2 us
    pallas_call x2, Pallas kernels, grads(): call(functools.partial(grads_kernel, mine=not into), 4, (n,), [whole(v.sh...  12.9 us
    pallas_call x4, Pallas kernels, project(): call(functools.partial(project_kernel, base=base, parts=parts), 1, (1,),...  8.34 us
    pallas_call x2, Pallas kernels, backward(): call(backward_kernel, 0, (width // step,), [whole(acts.shape), pl.BlockSp...  6.57 us
    ppermute x14, waiting for transfers between devices, swap_row(): lax.ppermute(value, 'row', [(i, flip_row(i, dims)) for i in range(8)])  6.22 us
    pallas_call x1, Pallas kernels, prepare(): call(prepare_kernel, 4, (width // BLK,), [wide(0), wide(1), wide(0), wide...  6.17 us
  transfers between devices with their start and end apart: 38, of which 21 were waited for; matrix products, arithmetic and copies ran while one was open for 2% of the time, Pallas kernels for 21%

profile of v3, /device:TPU:0, one launch (start us, length us, event | category | flops | bytes accessed | tf_op | source)
XLA Modules:
  0.0 144.0 jit_solution(10855333869393262329)
XLA Ops:
  2.4 3.3 %collective-permute-start.3 = (bf16[96,1024]{1,0:T(8,128)(2,1)S(1)}, bf16[96,1024]{1,0:T(8,128)(2,1)S(1)}, u32[]{:S(2)}, u32[]{:S(2)}) collective-permute-start(bf16[96,1024]{1,0:T(8,128)(2,1)S(1)} %constant_dynamic-update-slice_fusion), channel_id=1, source_target_pairs={{0,32},{16,48},{32,0},{48,16},{64,96},{80,112},{96,64},{112,80},{1... | collective-permute-start | bytes 589832 | tf_op jit(solution)/shard_map/ppermute | solution.py:46
  6.8 3.0 %collective-permute-start = (bf16[96,1024]{1,0:T(8,128)(2,1)S(1)}, bf16[96,1024]{1,0:T(8,128)(2,1)S(1)}, u32[]{:S(2)}, u32[]{:S(2)}) collective-permute-start(bf16[96,1024]{1,0:T(8,128)(2,1)S(1)} %constant_dynamic-update-slice_fusion), channel_id=1, source_target_pairs={{0,64},{16,80},{32,96},{48,112},{64,0},{80,16},{96,32},{112,48},{1... | collective-permute-start | bytes 589832 | tf_op jit(solution)/shard_map/ppermute | solution.py:46
  12.6 6.2 %shard_map.128 = (bf16[2,512,896]{2,1,0:T(8,128)(2,1)}, bf16[2,512,896]{2,1,0:T(8,128)(2,1)}, bf16[896,512]{1,0:T(8,128)(2,1)S(1)}, bf16[896,512]{1,0:T(8,128)(2,1)S(1)}) custom-call(s32[25]{0:T(128)S(1)} %dynamic-slice_bitcast_fusion.info, s32[4,14]{1,0:T(4,128)S(1)} %copy-done.1, s32[4,14]{1,0:T(4,128)S(1)} %copy-done.2, s32[14,4]{1,0:T(8,128)S(1)} %copy.17.dm, ...), custom_call_target="tpu_custom_call" | custom-call | bytes 11010048 | tf_op jit(solution)/shard_map/pallas_call | solution.py:126
  19.4 2.3 %collective-permute-start.5 = (bf16[96,1024]{1,0:T(8,128)(2,1)S(1)}, bf16[96,1024]{1,0:T(8,128)(2,1)S(1)}, u32[]{:S(2)}, u32[]{:S(2)}) collective-permute-start(bf16[96,1024]{1,0:T(8,128)(2,1)S(1)} %collective-permute-done), channel_id=1, source_target_pairs={{0,48},{16,32},{32,16},{48,0},{64,112},{80,96},{96,80},{112,64},{1... | collective-permute-start | bytes 589832 | tf_op jit(solution)/shard_map/ppermute | solution.py:46
  23.0 3.2 %collective-permute-done.6 = bf16[96,1024]{1,0:T(8,128)(2,1)S(1)} collective-permute-done((bf16[96,1024]{1,0:T(8,128)(2,1)S(1)}, bf16[96,1024]{1,0:T(8,128)(2,1)S(1)}, u32[]{:S(2)}, u32[]{:S(2)}) %collective-permute-start.6) | collective-permute-done | bytes 196640 | tf_op jit(solution)/shard_map/ppermute | solution.py:46
  28.9 2.3 %collective-permute-done.7.oth_a = bf16[384,1024]{1,0:T(8,128)(2,1)S(1)} collective-permute-done((bf16[384,1024]{1,0:T(8,128)(2,1)S(1)}, bf16[384,1024]{1,0:T(8,128)(2,1)S(1)}, u32[]{:S(2)}, u32[]{:S(2)}) %collective-permute-start.7) | collective-permute-done | bytes 786464 | tf_op jit(solution)/shard_map/ppermute | solution.py:35
  31.1 1.6 %shard_map.130 = bf16[384,896]{1,0:T(8,128)(2,1)S(1)} custom-call(s32[25]{0:T(128)S(1)} %dynamic-slice_bitcast_fusion.info, bf16[384,1024]{1,0:T(8,128)(2,1)S(1)} %pad_maximum_fusion.own_a, bf16[384,1024]{1,0:T(8,128)(2,1)S(1)} %constant_dynamic-update-slice_fusion.2.own_b, bf16[384,1024]{1,0:T(8,128)(2,1)S(1)} %collective-permute-done.7.oth_a, ...), custom_call_target="tpu_custom_call" | custom-call | flops 704643072 | bytes 4784128 | tf_op jit(solution)/shard_map/pallas_call | solution.py:180
  36.0 4.1 %collective-permute-start.14 = (bf16[384,896]{1,0:T(8,128)(2,1)S(1)}, bf16[384,896]{1,0:T(8,128)(2,1)S(1)}, u32[]{:S(2)}, u32[]{:S(2)}) collective-permute-start(bf16[384,896]{1,0:T(8,128)(2,1)S(1)} %shard_map.131), channel_id=1, source_target_pairs={{0,12},{1,13},{2,14},{3,15},{4,8},{5,9},{6,10},{7,11},{8,4},{9,5},... | collective-permute-start | bytes 2064392 | tf_op jit(solution)/shard_map/ppermute | solution.py:40
  41.8 3.5 %shard_map.129 = (f32[384,896]{1,0:T(8,128)S(1)}, f32[384,896]{1,0:T(8,128)S(1)}, f32[384,896]{1,0:T(8,128)S(1)}) custom-call(s32[25]{0:T(128)S(1)} %dynamic-slice_bitcast_fusion.info, bf16[384,1024]{1,0:T(8,128)(2,1)S(1)} %pad_maximum_fusion.own_a, bf16[384,1024]{1,0:T(8,128)(2,1)S(1)} %constant_dynamic-update-slice_fusion.2.own_b, ...), custom_call_target="tpu_custom_call" | custom-call | flops 2113929216 | bytes 11206656 | tf_op jit(solution)/shard_map/pallas_call | solution.py:180
  45.3 5.1 %collective-permute-done.11 = bf16[384,896]{1,0:T(8,128)(2,1)S(1)} collective-permute-done((bf16[384,896]{1,0:T(8,128)(2,1)S(1)}, bf16[384,896]{1,0:T(8,128)(2,1)S(1)}, u32[]{:S(2)}, u32[]{:S(2)}) %collective-permute-start.11) | collective-permute-done | bytes 688160 | tf_op jit(solution)/shard_map/ppermute | solution.py:40
  50.5 2.0 %collective-permute-start.12 = (bf16[192,896]{1,0:T(8,128)(2,1)S(1)}, bf16[192,896]{1,0:T(8,128)(2,1)S(1)}, u32[]{:S(2)}, u32[]{:S(2)}) collective-permute-start(bf16[192,896]{1,0:T(8,128)(2,1)S(1)} %slice.108), channel_id=1, source_target_pairs={{0,4},{1,5},{2,6},{3,7},{4,0},{5,1},{6,2},{7,3},{8,12},{9,13},{10,... | collective-permute-start | bytes 1032200 | tf_op jit(solution)/shard_map/ppermute | solution.py:40
  52.5 3.1 %collective-permute-done.14 = bf16[384,896]{1,0:T(8,128)(2,1)S(1)} collective-permute-done((bf16[384,896]{1,0:T(8,128)(2,1)S(1)}, bf16[384,896]{1,0:T(8,128)(2,1)S(1)}, u32[]{:S(2)}, u32[]{:S(2)}) %collective-permute-start.14) | collective-permute-done | bytes 688160 | tf_op jit(solution)/shard_map/ppermute | solution.py:40
  56.3 3.8 %collective-permute-done.17 = bf16[384,896]{1,0:T(8,128)(2,1)S(1)} collective-permute-done((bf16[384,896]{1,0:T(8,128)(2,1)S(1)}, bf16[384,896]{1,0:T(8,128)(2,1)S(1)}, u32[]{:S(2)}, u32[]{:S(2)}) %collective-permute-start.17) | collective-permute-done | bytes 688160 | tf_op jit(solution)/shard_map/ppermute | solution.py:40
  60.4 5.7 %collective-permute-done.12 = bf16[192,896]{1,0:T(8,128)(2,1)S(1)} collective-permute-done((bf16[192,896]{1,0:T(8,128)(2,1)S(1)}, bf16[192,896]{1,0:T(8,128)(2,1)S(1)}, u32[]{:S(2)}, u32[]{:S(2)}) %collective-permute-start.12) | collective-permute-done | bytes 344096 | tf_op jit(solution)/shard_map/ppermute | solution.py:40
  66.7 2.2 %collective-permute-done.18 = bf16[192,896]{1,0:T(8,128)(2,1)S(1)} collective-permute-done((bf16[192,896]{1,0:T(8,128)(2,1)S(1)}, bf16[192,896]{1,0:T(8,128)(2,1)S(1)}, u32[]{:S(2)}, u32[]{:S(2)}) %collective-permute-start.18) | collective-permute-done | bytes 344096 | tf_op jit(solution)/shard_map/ppermute | solution.py:40
  69.6 3.2 %collective-permute-done.13 = bf16[96,896]{1,0:T(8,128)(2,1)S(1)} collective-permute-done((bf16[96,896]{1,0:T(8,128)(2,1)S(1)}, bf16[96,896]{1,0:T(8,128)(2,1)S(1)}, u32[]{:S(2)}, u32[]{:S(2)}) %collective-permute-start.13) | collective-permute-done | bytes 172064 | tf_op jit(solution)/shard_map/ppermute | solution.py:40
  72.9 1.6 %collective-permute-done.19 = bf16[96,896]{1,0:T(8,128)(2,1)S(1)} collective-permute-done((bf16[96,896]{1,0:T(8,128)(2,1)S(1)}, bf16[96,896]{1,0:T(8,128)(2,1)S(1)}, u32[]{:S(2)}, u32[]{:S(2)}) %collective-permute-start.19) | collective-permute-done | bytes 172064 | tf_op jit(solution)/shard_map/ppermute | solution.py:40
  75.7 2.7 %collective-permute-start.24 = (bf16[96,896]{1,0:T(8,128)(2,1)S(1)}, bf16[96,896]{1,0:T(8,128)(2,1)S(1)}, u32[]{:S(2)}, u32[]{:S(2)}) collective-permute-start(bf16[96,896]{1,0:T(8,128)(2,1)S(1)} %get-tuple-element.89), channel_id=1, source_target_pairs={{0,12},{1,13},{2,14},{3,15},{4,8},{5,9},{6,10},{7,11},{8,4},{9,5},... | collective-permute-start | bytes 516104 | tf_op jit(solution)/shard_map/ppermute | solution.py:40
  78.3 2.1 %collective-permute-done.22 = bf16[96,896]{1,0:T(8,128)(2,1)S(1)} collective-permute-done((bf16[96,896]{1,0:T(8,128)(2,1)S(1)}, bf16[96,896]{1,0:T(8,128)(2,1)S(1)}, u32[]{:S(2)}, u32[]{:S(2)}) %collective-permute-start.22) | collective-permute-done | bytes 172064 | tf_op jit(solution)/shard_map/ppermute | solution.py:40
  82.4 2.8 %collective-permute-start.21 = (bf16[192,896]{1,0:T(8,128)(2,1)S(1)}, bf16[192,896]{1,0:T(8,128)(2,1)S(1)}, u32[]{:S(2)}, u32[]{:S(2)}) collective-permute-start(bf16[192,896]{1,0:T(8,128)(2,1)S(1)} %pad_maximum_fusion.4), channel_id=1, source_target_pairs={{0,12},{1,13},{2,14},{3,15},{4,8},{5,9},{6,10},{7,11},{8,4},{9,5},... | collective-permute-start | bytes 1032200 | tf_op jit(solution)/shard_map/ppermute | solution.py:40
  85.3 2.5 %collective-permute-done.23 = bf16[192,896]{1,0:T(8,128)(2,1)S(1)} collective-permute-done((bf16[192,896]{1,0:T(8,128)(2,1)S(1)}, bf16[192,896]{1,0:T(8,128)(2,1)S(1)}, u32[]{:S(2)}, u32[]{:S(2)}) %collective-permute-start.23) | collective-permute-done | bytes 344096 | tf_op jit(solution)/shard_map/ppermute | solution.py:40
  87.9 1.8 %collective-permute-start.27 = (bf16[384,896]{1,0:T(8,128)(2,1)S(1)}, bf16[384,896]{1,0:T(8,128)(2,1)S(1)}, u32[]{:S(2)}, u32[]{:S(2)}) collective-permute-start(bf16[384,896]{1,0:T(8,128)(2,1)S(1)} %pad_maximum_fusion.2.refs_1_), channel_id=1, source_target_pairs={{0,12},{1,13},{2,14},{3,15},{4,8},{5,9},{6,10},{7,11},{8,4},{9,5},... | collective-permute-start | bytes 2064392 | tf_op jit(solution)/shard_map/ppermute | solution.py:40
  89.7 4.6 %collective-permute-done.21 = bf16[192,896]{1,0:T(8,128)(2,1)S(1)} collective-permute-done((bf16[192,896]{1,0:T(8,128)(2,1)S(1)}, bf16[192,896]{1,0:T(8,128)(2,1)S(1)}, u32[]{:S(2)}, u32[]{:S(2)}) %collective-permute-start.21) | collective-permute-done | bytes 344096 | tf_op jit(solution)/shard_map/ppermute | solution.py:40
  96.8 8.9 %collective-permute-done.27.refs_4_ = bf16[384,896]{1,0:T(8,128)(2,1)S(1)} collective-permute-done((bf16[384,896]{1,0:T(8,128)(2,1)S(1)}, bf16[384,896]{1,0:T(8,128)(2,1)S(1)}, u32[]{:S(2)}, u32[]{:S(2)}) %collective-permute-start.27) | collective-permute-done | bytes 688160 | tf_op jit(solution)/shard_map/ppermute | solution.py:40
  108.1 3.3 %shard_map.135 = f32[2,768,512]{2,1,0:T(8,128)S(1)} custom-call(bf16[768,2688]{1,0:T(8,128)(2,1)S(1)} %shard_map.133.acts.gg.ug.hid, bf16[2,512,896]{2,1,0:T(8,128)(2,1)S(1)} %collective-permute-done.9.refs_1_.refs_3_.gu, bf16[896,512]{1,0:T(8,128)(2,1)S(1)} %collective-permute-done.10.refs_5_.refs_1_.d), custom_call_target="tpu_custom_call" | custom-call | flops 2113929216 | bytes 6881280 | tf_op jit(solution)/shard_map/pallas_call | solution.py:254
  111.5 3.3 %shard_map.134 = f32[2,768,512]{2,1,0:T(8,128)S(1)} custom-call(bf16[768,2688]{1,0:T(8,128)(2,1)S(1)} %shard_map.133.acts.gg.ug.hid, bf16[2,512,896]{2,1,0:T(8,128)(2,1)S(1)} %copy-done, bf16[896,512]{1,0:T(8,128)(2,1)S(1)} %get-tuple-element.53.refs_4_.refs_0_.d), custom_call_target="tpu_custom_call" | custom-call | flops 2113929216 | bytes 6881280 | tf_op jit(solution)/shard_map/pallas_call | solution.py:254
  114.8 2.4 %collective-permute-done.29 = f32[2,768,512]{2,1,0:T(8,128)S(1)} collective-permute-done((f32[2,768,512]{2,1,0:T(8,128)S(1)}, f32[2,768,512]{2,1,0:T(8,128)S(1)}, u32[]{:S(2)}, u32[]{:S(2)}) %collective-permute-start.29) | collective-permute-done | bytes 3145760 | tf_op jit(solution)/shard_map/ppermute | solution.py:35
  120.9 2.7 %collective-permute-start.33 = (bf16[2,96,512]{2,1,0:T(8,128)(2,1)S(1)}, bf16[2,96,512]{2,1,0:T(8,128)(2,1)S(1)}, u32[]{:S(2)}, u32[]{:S(2)}) collective-permute-start(bf16[2,96,512]{2,1,0:T(8,128)(2,1)S(1)} %get-tuple-element.61), channel_id=1, source_target_pairs={{0,64},{16,80},{32,96},{48,112},{64,0},{80,16},{96,32},{112,48},{1... | collective-permute-start | bytes 589832 | tf_op jit(solution)/shard_map/ppermute | solution.py:46
  123.6 6.5 %shard_map.136 = (bf16[512,1792]{1,0:T(8,128)(2,1)}, bf16[512,1792]{1,0:T(8,128)(2,1)}, bf16[1792,512]{1,0:T(8,128)(2,1)}) custom-call(s32[25]{0:T(128)S(1)} %dynamic-slice_bitcast_fusion.info, s32[4,14]{1,0:T(4,128)S(1)} %copy-done.1, s32[4,14]{1,0:T(4,128)S(1)} %copy-done.2, s32[14,4]{1,0:T(8,128)S(1)} %copy.17.dm, ...), custom_call_target="tpu_custom_call" | custom-call | flops 2113929216 | bytes 6881280 | tf_op jit(solution)/shard_map/pallas_call | solution.py:304
  130.2 1.7 %collective-permute-start.35 = (f32[2,96,512]{2,1,0:T(8,128)S(1)}, f32[2,96,512]{2,1,0:T(8,128)S(1)}, u32[]{:S(2)}, u32[]{:S(2)}) collective-permute-start(f32[2,96,512]{2,1,0:T(8,128)S(1)} %get-tuple-element.75), channel_id=1, source_target_pairs={{0,64},{16,80},{32,96},{48,112},{64,0},{80,16},{96,32},{112,48},{1... | collective-permute-start | bytes 1179656 | tf_op jit(solution)/shard_map/ppermute | solution.py:46
  131.9 1.7 %collective-permute-start.34 = (bf16[2,96,512]{2,1,0:T(8,128)(2,1)S(1)}, bf16[2,96,512]{2,1,0:T(8,128)(2,1)S(1)}, u32[]{:S(2)}, u32[]{:S(2)}) collective-permute-start(bf16[2,96,512]{2,1,0:T(8,128)(2,1)S(1)} %get-tuple-element.74), channel_id=1, source_target_pairs={{0,32},{16,48},{32,0},{48,16},{64,96},{80,112},{96,64},{112,80},{1... | collective-permute-start | bytes 589832 | tf_op jit(solution)/shard_map/ppermute | solution.py:46
  136.0 6.5 %shard_map.137 = (bf16[512,1792]{1,0:T(8,128)(2,1)}, bf16[512,1792]{1,0:T(8,128)(2,1)}, bf16[1792,512]{1,0:T(8,128)(2,1)}) custom-call(s32[25]{0:T(128)S(1)} %dynamic-slice_bitcast_fusion.info, s32[4,14]{1,0:T(4,128)S(1)} %copy-done.1, s32[4,14]{1,0:T(4,128)S(1)} %copy-done.2, ...), custom_call_target="tpu_custom_call", output_to_operand_aliasing={{0}: (9, {}), {1}: (10, {}), {2}: (11, {})} | custom-call | flops 2113929216 | bytes 6881280 | tf_op jit(solution)/shard_map/pallas_call | solution.py:304
  (93 shorter events, 33.7 us)
Async XLA Ops:
  2.4 16.4 %collective-permute-start.3 = (bf16[96,1024]{1,0:T(8,128)(2,1)S(1)}, bf16[96,1024]{1,0:T(8,128)(2,1)S(1)}, u32[]{:S(2)}, u32[]{:S(2)}) collective-permute-start(bf16[96,1024]{1,0:T(8,128)(2,1)S(1)} %constant_dynamic-update-slice_fusion), channel_id=1, source_target_pairs={{0,32},{16,48},{32,0},{48,16},{64,96},{80,112},{96,64},{112,80},{1... | collective-permute-start | bytes 589832 | tf_op jit(solution)/shard_map/ppermute | solution.py:46
  5.7 13.1 %collective-permute-start.2 = (bf16[96,1024]{1,0:T(8,128)(2,1)S(1)}, bf16[96,1024]{1,0:T(8,128)(2,1)S(1)}, u32[]{:S(2)}, u32[]{:S(2)}) collective-permute-start(bf16[96,1024]{1,0:T(8,128)(2,1)S(1)} %constant_dynamic-update-slice_fusion), channel_id=1, source_target_pairs={{0,48},{16,32},{32,16},{48,0},{64,112},{80,96},{96,80},{112,64},{1... | collective-permute-start | bytes 589832 | tf_op jit(solution)/shard_map/ppermute | solution.py:46
  6.8 12.0 %collective-permute-start.1 = (bf16[96,1024]{1,0:T(8,128)(2,1)S(1)}, bf16[96,1024]{1,0:T(8,128)(2,1)S(1)}, u32[]{:S(2)}, u32[]{:S(2)}) collective-permute-start(bf16[96,1024]{1,0:T(8,128)(2,1)S(1)} %constant_dynamic-update-slice_fusion), channel_id=1, source_target_pairs={{0,16},{16,0},{32,48},{48,32},{64,80},{80,64},{96,112},{112,96},{1... | collective-permute-start | bytes 589832 | tf_op jit(solution)/shard_map/ppermute | solution.py:46
  6.8 12.1 %collective-permute-start = (bf16[96,1024]{1,0:T(8,128)(2,1)S(1)}, bf16[96,1024]{1,0:T(8,128)(2,1)S(1)}, u32[]{:S(2)}, u32[]{:S(2)}) collective-permute-start(bf16[96,1024]{1,0:T(8,128)(2,1)S(1)} %constant_dynamic-update-slice_fusion), channel_id=1, source_target_pairs={{0,64},{16,80},{32,96},{48,112},{64,0},{80,16},{96,32},{112,48},{1... | collective-permute-start | bytes 589832 | tf_op jit(solution)/shard_map/ppermute | solution.py:46
  18.8 7.4 %collective-permute-start.6 = (bf16[96,1024]{1,0:T(8,128)(2,1)S(1)}, bf16[96,1024]{1,0:T(8,128)(2,1)S(1)}, u32[]{:S(2)}, u32[]{:S(2)}) collective-permute-start(bf16[96,1024]{1,0:T(8,128)(2,1)S(1)} %collective-permute-done.3), channel_id=1, source_target_pairs={{0,64},{16,80},{32,96},{48,112},{64,0},{80,16},{96,32},{112,48},{1... | collective-permute-start | bytes 589832 | tf_op jit(solution)/shard_map/ppermute | solution.py:46
  19.4 14.9 %collective-permute-start.9 = (bf16[2,512,896]{2,1,0:T(8,128)(2,1)}, bf16[2,512,896]{2,1,0:T(8,128)(2,1)S(1)}, u32[]{:S(2)}, u32[]{:S(2)}) collective-permute-start(bf16[2,512,896]{2,1,0:T(8,128)(2,1)} %get-tuple-element.52), channel_id=1, source_target_pairs={{0,1},{1,0},{2,3},{3,2},{4,5},{5,4},{6,7},{7,6},{8,9},{9,8},{10,11... | collective-permute-start | bytes 5505032 | tf_op jit(solution)/shard_map/ppermute | solution.py:35
  19.4 8.5 %collective-permute-start.5 = (bf16[96,1024]{1,0:T(8,128)(2,1)S(1)}, bf16[96,1024]{1,0:T(8,128)(2,1)S(1)}, u32[]{:S(2)}, u32[]{:S(2)}) collective-permute-start(bf16[96,1024]{1,0:T(8,128)(2,1)S(1)} %collective-permute-done), channel_id=1, source_target_pairs={{0,48},{16,32},{32,16},{48,0},{64,112},{80,96},{96,80},{112,64},{1... | collective-permute-start | bytes 589832 | tf_op jit(solution)/shard_map/ppermute | solution.py:46
  21.7 7.0 %collective-permute-start.4 = (bf16[96,1024]{1,0:T(8,128)(2,1)S(1)}, bf16[96,1024]{1,0:T(8,128)(2,1)S(1)}, u32[]{:S(2)}, u32[]{:S(2)}) collective-permute-start(bf16[96,1024]{1,0:T(8,128)(2,1)S(1)} %collective-permute-done), channel_id=1, source_target_pairs={{0,16},{16,0},{32,48},{48,32},{64,80},{80,64},{96,112},{112,96},{1... | collective-permute-start | bytes 589832 | tf_op jit(solution)/shard_map/ppermute | solution.py:46
  32.8 17.6 %collective-permute-start.11 = (bf16[384,896]{1,0:T(8,128)(2,1)S(1)}, bf16[384,896]{1,0:T(8,128)(2,1)S(1)}, u32[]{:S(2)}, u32[]{:S(2)}) collective-permute-start(bf16[384,896]{1,0:T(8,128)(2,1)S(1)} %shard_map.130), channel_id=1, source_target_pairs={{0,2},{1,3},{2,0},{3,1},{4,6},{5,7},{6,4},{7,5},{8,10},{9,11},{10,... | collective-permute-start | bytes 2064392 | tf_op jit(solution)/shard_map/ppermute | solution.py:40
  36.0 19.6 %collective-permute-start.14 = (bf16[384,896]{1,0:T(8,128)(2,1)S(1)}, bf16[384,896]{1,0:T(8,128)(2,1)S(1)}, u32[]{:S(2)}, u32[]{:S(2)}) collective-permute-start(bf16[384,896]{1,0:T(8,128)(2,1)S(1)} %shard_map.131), channel_id=1, source_target_pairs={{0,12},{1,13},{2,14},{3,15},{4,8},{5,9},{6,10},{7,11},{8,4},{9,5},... | collective-permute-start | bytes 2064392 | tf_op jit(solution)/shard_map/ppermute | solution.py:40
  41.7 18.4 %collective-permute-start.17 = (bf16[384,896]{1,0:T(8,128)(2,1)S(1)}, bf16[384,896]{1,0:T(8,128)(2,1)S(1)}, u32[]{:S(2)}, u32[]{:S(2)}) collective-permute-start(bf16[384,896]{1,0:T(8,128)(2,1)S(1)} %shard_map.132), channel_id=1, source_target_pairs={{0,4},{1,5},{2,6},{3,7},{4,0},{5,1},{6,2},{7,3},{8,12},{9,13},{10,... | collective-permute-start | bytes 2064392 | tf_op jit(solution)/shard_map/ppermute | solution.py:40
  50.5 15.6 %collective-permute-start.12 = (bf16[192,896]{1,0:T(8,128)(2,1)S(1)}, bf16[192,896]{1,0:T(8,128)(2,1)S(1)}, u32[]{:S(2)}, u32[]{:S(2)}) collective-permute-start(bf16[192,896]{1,0:T(8,128)(2,1)S(1)} %slice.108), channel_id=1, source_target_pairs={{0,4},{1,5},{2,6},{3,7},{4,0},{5,1},{6,2},{7,3},{8,12},{9,13},{10,... | collective-permute-start | bytes 1032200 | tf_op jit(solution)/shard_map/ppermute | solution.py:40
  55.7 10.8 %collective-permute-start.15 = (bf16[192,896]{1,0:T(8,128)(2,1)S(1)}, bf16[192,896]{1,0:T(8,128)(2,1)S(1)}, u32[]{:S(2)}, u32[]{:S(2)}) collective-permute-start(bf16[192,896]{1,0:T(8,128)(2,1)S(1)} %slice.107), channel_id=1, source_target_pairs={{0,2},{1,3},{2,0},{3,1},{4,6},{5,7},{6,4},{7,5},{8,10},{9,11},{10,... | collective-permute-start | bytes 1032200 | tf_op jit(solution)/shard_map/ppermute | solution.py:40
  60.3 8.6 %collective-permute-start.18 = (bf16[192,896]{1,0:T(8,128)(2,1)S(1)}, bf16[192,896]{1,0:T(8,128)(2,1)S(1)}, u32[]{:S(2)}, u32[]{:S(2)}) collective-permute-start(bf16[192,896]{1,0:T(8,128)(2,1)S(1)} %slice.106), channel_id=1, source_target_pairs={{0,12},{1,13},{2,14},{3,15},{4,8},{5,9},{6,10},{7,11},{8,4},{9,5},... | collective-permute-start | bytes 1032200 | tf_op jit(solution)/shard_map/ppermute | solution.py:40
  66.2 6.7 %collective-permute-start.13 = (bf16[96,896]{1,0:T(8,128)(2,1)S(1)}, bf16[96,896]{1,0:T(8,128)(2,1)S(1)}, u32[]{:S(2)}, u32[]{:S(2)}) collective-permute-start(bf16[96,896]{1,0:T(8,128)(2,1)S(1)} %slice.111), channel_id=1, source_target_pairs={{0,12},{1,13},{2,14},{3,15},{4,8},{5,9},{6,10},{7,11},{8,4},{9,5},... | collective-permute-start | bytes 516104 | tf_op jit(solution)/shard_map/ppermute | solution.py:40
  66.7 6.2 %collective-permute-start.16 = (bf16[96,896]{1,0:T(8,128)(2,1)S(1)}, bf16[96,896]{1,0:T(8,128)(2,1)S(1)}, u32[]{:S(2)}, u32[]{:S(2)}) collective-permute-start(bf16[96,896]{1,0:T(8,128)(2,1)S(1)} %slice.110), channel_id=1, source_target_pairs={{0,4},{1,5},{2,6},{3,7},{4,0},{5,1},{6,2},{7,3},{8,12},{9,13},{10,... | collective-permute-start | bytes 516104 | tf_op jit(solution)/shard_map/ppermute | solution.py:40
  75.1 7.3 %collective-permute-start.20 = (bf16[96,896]{1,0:T(8,128)(2,1)S(1)}, bf16[96,896]{1,0:T(8,128)(2,1)S(1)}, u32[]{:S(2)}, u32[]{:S(2)}) collective-permute-start(bf16[96,896]{1,0:T(8,128)(2,1)S(1)} %get-tuple-element.90), channel_id=1, source_target_pairs={{0,2},{1,3},{2,0},{3,1},{4,6},{5,7},{6,4},{7,5},{8,10},{9,11},{10,... | collective-permute-start | bytes 516104 | tf_op jit(solution)/shard_map/ppermute | solution.py:40
  75.7 9.5 %collective-permute-start.24 = (bf16[96,896]{1,0:T(8,128)(2,1)S(1)}, bf16[96,896]{1,0:T(8,128)(2,1)S(1)}, u32[]{:S(2)}, u32[]{:S(2)}) collective-permute-start(bf16[96,896]{1,0:T(8,128)(2,1)S(1)} %get-tuple-element.89), channel_id=1, source_target_pairs={{0,12},{1,13},{2,14},{3,15},{4,8},{5,9},{6,10},{7,11},{8,4},{9,5},... | collective-permute-start | bytes 516104 | tf_op jit(solution)/shard_map/ppermute | solution.py:40
  80.5 7.3 %collective-permute-start.23 = (bf16[192,896]{1,0:T(8,128)(2,1)S(1)}, bf16[192,896]{1,0:T(8,128)(2,1)S(1)}, u32[]{:S(2)}, u32[]{:S(2)}) collective-permute-start(bf16[192,896]{1,0:T(8,128)(2,1)S(1)} %pad_maximum_fusion.5), channel_id=1, source_target_pairs={{0,2},{1,3},{2,0},{3,1},{4,6},{5,7},{6,4},{7,5},{8,10},{9,11},{10,... | collective-permute-start | bytes 1032200 | tf_op jit(solution)/shard_map/ppermute | solution.py:40
  82.4 11.8 %collective-permute-start.21 = (bf16[192,896]{1,0:T(8,128)(2,1)S(1)}, bf16[192,896]{1,0:T(8,128)(2,1)S(1)}, u32[]{:S(2)}, u32[]{:S(2)}) collective-permute-start(bf16[192,896]{1,0:T(8,128)(2,1)S(1)} %pad_maximum_fusion.4), channel_id=1, source_target_pairs={{0,12},{1,13},{2,14},{3,15},{4,8},{5,9},{6,10},{7,11},{8,4},{9,5},... | collective-permute-start | bytes 1032200 | tf_op jit(solution)/shard_map/ppermute | solution.py:40
  85.2 10.6 %collective-permute-start.25 = (bf16[192,896]{1,0:T(8,128)(2,1)S(1)}, bf16[192,896]{1,0:T(8,128)(2,1)S(1)}, u32[]{:S(2)}, u32[]{:S(2)}) collective-permute-start(bf16[192,896]{1,0:T(8,128)(2,1)S(1)} %pad_maximum_fusion.6), channel_id=1, source_target_pairs={{0,4},{1,5},{2,6},{3,7},{4,0},{5,1},{6,2},{7,3},{8,12},{9,13},{10,... | collective-permute-start | bytes 1032200 | tf_op jit(solution)/shard_map/ppermute | solution.py:40
  87.9 17.8 %collective-permute-start.27 = (bf16[384,896]{1,0:T(8,128)(2,1)S(1)}, bf16[384,896]{1,0:T(8,128)(2,1)S(1)}, u32[]{:S(2)}, u32[]{:S(2)}) collective-permute-start(bf16[384,896]{1,0:T(8,128)(2,1)S(1)} %pad_maximum_fusion.2.refs_1_), channel_id=1, source_target_pairs={{0,12},{1,13},{2,14},{3,15},{4,8},{5,9},{6,10},{7,11},{8,4},{9,5},... | collective-permute-start | bytes 2064392 | tf_op jit(solution)/shard_map/ppermute | solution.py:40
  94.3 13.0 %collective-permute-start.26 = (bf16[384,896]{1,0:T(8,128)(2,1)S(1)}, bf16[384,896]{1,0:T(8,128)(2,1)S(1)}, u32[]{:S(2)}, u32[]{:S(2)}) collective-permute-start(bf16[384,896]{1,0:T(8,128)(2,1)S(1)} %pad_maximum_fusion.1.refs_0_), channel_id=1, source_target_pairs={{0,4},{1,5},{2,6},{3,7},{4,0},{5,1},{6,2},{7,3},{8,12},{9,13},{10,... | collective-permute-start | bytes 2064392 | tf_op jit(solution)/shard_map/ppermute | solution.py:40
  95.9 11.4 %collective-permute-start.28 = (bf16[384,896]{1,0:T(8,128)(2,1)S(1)}, bf16[384,896]{1,0:T(8,128)(2,1)S(1)}, u32[]{:S(2)}, u32[]{:S(2)}) collective-permute-start(bf16[384,896]{1,0:T(8,128)(2,1)S(1)} %pad_maximum_fusion.3.refs_2_), channel_id=1, source_target_pairs={{0,2},{1,3},{2,0},{3,1},{4,6},{5,7},{6,4},{7,5},{8,10},{9,11},{10,... | collective-permute-start | bytes 2064392 | tf_op jit(solution)/shard_map/ppermute | solution.py:40
  118.2 12.0 %collective-permute-start.30 = (bf16[768,2688]{1,0:T(8,128)(2,1)S(1)}, bf16[768,2688]{1,0:T(8,128)(2,1)S(1)}, u32[]{:S(2)}, u32[]{:S(2)}) collective-permute-start(bf16[768,2688]{1,0:T(8,128)(2,1)S(1)} %shard_map.133.acts.gg.ug.hid), channel_id=1, source_target_pairs={{0,1},{1,0},{2,3},{3,2},{4,5},{5,4},{6,7},{7,6},{8,9},{9,8},{10,11... | collective-permute-start | bytes 12386312 | tf_op jit(solution)/shard_map/ppermute | solution.py:35
  118.4 11.6 %collective-permute-start.31 = (bf16[2,96,512]{2,1,0:T(8,128)(2,1)S(1)}, bf16[2,96,512]{2,1,0:T(8,128)(2,1)S(1)}, u32[]{:S(2)}, u32[]{:S(2)}) collective-permute-start(bf16[2,96,512]{2,1,0:T(8,128)(2,1)S(1)} %get-tuple-element.59), channel_id=1, source_target_pairs={{0,16},{16,0},{32,48},{48,32},{64,80},{80,64},{96,112},{112,96},{1... | collective-permute-start | bytes 589832 | tf_op jit(solution)/shard_map/ppermute | solution.py:46
  119.8 10.2 %collective-permute-start.32 = (bf16[2,96,512]{2,1,0:T(8,128)(2,1)S(1)}, bf16[2,96,512]{2,1,0:T(8,128)(2,1)S(1)}, u32[]{:S(2)}, u32[]{:S(2)}) collective-permute-start(bf16[2,96,512]{2,1,0:T(8,128)(2,1)S(1)} %get-tuple-element.60), channel_id=1, source_target_pairs={{0,48},{16,32},{32,16},{48,0},{64,112},{80,96},{96,80},{112,64},{1... | collective-permute-start | bytes 589832 | tf_op jit(solution)/shard_map/ppermute | solution.py:46
  120.9 9.2 %collective-permute-start.33 = (bf16[2,96,512]{2,1,0:T(8,128)(2,1)S(1)}, bf16[2,96,512]{2,1,0:T(8,128)(2,1)S(1)}, u32[]{:S(2)}, u32[]{:S(2)}) collective-permute-start(bf16[2,96,512]{2,1,0:T(8,128)(2,1)S(1)} %get-tuple-element.61), channel_id=1, source_target_pairs={{0,64},{16,80},{32,96},{48,112},{64,0},{80,16},{96,32},{112,48},{1... | collective-permute-start | bytes 589832 | tf_op jit(solution)/shard_map/ppermute | solution.py:46
  130.2 13.0 %collective-permute-start.35 = (f32[2,96,512]{2,1,0:T(8,128)S(1)}, f32[2,96,512]{2,1,0:T(8,128)S(1)}, u32[]{:S(2)}, u32[]{:S(2)}) collective-permute-start(f32[2,96,512]{2,1,0:T(8,128)S(1)} %get-tuple-element.75), channel_id=1, source_target_pairs={{0,64},{16,80},{32,96},{48,112},{64,0},{80,16},{96,32},{112,48},{1... | collective-permute-start | bytes 1179656 | tf_op jit(solution)/shard_map/ppermute | solution.py:46
  131.9 10.6 %collective-permute-start.34 = (bf16[2,96,512]{2,1,0:T(8,128)(2,1)S(1)}, bf16[2,96,512]{2,1,0:T(8,128)(2,1)S(1)}, u32[]{:S(2)}, u32[]{:S(2)}) collective-permute-start(bf16[2,96,512]{2,1,0:T(8,128)(2,1)S(1)} %get-tuple-element.74), channel_id=1, source_target_pairs={{0,32},{16,48},{32,0},{48,16},{64,96},{80,112},{96,64},{112,80},{1... | collective-permute-start | bytes 589832 | tf_op jit(solution)/shard_map/ppermute | solution.py:46
  133.6 9.0 %collective-permute-start.36 = (bf16[2,96,512]{2,1,0:T(8,128)(2,1)S(1)}, bf16[2,96,512]{2,1,0:T(8,128)(2,1)S(1)}, u32[]{:S(2)}, u32[]{:S(2)}) collective-permute-start(bf16[2,96,512]{2,1,0:T(8,128)(2,1)S(1)} %get-tuple-element.76), channel_id=1, source_target_pairs={{0,16},{16,0},{32,48},{48,32},{64,80},{80,64},{96,112},{112,96},{1... | collective-permute-start | bytes 589832 | tf_op jit(solution)/shard_map/ppermute | solution.py:46
  135.0 8.2 %collective-permute-start.37 = (bf16[2,96,512]{2,1,0:T(8,128)(2,1)S(1)}, bf16[2,96,512]{2,1,0:T(8,128)(2,1)S(1)}, u32[]{:S(2)}, u32[]{:S(2)}) collective-permute-start(bf16[2,96,512]{2,1,0:T(8,128)(2,1)S(1)} %get-tuple-element.77), channel_id=1, source_target_pairs={{0,48},{16,32},{32,16},{48,0},{64,112},{80,96},{96,80},{112,64},{1... | collective-permute-start | bytes 589832 | tf_op jit(solution)/shard_map/ppermute | solution.py:46
  (9 other events, 32.3 us)

commit v4 on v3

--- a/solution.py
+++ b/solution.py
@@ -94,45 +94,42 @@
 
 
 def times(block, keep):
-    return (block.astype(F32) * keep.astype(F32)).astype(BF)
-
-
-def prepare_kernel(info, gm, um, dm, gk, gs, uk, us, dk, ds, gu_keep, gu_send, d_keep, d_send):
+    return jnp.where(keep != 0, block, jnp.zeros_like(block))
+
+
+def prepare_kernel(info, gm, um, dm, g, u, d, gu_out, d_out, *, kept):
     f = pl.program_id(0)
-    n = gk.shape[1] // BLK
-    for side, (g, u, d, gu_out, d_out) in enumerate(
-        ((gk, uk, dk, gu_keep, d_keep), (gs, us, ds, gu_send, d_send))
-    ):
-        first = (info[0] if side == 0 else 1 - info[0]) * n
-        for j in range(n):
-            at = slice(j * BLK, (j + 1) * BLK)
-            gu_out[0, :, at] = times(g[:, at], gm[f, first + j])
-            gu_out[1, :, at] = times(u[:, at], um[f, first + j])
-            d_out[at, :] = times(d[at, :], dm[first + j, f])
-
-
-def prepare(info, gm, um, dm, gate_weight, up_weight, down_weight):
+    n = g.shape[1] // BLK
+    first = (info[0] if kept else 1 - info[0]) * n
+    for j in range(n):
+        at = slice(j * BLK, (j + 1) * BLK)
+        gu_out[0, :, at] = times(g[:, at], gm[f, first + j])
+        gu_out[1, :, at] = times(u[:, at], um[f, first + j])
+        d_out[at, :] = times(d[at, :], dm[first + j, f])
+
+
+def prepare(info, masks, gate_weight, up_weight, down_weight, kept):
     width, hidden = gate_weight.shape
     half = hidden // 2
 
-    def wide(side):
-        return pl.BlockSpec((BLK, half), lambda f, info, *_: (f, info[0] if side == 0 else 1 - info[0]))
-
-    def tall(side):
-        return pl.BlockSpec((half, BLK), lambda f, info, *_: (info[0] if side == 0 else 1 - info[0], f))
-
-    gu_spec = pl.BlockSpec((2, BLK, half), lambda f, *_: (0, f, 0))
-    d_spec = pl.BlockSpec((half, BLK), lambda f, *_: (0, f))
-    return call(
-        prepare_kernel,
+    def side(info):
+        return info[0] if kept else 1 - info[0]
+
+    wide = pl.BlockSpec((BLK, half), lambda f, info, *_: (f, side(info)))
+    tall = pl.BlockSpec((half, BLK), lambda f, info, *_: (side(info), f))
+    return call(
+        functools.partial(prepare_kernel, kept=kept),
         4,
         (width // BLK,),
-        [wide(0), wide(1), wide(0), wide(1), tall(0), tall(1)],
-        [gu_spec, gu_spec, d_spec, d_spec],
-        [shape((2, width, half), BF)] * 2 + [shape((half, width), BF)] * 2,
-        size=12 * width * hidden,
+        [wide, wide, tall],
+        [
+            pl.BlockSpec((2, BLK, half), lambda f, *_: (0, f, 0)),
+            pl.BlockSpec((half, BLK), lambda f, *_: (0, f)),
+        ],
+        [shape((2, width, half), BF), shape((half, width), BF)],
+        size=6 * width * hidden,
         params=pltpu.CompilerParams(vmem_limit_bytes=52 * 1024 * 1024),
-    )(info, gm, um, dm, gate_weight, gate_weight, up_weight, up_weight, down_weight, down_weight)
+    )(info, *masks, gate_weight, up_weight, down_weight)
 
 
 def project_kernel(info, own_a, own_b, oth_a, oth_b, *refs, base, parts):
@@ -267,57 +264,67 @@
     )(acts, gu, d)
 
 
-def grads_kernel(info, gm, um, dm, own_a, own_b, gg, ug, hid, *refs, mine):
-    outs, tok_t, cot = refs[-5:-2], refs[-2], refs[-1]
-    j = pl.program_id(0)
+def turn_kernel(own_a, own_b, tok_t, cot):
     rows, width = own_a.shape[0], own_a.shape[1] // 2
-
-    @pl.when(j == 0)
-    def _():
-        tok_t[:, :rows] = own_a[:, :width].T
-        tok_t[:, rows:] = own_b[:, :width].T
-        cot[:rows, :] = own_a[:, width:]
-        cot[rows:, :] = own_b[:, width:]
-
-    gu = dot(tok_t[...], jnp.concatenate([gg[...], ug[...]], axis=1))
-    d = dot(hid[...].T, cot[...])
-    at = (info[0] if mine else 1 - info[0]) * pl.num_programs(0) + j
-    g_out, u_out, d_out = outs
-    for f in range(width // BLK):
-        block = slice(f * BLK, (f + 1) * BLK)
-        g_out[block, :] = (gu[block, :BLK] * gm[f, at].astype(F32)).astype(BF)
-        u_out[block, :] = (gu[block, BLK:] * um[f, at].astype(F32)).astype(BF)
-        d_out[:, block] = (d[:, block] * dm[at, f].astype(F32)).astype(BF)
-
-
-def grads(info, masks, panels, acts, into=()):
-    rows, width = panels[0].shape[0], panels[0].shape[1] // 2
-    n = acts.shape[1] // 3 // BLK
-    hidden = 2 * n * BLK
+    tok_t[:, :rows] = own_a[:, :width].T
+    tok_t[:, rows:] = own_b[:, :width].T
+    cot[:rows, :] = own_a[:, width:]
+    cot[rows:, :] = own_b[:, width:]
+
+
+def turn(own_a, own_b):
+    rows, width = 2 * own_a.shape[0], own_a.shape[1] // 2
+    return call(
+        turn_kernel,
+        0,
+        (1,),
+        [whole(own_a.shape)] * 2,
+        [whole((width, rows)), whole((rows, width))],
+        [shape((width, rows), BF), shape((rows, width), BF)],
+        size=8 * rows * width,
+    )(own_a, own_b)
+
+
+def grads_kernel(info, gm, um, dm, tok_t, cot, acts, *refs, mine):
+    g_out, u_out, d_out = refs[-3:]
+    width, count = g_out.shape
+    n = count // BLK
+    first = (info[0] if mine else 1 - info[0]) * n
+    for out, mask, start in ((g_out, gm, 0), (u_out, um, count)):
+        grad = dot(tok_t[...], acts[:, start : start + count])
+        for f in range(width // BLK):
+            for j in range(n):
+                at = slice(f * BLK, (f + 1) * BLK), slice(j * BLK, (j + 1) * BLK)
+                out[at] = (grad[at] * mask[f, first + j].astype(F32)).astype(BF)
+    grad = dot(acts[:, 2 * count :], cot[...], ((0,), (0,)))
+    for j in range(n):
+        for f in range(width // BLK):
+            at = slice(j * BLK, (j + 1) * BLK), slice(f * BLK, (f + 1) * BLK)
+            d_out[at] = (grad[at] * dm[first + j, f].astype(F32)).astype(BF)
+
+
+def grads(info, masks, tok_t, cot, acts, into=()):
+    width, rows = tok_t.shape
+    count = acts.shape[1] // 3
+    hidden = 2 * count
 
     def half(info):
-        return (1 - info[0] if into else info[0]) * n
-
-    wide = pl.BlockSpec((width, BLK), lambda j, info, *_: (0, half(info) + j))
-    tall = pl.BlockSpec((BLK, width), lambda j, info, *_: (half(info) + j, 0))
+        return 1 - info[0] if into else info[0]
+
+    wide = pl.BlockSpec((width, count), lambda i, info, *_: (0, half(info)))
+    tall = pl.BlockSpec((count, width), lambda i, info, *_: (half(info), 0))
     wide_shape = shape((width, hidden), BF)
     return call(
         functools.partial(grads_kernel, mine=not into),
         4,
-        (n,),
-        [whole(v.shape) for v in panels]
-        + [
-            pl.BlockSpec((2 * rows, BLK), lambda j, *_, q=q: (0, q * n + j))
-            for q in range(3)
-        ]
-        + [pl.BlockSpec(memory_space=pl.ANY)] * len(into),
+        (1,),
+        [whole(v.shape) for v in (tok_t, cot, acts)] + [pl.BlockSpec(memory_space=pl.ANY)] * len(into),
         [wide, wide, tall],
         [wide_shape, wide_shape, shape((hidden, width), BF)],
-        [pltpu.VMEM((width, 2 * rows), BF), pltpu.VMEM((2 * rows, width), BF)],
-        flops=6 * rows * width * hidden,
-        size=3 * width * hidden + 6 * rows * hidden,
-        **({"input_output_aliases": {9: 0, 10: 1, 11: 2}} if into else {}),
-    )(info, *masks, *panels, acts, acts, acts, *into)
+        flops=3 * rows * width * hidden,
+        size=3 * width * hidden + 3 * rows * hidden,
+        **({"input_output_aliases": {7: 0, 8: 1, 9: 2}} if into else {}),
+    )(info, *masks, tok_t, cot, acts, *into)
 
 
 def per_device(
@@ -327,16 +334,20 @@
     info = lax.dynamic_index_in_dim(jnp.asarray(make_table()), lax.axis_index("col"), 0, keepdims=False)
     both = jnp.concatenate([tokens, cotangent], axis=1)
     x, a, b, ab = (swap_row(both, d) for d in ("X", "A", "B", "AB"))
-    gu_own, gu_send, d_own, d_send = prepare(info, *masks, gate_weight, up_weight, down_weight)
-    gu_send, d_send, x, a, b, ab = lax.optimization_barrier((gu_send, d_send, x, a, b, ab))
+    weights = (gate_weight, up_weight, down_weight)
+    gu_send, d_send = prepare(info, masks, *weights, False)
+    gu_send, d_send, x, a, b, ab, *weights = lax.optimization_barrier((gu_send, d_send, x, a, b, ab, *weights))
     ax, bx, abx = swap_row(x, "A"), swap_row(x, "B"), swap_row(ab, "X")
     gu_oth, d_oth = swap_core(gu_send), swap_core(d_send)
+    gu_own, d_own = prepare(info, masks, *weights, True)
+    gu_own, d_own, ax, bx, abx = lax.optimization_barrier((gu_own, d_own, ax, bx, abx))
     own = [jnp.concatenate(blocks, axis=0) for blocks in ([both, x, ax, bx], [abx, ab, a, b])]
     oth = [swap_core(panel) for panel in own]
 
     panels, weights = (*own, *oth), (gu_own, gu_oth, d_own, d_oth)
     sends = [project(info, panels, weights, 4, (q,), BF)[0] for q in range(3)]
     keeps = project(info, panels, weights, 0, (0, 1, 2), F32)
+    tok_t, cot = turn(*own)
     acts = gather(info, exchange(sends, keeps))
 
     got = swap_core(backward(acts, gu_oth, d_oth, F32))
@@ -346,12 +357,12 @@
     acts, ax, bx, abx, a, b = lax.optimization_barrier([acts] + [v.astype(BF) for v in (ax, bx, abx, a, b)])
     ax, bx, abx = swap_row(ax, "A"), swap_row(bx, "B"), swap_row(abx, "X")
     sib = swap_core(acts)
-    partial = grads(info, masks, own, acts)
+    partial = grads(info, masks, tok_t, cot, acts)
     x = x + ax.astype(F32) + bx.astype(F32)
     ab = (ab + abx.astype(F32)).astype(BF)
     sib, x, ab, a, b, *partial = lax.optimization_barrier((sib, x, ab, a, b, *partial))
     got = [swap_row(v, d) for v, d in ((ab, "AB"), (x, "X"), (a, "A"), (b, "B"))]
-    weight_grads = grads(info, masks, own, sib, partial)
+    weight_grads = grads(info, masks, tok_t, cot, sib, partial)
     *weight_grads, got = lax.optimization_barrier((*weight_grads, got))
     total = own_part
     for block in got:

time: 144 us -> 144 us (level)
  waiting for transfers between devices: 57.1 us -> 54.5 us
  starting transfers between devices: 43.2 us -> 44.7 us
    ppermute x14, waiting for transfers between devices: 6.22 us -> 3.26 us  [swap_row(): lax.ppermute(value, 'row', [(i, flip_row(i, dims)) for i in range(8)])]
    pallas_call x3 -> x5, Pallas kernels: 19.1 us -> 19.5 us  [the longest x2 9.83 us: prepare(): call(functools.partial(prepare_kernel, kept=kept), 4, (width // BLK,), [w...]
  transfers between devices with their start and end apart: 38 -> 38, of which waited for: 21 -> 21; matrix products, arithmetic and copies ran while one was open for 2% -> 2% of each run, Pallas kernels for 21% -> 22%
where the time goes in v4:
time: 144 us; the launch traced here: 143 us
  waiting for transfers between devices  54.5 us (38%)
  starting transfers between devices  44.7 us (31%)
  Pallas kernels  35.3 us (25%)
  local copies, waits for them, and re-layouts  5.63 us (4%)
  other arithmetic  2.18 us (2%)
    ppermute x18, waiting for transfers between devices, swap_cube(): lax.ppermute(part, 'col', [(i, flip_col(i, order[step])) for i in range(1...  46.1 us
    ppermute x14, starting transfers between devices, swap_row(): lax.ppermute(value, 'row', [(i, flip_row(i, dims)) for i in range(8)])  22.9 us
    ppermute x18, starting transfers between devices, swap_cube(): lax.ppermute(part, 'col', [(i, flip_col(i, order[step])) for i in range(1...  20.3 us
    pallas_call x2, Pallas kernels, prepare(): call(functools.partial(prepare_kernel, kept=kept), 4, (width // BLK,), [w...  9.83 us
    pallas_call x2, Pallas kernels, grads(): call(functools.partial(grads_kernel, mine=not into), 4, (1,), [whole(v.sh...  9.36 us
    pallas_call x4, Pallas kernels, project(): call(functools.partial(project_kernel, base=base, parts=parts), 1, (1,),...  8.4 us
    pallas_call x2, Pallas kernels, backward(): call(backward_kernel, 0, (width // step,), [whole(acts.shape), pl.BlockSp...  6.59 us
    ppermute x6, waiting for transfers between devices, swap_core(): return lax.ppermute(value, 'col', [(i, i ^ 1) for i in range(16)])  5.1 us
  transfers between devices with their start and end apart: 38, of which 21 were waited for; matrix products, arithmetic and copies ran while one was open for 2% of the time, Pallas kernels for 22%

profile of v4, /device:TPU:0, one launch (start us, length us, event | category | flops | bytes accessed | tf_op | source)
XLA Modules:
  0.0 143.2 jit_solution(9759369361643757082)
XLA Ops:
  2.4 3.3 %collective-permute-start.3 = (bf16[96,1024]{1,0:T(8,128)(2,1)S(1)}, bf16[96,1024]{1,0:T(8,128)(2,1)S(1)}, u32[]{:S(2)}, u32[]{:S(2)}) collective-permute-start(bf16[96,1024]{1,0:T(8,128)(2,1)S(1)} %constant_dynamic-update-slice_fusion), channel_id=1, source_target_pairs={{0,32},{16,48},{32,0},{48,16},{64,96},{80,112},{96,64},{112,80},{1... | collective-permute-start | bytes 589832 | tf_op jit(solution)/shard_map/ppermute | solution.py:46
  6.8 3.0 %collective-permute-start = (bf16[96,1024]{1,0:T(8,128)(2,1)S(1)}, bf16[96,1024]{1,0:T(8,128)(2,1)S(1)}, u32[]{:S(2)}, u32[]{:S(2)}) collective-permute-start(bf16[96,1024]{1,0:T(8,128)(2,1)S(1)} %constant_dynamic-update-slice_fusion), channel_id=1, source_target_pairs={{0,64},{16,80},{32,96},{48,112},{64,0},{80,16},{96,32},{112,48},{1... | collective-permute-start | bytes 589832 | tf_op jit(solution)/shard_map/ppermute | solution.py:46
  12.6 4.9 %shard_map.128 = (bf16[2,512,896]{2,1,0:T(8,128)(2,1)}, bf16[896,512]{1,0:T(8,128)(2,1)S(1)}) custom-call(s32[25]{0:T(128)S(1)} %dynamic-slice_bitcast_fusion.info, s32[4,14]{1,0:T(4,128)S(1)} %copy-done.1, s32[4,14]{1,0:T(4,128)S(1)} %copy-done.2, s32[14,4]{1,0:T(8,128)S(1)} %copy.17.dm, bf16[512,1792]{1,0:T(8,128)(2,1)} %g.2, bf16[512,1792]{1,0:T(8,128)(2,1)} %u.2, ...), custom_call_target="tpu_custom_call" | custom-call | bytes 5505024 | tf_op jit(solution)/shard_map/pallas_call | solution.py:120
  18.3 2.6 %collective-permute-start.5 = (bf16[96,1024]{1,0:T(8,128)(2,1)S(1)}, bf16[96,1024]{1,0:T(8,128)(2,1)S(1)}, u32[]{:S(2)}, u32[]{:S(2)}) collective-permute-start(bf16[96,1024]{1,0:T(8,128)(2,1)S(1)} %collective-permute-done), channel_id=1, source_target_pairs={{0,48},{16,32},{32,16},{48,0},{64,112},{80,96},{96,80},{112,64},{1... | collective-permute-start | bytes 589832 | tf_op jit(solution)/shard_map/ppermute | solution.py:46
  22.3 4.9 %shard_map.129 = (bf16[2,512,896]{2,1,0:T(8,128)(2,1)}, bf16[896,512]{1,0:T(8,128)(2,1)S(1)}) custom-call(s32[25]{0:T(128)S(1)} %dynamic-slice_bitcast_fusion.info, s32[4,14]{1,0:T(4,128)S(1)} %copy-done.1, s32[4,14]{1,0:T(4,128)S(1)} %copy-done.2, s32[14,4]{1,0:T(8,128)S(1)} %copy.17.dm, bf16[512,1792]{1,0:T(8,128)(2,1)} %g.2, bf16[512,1792]{1,0:T(8,128)(2,1)} %u.2, ...), custom_call_target="tpu_custom_call" | custom-call | bytes 5505024 | tf_op jit(solution)/shard_map/pallas_call | solution.py:120
  30.8 1.7 %shard_map.131 = bf16[384,896]{1,0:T(8,128)(2,1)S(1)} custom-call(s32[25]{0:T(128)S(1)} %dynamic-slice_bitcast_fusion.info, bf16[384,1024]{1,0:T(8,128)(2,1)S(1)} %pad_maximum_fusion.own_a, bf16[384,1024]{1,0:T(8,128)(2,1)S(1)} %constant_dynamic-update-slice_fusion.2.own_b, bf16[384,1024]{1,0:T(8,128)(2,1)S(1)} %collective-permute-done.7.oth_a, ...), custom_call_target="tpu_custom_call" | custom-call | flops 704643072 | bytes 4784128 | tf_op jit(solution)/shard_map/pallas_call | solution.py:177
  34.0 1.6 %shard_map.132 = bf16[384,896]{1,0:T(8,128)(2,1)S(1)} custom-call(s32[25]{0:T(128)S(1)} %dynamic-slice_bitcast_fusion.info, bf16[384,1024]{1,0:T(8,128)(2,1)S(1)} %pad_maximum_fusion.own_a, bf16[384,1024]{1,0:T(8,128)(2,1)S(1)} %constant_dynamic-update-slice_fusion.2.own_b, bf16[384,1024]{1,0:T(8,128)(2,1)S(1)} %collective-permute-done.7.oth_a, ...), custom_call_target="tpu_custom_call" | custom-call | flops 704643072 | bytes 4784128 | tf_op jit(solution)/shard_map/pallas_call | solution.py:177
  35.7 4.1 %collective-permute-start.14 = (bf16[384,896]{1,0:T(8,128)(2,1)S(1)}, bf16[384,896]{1,0:T(8,128)(2,1)S(1)}, u32[]{:S(2)}, u32[]{:S(2)}) collective-permute-start(bf16[384,896]{1,0:T(8,128)(2,1)S(1)} %shard_map.132), channel_id=1, source_target_pairs={{0,12},{1,13},{2,14},{3,15},{4,8},{5,9},{6,10},{7,11},{8,4},{9,5},... | collective-permute-start | bytes 2064392 | tf_op jit(solution)/shard_map/ppermute | solution.py:40
  41.5 3.5 %shard_map.130 = (f32[384,896]{1,0:T(8,128)S(1)}, f32[384,896]{1,0:T(8,128)S(1)}, f32[384,896]{1,0:T(8,128)S(1)}) custom-call(s32[25]{0:T(128)S(1)} %dynamic-slice_bitcast_fusion.info, bf16[384,1024]{1,0:T(8,128)(2,1)S(1)} %pad_maximum_fusion.own_a, bf16[384,1024]{1,0:T(8,128)(2,1)S(1)} %constant_dynamic-update-slice_fusion.2.own_b, ...), custom_call_target="tpu_custom_call" | custom-call | flops 2113929216 | bytes 11206656 | tf_op jit(solution)/shard_map/pallas_call | solution.py:177
  45.0 5.0 %collective-permute-done.11 = bf16[384,896]{1,0:T(8,128)(2,1)S(1)} collective-permute-done((bf16[384,896]{1,0:T(8,128)(2,1)S(1)}, bf16[384,896]{1,0:T(8,128)(2,1)S(1)}, u32[]{:S(2)}, u32[]{:S(2)}) %collective-permute-start.11) | collective-permute-done | bytes 688160 | tf_op jit(solution)/shard_map/ppermute | solution.py:40
  50.2 2.0 %collective-permute-start.12 = (bf16[192,896]{1,0:T(8,128)(2,1)S(1)}, bf16[192,896]{1,0:T(8,128)(2,1)S(1)}, u32[]{:S(2)}, u32[]{:S(2)}) collective-permute-start(bf16[192,896]{1,0:T(8,128)(2,1)S(1)} %slice.108), channel_id=1, source_target_pairs={{0,4},{1,5},{2,6},{3,7},{4,0},{5,1},{6,2},{7,3},{8,12},{9,13},{10,... | collective-permute-start | bytes 1032200 | tf_op jit(solution)/shard_map/ppermute | solution.py:40
  52.2 3.1 %collective-permute-done.14 = bf16[384,896]{1,0:T(8,128)(2,1)S(1)} collective-permute-done((bf16[384,896]{1,0:T(8,128)(2,1)S(1)}, bf16[384,896]{1,0:T(8,128)(2,1)S(1)}, u32[]{:S(2)}, u32[]{:S(2)}) %collective-permute-start.14) | collective-permute-done | bytes 688160 | tf_op jit(solution)/shard_map/ppermute | solution.py:40
  56.0 3.8 %collective-permute-done.17 = bf16[384,896]{1,0:T(8,128)(2,1)S(1)} collective-permute-done((bf16[384,896]{1,0:T(8,128)(2,1)S(1)}, bf16[384,896]{1,0:T(8,128)(2,1)S(1)}, u32[]{:S(2)}, u32[]{:S(2)}) %collective-permute-start.17) | collective-permute-done | bytes 688160 | tf_op jit(solution)/shard_map/ppermute | solution.py:40
  60.1 5.7 %collective-permute-done.12 = bf16[192,896]{1,0:T(8,128)(2,1)S(1)} collective-permute-done((bf16[192,896]{1,0:T(8,128)(2,1)S(1)}, bf16[192,896]{1,0:T(8,128)(2,1)S(1)}, u32[]{:S(2)}, u32[]{:S(2)}) %collective-permute-start.12) | collective-permute-done | bytes 344096 | tf_op jit(solution)/shard_map/ppermute | solution.py:40
  66.4 2.2 %collective-permute-done.18 = bf16[192,896]{1,0:T(8,128)(2,1)S(1)} collective-permute-done((bf16[192,896]{1,0:T(8,128)(2,1)S(1)}, bf16[192,896]{1,0:T(8,128)(2,1)S(1)}, u32[]{:S(2)}, u32[]{:S(2)}) %collective-permute-start.18) | collective-permute-done | bytes 344096 | tf_op jit(solution)/shard_map/ppermute | solution.py:40
  69.3 3.2 %collective-permute-done.13 = bf16[96,896]{1,0:T(8,128)(2,1)S(1)} collective-permute-done((bf16[96,896]{1,0:T(8,128)(2,1)S(1)}, bf16[96,896]{1,0:T(8,128)(2,1)S(1)}, u32[]{:S(2)}, u32[]{:S(2)}) %collective-permute-start.13) | collective-permute-done | bytes 172064 | tf_op jit(solution)/shard_map/ppermute | solution.py:40
  72.6 1.6 %collective-permute-done.19 = bf16[96,896]{1,0:T(8,128)(2,1)S(1)} collective-permute-done((bf16[96,896]{1,0:T(8,128)(2,1)S(1)}, bf16[96,896]{1,0:T(8,128)(2,1)S(1)}, u32[]{:S(2)}, u32[]{:S(2)}) %collective-permute-start.19) | collective-permute-done | bytes 172064 | tf_op jit(solution)/shard_map/ppermute | solution.py:40
  75.4 2.7 %collective-permute-start.24 = (bf16[96,896]{1,0:T(8,128)(2,1)S(1)}, bf16[96,896]{1,0:T(8,128)(2,1)S(1)}, u32[]{:S(2)}, u32[]{:S(2)}) collective-permute-start(bf16[96,896]{1,0:T(8,128)(2,1)S(1)} %get-tuple-element.109), channel_id=1, source_target_pairs={{0,12},{1,13},{2,14},{3,15},{4,8},{5,9},{6,10},{7,11},{8,4},{9,5},... | collective-permute-start | bytes 516104 | tf_op jit(solution)/shard_map/ppermute | solution.py:40
  78.0 2.1 %collective-permute-done.22 = bf16[96,896]{1,0:T(8,128)(2,1)S(1)} collective-permute-done((bf16[96,896]{1,0:T(8,128)(2,1)S(1)}, bf16[96,896]{1,0:T(8,128)(2,1)S(1)}, u32[]{:S(2)}, u32[]{:S(2)}) %collective-permute-start.22) | collective-permute-done | bytes 172064 | tf_op jit(solution)/shard_map/ppermute | solution.py:40
  82.1 2.8 %collective-permute-start.21 = (bf16[192,896]{1,0:T(8,128)(2,1)S(1)}, bf16[192,896]{1,0:T(8,128)(2,1)S(1)}, u32[]{:S(2)}, u32[]{:S(2)}) collective-permute-start(bf16[192,896]{1,0:T(8,128)(2,1)S(1)} %pad_maximum_fusion.4), channel_id=1, source_target_pairs={{0,12},{1,13},{2,14},{3,15},{4,8},{5,9},{6,10},{7,11},{8,4},{9,5},... | collective-permute-start | bytes 1032200 | tf_op jit(solution)/shard_map/ppermute | solution.py:40
  85.0 2.5 %collective-permute-done.23 = bf16[192,896]{1,0:T(8,128)(2,1)S(1)} collective-permute-done((bf16[192,896]{1,0:T(8,128)(2,1)S(1)}, bf16[192,896]{1,0:T(8,128)(2,1)S(1)}, u32[]{:S(2)}, u32[]{:S(2)}) %collective-permute-start.23) | collective-permute-done | bytes 344096 | tf_op jit(solution)/shard_map/ppermute | solution.py:40
  87.6 1.8 %collective-permute-start.27 = (bf16[384,896]{1,0:T(8,128)(2,1)S(1)}, bf16[384,896]{1,0:T(8,128)(2,1)S(1)}, u32[]{:S(2)}, u32[]{:S(2)}) collective-permute-start(bf16[384,896]{1,0:T(8,128)(2,1)S(1)} %pad_maximum_fusion.2.refs_1_), channel_id=1, source_target_pairs={{0,12},{1,13},{2,14},{3,15},{4,8},{5,9},{6,10},{7,11},{8,4},{9,5},... | collective-permute-start | bytes 2064392 | tf_op jit(solution)/shard_map/ppermute | solution.py:40
  89.3 4.6 %collective-permute-done.21 = bf16[192,896]{1,0:T(8,128)(2,1)S(1)} collective-permute-done((bf16[192,896]{1,0:T(8,128)(2,1)S(1)}, bf16[192,896]{1,0:T(8,128)(2,1)S(1)}, u32[]{:S(2)}, u32[]{:S(2)}) %collective-permute-start.21) | collective-permute-done | bytes 344096 | tf_op jit(solution)/shard_map/ppermute | solution.py:40
  96.5 8.8 %collective-permute-done.27.refs_4_ = bf16[384,896]{1,0:T(8,128)(2,1)S(1)} collective-permute-done((bf16[384,896]{1,0:T(8,128)(2,1)S(1)}, bf16[384,896]{1,0:T(8,128)(2,1)S(1)}, u32[]{:S(2)}, u32[]{:S(2)}) %collective-permute-start.27) | collective-permute-done | bytes 688160 | tf_op jit(solution)/shard_map/ppermute | solution.py:40
  107.8 3.3 %shard_map.136 = f32[2,768,512]{2,1,0:T(8,128)S(1)} custom-call(bf16[768,2688]{1,0:T(8,128)(2,1)S(1)} %shard_map.134.acts, bf16[2,512,896]{2,1,0:T(8,128)(2,1)S(1)} %collective-permute-done.9.refs_1_.refs_3_.gu, bf16[896,512]{1,0:T(8,128)(2,1)S(1)} %collective-permute-done.10.refs_5_.refs_1_.d), custom_call_target="tpu_custom_call" | custom-call | flops 2113929216 | bytes 6881280 | tf_op jit(solution)/shard_map/pallas_call | solution.py:251
  111.2 3.3 %shard_map.135 = f32[2,768,512]{2,1,0:T(8,128)S(1)} custom-call(bf16[768,2688]{1,0:T(8,128)(2,1)S(1)} %shard_map.134.acts, bf16[2,512,896]{2,1,0:T(8,128)(2,1)S(1)} %copy-done, bf16[896,512]{1,0:T(8,128)(2,1)S(1)} %get-tuple-element.71.refs_4_.refs_0_.d), custom_call_target="tpu_custom_call" | custom-call | flops 2113929216 | bytes 6881280 | tf_op jit(solution)/shard_map/pallas_call | solution.py:251
  114.5 2.3 %collective-permute-done.29 = f32[2,768,512]{2,1,0:T(8,128)S(1)} collective-permute-done((f32[2,768,512]{2,1,0:T(8,128)S(1)}, f32[2,768,512]{2,1,0:T(8,128)S(1)}, u32[]{:S(2)}, u32[]{:S(2)}) %collective-permute-start.29) | collective-permute-done | bytes 3145760 | tf_op jit(solution)/shard_map/ppermute | solution.py:35
  120.0 2.7 %collective-permute-start.33 = (bf16[2,96,512]{2,1,0:T(8,128)(2,1)S(1)}, bf16[2,96,512]{2,1,0:T(8,128)(2,1)S(1)}, u32[]{:S(2)}, u32[]{:S(2)}) collective-permute-start(bf16[2,96,512]{2,1,0:T(8,128)(2,1)S(1)} %get-tuple-element.81), channel_id=1, source_target_pairs={{0,64},{16,80},{32,96},{48,112},{64,0},{80,16},{96,32},{112,48},{1... | collective-permute-start | bytes 589832 | tf_op jit(solution)/shard_map/ppermute | solution.py:46
  122.7 4.7 %shard_map.138 = (bf16[512,1792]{1,0:T(8,128)(2,1)}, bf16[512,1792]{1,0:T(8,128)(2,1)}, bf16[1792,512]{1,0:T(8,128)(2,1)}) custom-call(s32[25]{0:T(128)S(1)} %dynamic-slice_bitcast_fusion.info, s32[4,14]{1,0:T(4,128)S(1)} %copy-done.1, s32[4,14]{1,0:T(4,128)S(1)} %copy-done.2, s32[14,4]{1,0:T(8,128)S(1)} %copy.17.dm, ...), custom_call_target="tpu_custom_call" | custom-call | flops 2113929216 | bytes 6881280 | tf_op jit(solution)/shard_map/pallas_call | solution.py:317
  128.3 2.8 %collective-permute-start.35 = (f32[2,96,512]{2,1,0:T(8,128)S(1)}, f32[2,96,512]{2,1,0:T(8,128)S(1)}, u32[]{:S(2)}, u32[]{:S(2)}) collective-permute-start(f32[2,96,512]{2,1,0:T(8,128)S(1)} %get-tuple-element.95), channel_id=1, source_target_pairs={{0,64},{16,80},{32,96},{48,112},{64,0},{80,16},{96,32},{112,48},{1... | collective-permute-start | bytes 1179656 | tf_op jit(solution)/shard_map/ppermute | solution.py:46
  131.1 2.4 %collective-permute-start.34 = (bf16[2,96,512]{2,1,0:T(8,128)(2,1)S(1)}, bf16[2,96,512]{2,1,0:T(8,128)(2,1)S(1)}, u32[]{:S(2)}, u32[]{:S(2)}) collective-permute-start(bf16[2,96,512]{2,1,0:T(8,128)(2,1)S(1)} %get-tuple-element.94), channel_id=1, source_target_pairs={{0,32},{16,48},{32,0},{48,16},{64,96},{80,112},{96,64},{112,80},{1... | collective-permute-start | bytes 589832 | tf_op jit(solution)/shard_map/ppermute | solution.py:46
  135.2 4.7 %shard_map.139 = (bf16[512,1792]{1,0:T(8,128)(2,1)}, bf16[512,1792]{1,0:T(8,128)(2,1)}, bf16[1792,512]{1,0:T(8,128)(2,1)}) custom-call(s32[25]{0:T(128)S(1)} %dynamic-slice_bitcast_fusion.info, s32[4,14]{1,0:T(4,128)S(1)} %copy-done.1, s32[4,14]{1,0:T(4,128)S(1)} %copy-done.2, ...), custom_call_target="tpu_custom_call", output_to_operand_aliasing={{0}: (7, {}), {1}: (8, {}), {2}: (9, {})} | custom-call | flops 2113929216 | bytes 6881280 | tf_op jit(solution)/shard_map/pallas_call | solution.py:317
  (95 shorter events, 34.5 us)
Async XLA Ops:
  2.4 15.1 %collective-permute-start.3 = (bf16[96,1024]{1,0:T(8,128)(2,1)S(1)}, bf16[96,1024]{1,0:T(8,128)(2,1)S(1)}, u32[]{:S(2)}, u32[]{:S(2)}) collective-permute-start(bf16[96,1024]{1,0:T(8,128)(2,1)S(1)} %constant_dynamic-update-slice_fusion), channel_id=1, source_target_pairs={{0,32},{16,48},{32,0},{48,16},{64,96},{80,112},{96,64},{112,80},{1... | collective-permute-start | bytes 589832 | tf_op jit(solution)/shard_map/ppermute | solution.py:46
  5.7 11.8 %collective-permute-start.2 = (bf16[96,1024]{1,0:T(8,128)(2,1)S(1)}, bf16[96,1024]{1,0:T(8,128)(2,1)S(1)}, u32[]{:S(2)}, u32[]{:S(2)}) collective-permute-start(bf16[96,1024]{1,0:T(8,128)(2,1)S(1)} %constant_dynamic-update-slice_fusion), channel_id=1, source_target_pairs={{0,48},{16,32},{32,16},{48,0},{64,112},{80,96},{96,80},{112,64},{1... | collective-permute-start | bytes 589832 | tf_op jit(solution)/shard_map/ppermute | solution.py:46
  6.8 10.8 %collective-permute-start.1 = (bf16[96,1024]{1,0:T(8,128)(2,1)S(1)}, bf16[96,1024]{1,0:T(8,128)(2,1)S(1)}, u32[]{:S(2)}, u32[]{:S(2)}) collective-permute-start(bf16[96,1024]{1,0:T(8,128)(2,1)S(1)} %constant_dynamic-update-slice_fusion), channel_id=1, source_target_pairs={{0,16},{16,0},{32,48},{48,32},{64,80},{80,64},{96,112},{112,96},{1... | collective-permute-start | bytes 589832 | tf_op jit(solution)/shard_map/ppermute | solution.py:46
  6.8 10.8 %collective-permute-start = (bf16[96,1024]{1,0:T(8,128)(2,1)S(1)}, bf16[96,1024]{1,0:T(8,128)(2,1)S(1)}, u32[]{:S(2)}, u32[]{:S(2)}) collective-permute-start(bf16[96,1024]{1,0:T(8,128)(2,1)S(1)} %constant_dynamic-update-slice_fusion), channel_id=1, source_target_pairs={{0,64},{16,80},{32,96},{48,112},{64,0},{80,16},{96,32},{112,48},{1... | collective-permute-start | bytes 589832 | tf_op jit(solution)/shard_map/ppermute | solution.py:46
  17.6 9.6 %collective-permute-start.6 = (bf16[96,1024]{1,0:T(8,128)(2,1)S(1)}, bf16[96,1024]{1,0:T(8,128)(2,1)S(1)}, u32[]{:S(2)}, u32[]{:S(2)}) collective-permute-start(bf16[96,1024]{1,0:T(8,128)(2,1)S(1)} %collective-permute-done.3), channel_id=1, source_target_pairs={{0,64},{16,80},{32,96},{48,112},{64,0},{80,16},{96,32},{112,48},{1... | collective-permute-start | bytes 589832 | tf_op jit(solution)/shard_map/ppermute | solution.py:46
  18.3 8.9 %collective-permute-start.5 = (bf16[96,1024]{1,0:T(8,128)(2,1)S(1)}, bf16[96,1024]{1,0:T(8,128)(2,1)S(1)}, u32[]{:S(2)}, u32[]{:S(2)}) collective-permute-start(bf16[96,1024]{1,0:T(8,128)(2,1)S(1)} %collective-permute-done), channel_id=1, source_target_pairs={{0,48},{16,32},{32,16},{48,0},{64,112},{80,96},{96,80},{112,64},{1... | collective-permute-start | bytes 589832 | tf_op jit(solution)/shard_map/ppermute | solution.py:46
  20.9 6.3 %collective-permute-start.4 = (bf16[96,1024]{1,0:T(8,128)(2,1)S(1)}, bf16[96,1024]{1,0:T(8,128)(2,1)S(1)}, u32[]{:S(2)}, u32[]{:S(2)}) collective-permute-start(bf16[96,1024]{1,0:T(8,128)(2,1)S(1)} %collective-permute-done), channel_id=1, source_target_pairs={{0,16},{16,0},{32,48},{48,32},{64,80},{80,64},{96,112},{112,96},{1... | collective-permute-start | bytes 589832 | tf_op jit(solution)/shard_map/ppermute | solution.py:46
  21.8 12.3 %collective-permute-start.9 = (bf16[2,512,896]{2,1,0:T(8,128)(2,1)}, bf16[2,512,896]{2,1,0:T(8,128)(2,1)S(1)}, u32[]{:S(2)}, u32[]{:S(2)}) collective-permute-start(bf16[2,512,896]{2,1,0:T(8,128)(2,1)} %get-tuple-element.70), channel_id=1, source_target_pairs={{0,1},{1,0},{2,3},{3,2},{4,5},{5,4},{6,7},{7,6},{8,9},{9,8},{10,11... | collective-permute-start | bytes 5505032 | tf_op jit(solution)/shard_map/ppermute | solution.py:35
  21.8 6.3 %collective-permute-start.10 = (bf16[896,512]{1,0:T(8,128)(2,1)S(1)}, bf16[896,512]{1,0:T(8,128)(2,1)S(1)}, u32[]{:S(2)}, u32[]{:S(2)}) collective-permute-start(bf16[896,512]{1,0:T(8,128)(2,1)S(1)} %get-tuple-element.72), channel_id=1, source_target_pairs={{0,1},{1,0},{2,3},{3,2},{4,5},{5,4},{6,7},{7,6},{8,9},{9,8},{10,11... | collective-permute-start | bytes 2752520 | tf_op jit(solution)/shard_map/ppermute | solution.py:35
  32.4 17.6 %collective-permute-start.11 = (bf16[384,896]{1,0:T(8,128)(2,1)S(1)}, bf16[384,896]{1,0:T(8,128)(2,1)S(1)}, u32[]{:S(2)}, u32[]{:S(2)}) collective-permute-start(bf16[384,896]{1,0:T(8,128)(2,1)S(1)} %shard_map.131), channel_id=1, source_target_pairs={{0,2},{1,3},{2,0},{3,1},{4,6},{5,7},{6,4},{7,5},{8,10},{9,11},{10,... | collective-permute-start | bytes 2064392 | tf_op jit(solution)/shard_map/ppermute | solution.py:40
  35.7 19.6 %collective-permute-start.14 = (bf16[384,896]{1,0:T(8,128)(2,1)S(1)}, bf16[384,896]{1,0:T(8,128)(2,1)S(1)}, u32[]{:S(2)}, u32[]{:S(2)}) collective-permute-start(bf16[384,896]{1,0:T(8,128)(2,1)S(1)} %shard_map.132), channel_id=1, source_target_pairs={{0,12},{1,13},{2,14},{3,15},{4,8},{5,9},{6,10},{7,11},{8,4},{9,5},... | collective-permute-start | bytes 2064392 | tf_op jit(solution)/shard_map/ppermute | solution.py:40
  41.4 18.4 %collective-permute-start.17 = (bf16[384,896]{1,0:T(8,128)(2,1)S(1)}, bf16[384,896]{1,0:T(8,128)(2,1)S(1)}, u32[]{:S(2)}, u32[]{:S(2)}) collective-permute-start(bf16[384,896]{1,0:T(8,128)(2,1)S(1)} %shard_map.133), channel_id=1, source_target_pairs={{0,4},{1,5},{2,6},{3,7},{4,0},{5,1},{6,2},{7,3},{8,12},{9,13},{10,... | collective-permute-start | bytes 2064392 | tf_op jit(solution)/shard_map/ppermute | solution.py:40
  50.2 15.6 %collective-permute-start.12 = (bf16[192,896]{1,0:T(8,128)(2,1)S(1)}, bf16[192,896]{1,0:T(8,128)(2,1)S(1)}, u32[]{:S(2)}, u32[]{:S(2)}) collective-permute-start(bf16[192,896]{1,0:T(8,128)(2,1)S(1)} %slice.108), channel_id=1, source_target_pairs={{0,4},{1,5},{2,6},{3,7},{4,0},{5,1},{6,2},{7,3},{8,12},{9,13},{10,... | collective-permute-start | bytes 1032200 | tf_op jit(solution)/shard_map/ppermute | solution.py:40
  55.4 10.8 %collective-permute-start.15 = (bf16[192,896]{1,0:T(8,128)(2,1)S(1)}, bf16[192,896]{1,0:T(8,128)(2,1)S(1)}, u32[]{:S(2)}, u32[]{:S(2)}) collective-permute-start(bf16[192,896]{1,0:T(8,128)(2,1)S(1)} %slice.107), channel_id=1, source_target_pairs={{0,2},{1,3},{2,0},{3,1},{4,6},{5,7},{6,4},{7,5},{8,10},{9,11},{10,... | collective-permute-start | bytes 1032200 | tf_op jit(solution)/shard_map/ppermute | solution.py:40
  60.0 8.6 %collective-permute-start.18 = (bf16[192,896]{1,0:T(8,128)(2,1)S(1)}, bf16[192,896]{1,0:T(8,128)(2,1)S(1)}, u32[]{:S(2)}, u32[]{:S(2)}) collective-permute-start(bf16[192,896]{1,0:T(8,128)(2,1)S(1)} %slice.106), channel_id=1, source_target_pairs={{0,12},{1,13},{2,14},{3,15},{4,8},{5,9},{6,10},{7,11},{8,4},{9,5},... | collective-permute-start | bytes 1032200 | tf_op jit(solution)/shard_map/ppermute | solution.py:40
  65.9 6.7 %collective-permute-start.13 = (bf16[96,896]{1,0:T(8,128)(2,1)S(1)}, bf16[96,896]{1,0:T(8,128)(2,1)S(1)}, u32[]{:S(2)}, u32[]{:S(2)}) collective-permute-start(bf16[96,896]{1,0:T(8,128)(2,1)S(1)} %slice.111), channel_id=1, source_target_pairs={{0,12},{1,13},{2,14},{3,15},{4,8},{5,9},{6,10},{7,11},{8,4},{9,5},... | collective-permute-start | bytes 516104 | tf_op jit(solution)/shard_map/ppermute | solution.py:40
  74.7 7.3 %collective-permute-start.20 = (bf16[96,896]{1,0:T(8,128)(2,1)S(1)}, bf16[96,896]{1,0:T(8,128)(2,1)S(1)}, u32[]{:S(2)}, u32[]{:S(2)}) collective-permute-start(bf16[96,896]{1,0:T(8,128)(2,1)S(1)} %get-tuple-element.110), channel_id=1, source_target_pairs={{0,2},{1,3},{2,0},{3,1},{4,6},{5,7},{6,4},{7,5},{8,10},{9,11},{10,... | collective-permute-start | bytes 516104 | tf_op jit(solution)/shard_map/ppermute | solution.py:40
  75.4 9.5 %collective-permute-start.24 = (bf16[96,896]{1,0:T(8,128)(2,1)S(1)}, bf16[96,896]{1,0:T(8,128)(2,1)S(1)}, u32[]{:S(2)}, u32[]{:S(2)}) collective-permute-start(bf16[96,896]{1,0:T(8,128)(2,1)S(1)} %get-tuple-element.109), channel_id=1, source_target_pairs={{0,12},{1,13},{2,14},{3,15},{4,8},{5,9},{6,10},{7,11},{8,4},{9,5},... | collective-permute-start | bytes 516104 | tf_op jit(solution)/shard_map/ppermute | solution.py:40
  80.2 7.3 %collective-permute-start.23 = (bf16[192,896]{1,0:T(8,128)(2,1)S(1)}, bf16[192,896]{1,0:T(8,128)(2,1)S(1)}, u32[]{:S(2)}, u32[]{:S(2)}) collective-permute-start(bf16[192,896]{1,0:T(8,128)(2,1)S(1)} %pad_maximum_fusion.5), channel_id=1, source_target_pairs={{0,2},{1,3},{2,0},{3,1},{4,6},{5,7},{6,4},{7,5},{8,10},{9,11},{10,... | collective-permute-start | bytes 1032200 | tf_op jit(solution)/shard_map/ppermute | solution.py:40
  82.1 11.8 %collective-permute-start.21 = (bf16[192,896]{1,0:T(8,128)(2,1)S(1)}, bf16[192,896]{1,0:T(8,128)(2,1)S(1)}, u32[]{:S(2)}, u32[]{:S(2)}) collective-permute-start(bf16[192,896]{1,0:T(8,128)(2,1)S(1)} %pad_maximum_fusion.4), channel_id=1, source_target_pairs={{0,12},{1,13},{2,14},{3,15},{4,8},{5,9},{6,10},{7,11},{8,4},{9,5},... | collective-permute-start | bytes 1032200 | tf_op jit(solution)/shard_map/ppermute | solution.py:40
  84.9 10.6 %collective-permute-start.25 = (bf16[192,896]{1,0:T(8,128)(2,1)S(1)}, bf16[192,896]{1,0:T(8,128)(2,1)S(1)}, u32[]{:S(2)}, u32[]{:S(2)}) collective-permute-start(bf16[192,896]{1,0:T(8,128)(2,1)S(1)} %pad_maximum_fusion.6), channel_id=1, source_target_pairs={{0,4},{1,5},{2,6},{3,7},{4,0},{5,1},{6,2},{7,3},{8,12},{9,13},{10,... | collective-permute-start | bytes 1032200 | tf_op jit(solution)/shard_map/ppermute | solution.py:40
  87.6 17.8 %collective-permute-start.27 = (bf16[384,896]{1,0:T(8,128)(2,1)S(1)}, bf16[384,896]{1,0:T(8,128)(2,1)S(1)}, u32[]{:S(2)}, u32[]{:S(2)}) collective-permute-start(bf16[384,896]{1,0:T(8,128)(2,1)S(1)} %pad_maximum_fusion.2.refs_1_), channel_id=1, source_target_pairs={{0,12},{1,13},{2,14},{3,15},{4,8},{5,9},{6,10},{7,11},{8,4},{9,5},... | collective-permute-start | bytes 2064392 | tf_op jit(solution)/shard_map/ppermute | solution.py:40
  94.0 13.0 %collective-permute-start.26 = (bf16[384,896]{1,0:T(8,128)(2,1)S(1)}, bf16[384,896]{1,0:T(8,128)(2,1)S(1)}, u32[]{:S(2)}, u32[]{:S(2)}) collective-permute-start(bf16[384,896]{1,0:T(8,128)(2,1)S(1)} %pad_maximum_fusion.1.refs_0_), channel_id=1, source_target_pairs={{0,4},{1,5},{2,6},{3,7},{4,0},{5,1},{6,2},{7,3},{8,12},{9,13},{10,... | collective-permute-start | bytes 2064392 | tf_op jit(solution)/shard_map/ppermute | solution.py:40
  95.6 11.4 %collective-permute-start.28 = (bf16[384,896]{1,0:T(8,128)(2,1)S(1)}, bf16[384,896]{1,0:T(8,128)(2,1)S(1)}, u32[]{:S(2)}, u32[]{:S(2)}) collective-permute-start(bf16[384,896]{1,0:T(8,128)(2,1)S(1)} %pad_maximum_fusion.3.refs_2_), channel_id=1, source_target_pairs={{0,2},{1,3},{2,0},{3,1},{4,6},{5,7},{6,4},{7,5},{8,10},{9,11},{10,... | collective-permute-start | bytes 2064392 | tf_op jit(solution)/shard_map/ppermute | solution.py:40
  117.7 10.5 %collective-permute-start.30 = (bf16[768,2688]{1,0:T(8,128)(2,1)S(1)}, bf16[768,2688]{1,0:T(8,128)(2,1)S(1)}, u32[]{:S(2)}, u32[]{:S(2)}) collective-permute-start(bf16[768,2688]{1,0:T(8,128)(2,1)S(1)} %shard_map.134.acts), channel_id=1, source_target_pairs={{0,1},{1,0},{2,3},{3,2},{4,5},{5,4},{6,7},{7,6},{8,9},{9,8},{10,11... | collective-permute-start | bytes 12386312 | tf_op jit(solution)/shard_map/ppermute | solution.py:35
  118.2 9.2 %collective-permute-start.31 = (bf16[2,96,512]{2,1,0:T(8,128)(2,1)S(1)}, bf16[2,96,512]{2,1,0:T(8,128)(2,1)S(1)}, u32[]{:S(2)}, u32[]{:S(2)}) collective-permute-start(bf16[2,96,512]{2,1,0:T(8,128)(2,1)S(1)} %get-tuple-element.79), channel_id=1, source_target_pairs={{0,16},{16,0},{32,48},{48,32},{64,80},{80,64},{96,112},{112,96},{1... | collective-permute-start | bytes 589832 | tf_op jit(solution)/shard_map/ppermute | solution.py:46
  119.0 8.4 %collective-permute-start.32 = (bf16[2,96,512]{2,1,0:T(8,128)(2,1)S(1)}, bf16[2,96,512]{2,1,0:T(8,128)(2,1)S(1)}, u32[]{:S(2)}, u32[]{:S(2)}) collective-permute-start(bf16[2,96,512]{2,1,0:T(8,128)(2,1)S(1)} %get-tuple-element.80), channel_id=1, source_target_pairs={{0,48},{16,32},{32,16},{48,0},{64,112},{80,96},{96,80},{112,64},{1... | collective-permute-start | bytes 589832 | tf_op jit(solution)/shard_map/ppermute | solution.py:46
  120.0 8.1 %collective-permute-start.33 = (bf16[2,96,512]{2,1,0:T(8,128)(2,1)S(1)}, bf16[2,96,512]{2,1,0:T(8,128)(2,1)S(1)}, u32[]{:S(2)}, u32[]{:S(2)}) collective-permute-start(bf16[2,96,512]{2,1,0:T(8,128)(2,1)S(1)} %get-tuple-element.81), channel_id=1, source_target_pairs={{0,64},{16,80},{32,96},{48,112},{64,0},{80,16},{96,32},{112,48},{1... | collective-permute-start | bytes 589832 | tf_op jit(solution)/shard_map/ppermute | solution.py:46
  128.3 14.1 %collective-permute-start.35 = (f32[2,96,512]{2,1,0:T(8,128)S(1)}, f32[2,96,512]{2,1,0:T(8,128)S(1)}, u32[]{:S(2)}, u32[]{:S(2)}) collective-permute-start(f32[2,96,512]{2,1,0:T(8,128)S(1)} %get-tuple-element.95), channel_id=1, source_target_pairs={{0,64},{16,80},{32,96},{48,112},{64,0},{80,16},{96,32},{112,48},{1... | collective-permute-start | bytes 1179656 | tf_op jit(solution)/shard_map/ppermute | solution.py:46
  131.1 9.2 %collective-permute-start.34 = (bf16[2,96,512]{2,1,0:T(8,128)(2,1)S(1)}, bf16[2,96,512]{2,1,0:T(8,128)(2,1)S(1)}, u32[]{:S(2)}, u32[]{:S(2)}) collective-permute-start(bf16[2,96,512]{2,1,0:T(8,128)(2,1)S(1)} %get-tuple-element.94), channel_id=1, source_target_pairs={{0,32},{16,48},{32,0},{48,16},{64,96},{80,112},{96,64},{112,80},{1... | collective-permute-start | bytes 589832 | tf_op jit(solution)/shard_map/ppermute | solution.py:46
  133.5 8.3 %collective-permute-start.36 = (bf16[2,96,512]{2,1,0:T(8,128)(2,1)S(1)}, bf16[2,96,512]{2,1,0:T(8,128)(2,1)S(1)}, u32[]{:S(2)}, u32[]{:S(2)}) collective-permute-start(bf16[2,96,512]{2,1,0:T(8,128)(2,1)S(1)} %get-tuple-element.96), channel_id=1, source_target_pairs={{0,16},{16,0},{32,48},{48,32},{64,80},{80,64},{96,112},{112,96},{1... | collective-permute-start | bytes 589832 | tf_op jit(solution)/shard_map/ppermute | solution.py:46
  134.2 8.2 %collective-permute-start.37 = (bf16[2,96,512]{2,1,0:T(8,128)(2,1)S(1)}, bf16[2,96,512]{2,1,0:T(8,128)(2,1)S(1)}, u32[]{:S(2)}, u32[]{:S(2)}) collective-permute-start(bf16[2,96,512]{2,1,0:T(8,128)(2,1)S(1)} %get-tuple-element.97), channel_id=1, source_target_pairs={{0,48},{16,32},{32,16},{48,0},{64,112},{80,96},{96,80},{112,64},{1... | collective-permute-start | bytes 589832 | tf_op jit(solution)/shard_map/ppermute | solution.py:46
  (9 other events, 36.7 us)

commit v5 on v4

--- a/solution.py
+++ b/solution.py
@@ -98,14 +98,16 @@
 
 
 def prepare_kernel(info, gm, um, dm, g, u, d, gu_out, d_out, *, kept):
-    f = pl.program_id(0)
-    n = g.shape[1] // BLK
+    rows, n = g.shape[0] // BLK, g.shape[1] // BLK
     first = (info[0] if kept else 1 - info[0]) * n
-    for j in range(n):
-        at = slice(j * BLK, (j + 1) * BLK)
-        gu_out[0, :, at] = times(g[:, at], gm[f, first + j])
-        gu_out[1, :, at] = times(u[:, at], um[f, first + j])
-        d_out[at, :] = times(d[at, :], dm[first + j, f])
+    for k in range(rows):
+        f = pl.program_id(0) * rows + k
+        of = slice(k * BLK, (k + 1) * BLK)
+        for j in range(n):
+            at = slice(j * BLK, (j + 1) * BLK)
+            gu_out[0, of, at] = times(g[of, at], gm[f, first + j])
+            gu_out[1, of, at] = times(u[of, at], um[f, first + j])
+            d_out[at, of] = times(d[at, of], dm[first + j, f])
 
 
 def prepare(info, masks, gate_weight, up_weight, down_weight, kept):
@@ -115,16 +117,17 @@
     def side(info):
         return info[0] if kept else 1 - info[0]
 
-    wide = pl.BlockSpec((BLK, half), lambda f, info, *_: (f, side(info)))
-    tall = pl.BlockSpec((half, BLK), lambda f, info, *_: (side(info), f))
+    step = 2 * BLK
+    wide = pl.BlockSpec((step, half), lambda f, info, *_: (f, side(info)))
+    tall = pl.BlockSpec((half, step), lambda f, info, *_: (side(info), f))
     return call(
         functools.partial(prepare_kernel, kept=kept),
         4,
-        (width // BLK,),
+        (width // step,),
         [wide, wide, tall],
         [
-            pl.BlockSpec((2, BLK, half), lambda f, *_: (0, f, 0)),
-            pl.BlockSpec((half, BLK), lambda f, *_: (0, f)),
+            pl.BlockSpec((2, step, half), lambda f, *_: (0, f, 0)),
+            pl.BlockSpec((half, step), lambda f, *_: (0, f)),
         ],
         [shape((2, width, half), BF), shape((half, width), BF)],
         size=6 * width * hidden,
@@ -333,10 +336,10 @@
     masks = (gate_mask, up_mask, down_mask)
     info = lax.dynamic_index_in_dim(jnp.asarray(make_table()), lax.axis_index("col"), 0, keepdims=False)
     both = jnp.concatenate([tokens, cotangent], axis=1)
-    x, a, b, ab = (swap_row(both, d) for d in ("X", "A", "B", "AB"))
+    a, b, x, ab = (swap_row(both, d) for d in ("A", "B", "X", "AB"))
     weights = (gate_weight, up_weight, down_weight)
     gu_send, d_send = prepare(info, masks, *weights, False)
-    gu_send, d_send, x, a, b, ab, *weights = lax.optimization_barrier((gu_send, d_send, x, a, b, ab, *weights))
+    gu_send, d_send, a, b, x, ab, *weights = lax.optimization_barrier((gu_send, d_send, a, b, x, ab, *weights))
     ax, bx, abx = swap_row(x, "A"), swap_row(x, "B"), swap_row(ab, "X")
     gu_oth, d_oth = swap_core(gu_send), swap_core(d_send)
     gu_own, d_own = prepare(info, masks, *weights, True)

time: 144 us -> 142 us (0.986)
  starting transfers between devices: 44.7 us -> 49.4 us
  waiting for transfers between devices: 54.5 us -> 50.6 us
  Pallas kernels: 35.3 us -> 32.9 us
    ppermute x18, waiting for transfers between devices: 46.1 us -> 39.5 us  [swap_cube(): lax.ppermute(part, 'col', [(i, flip_col(i, order[step])) for i in range(1...]
    ppermute x18, starting transfers between devices: 20.3 us -> 25.8 us  [swap_cube(): lax.ppermute(part, 'col', [(i, flip_col(i, order[step])) for i in range(1...]
    ppermute x14, waiting for transfers between devices: 3.26 us -> 5.92 us  [swap_row(): lax.ppermute(value, 'row', [(i, flip_row(i, dims)) for i in range(8)])]
    pallas_call x2, Pallas kernels: 9.83 us -> 7.44 us  [prepare(): call(functools.partial(prepare_kernel, kept=kept), 4, (width // step,), [...]
  transfers between devices with their start and end apart: 38 -> 38, of which waited for: 21 -> 24; matrix products, arithmetic and copies ran while one was open for 2% -> 2% of each run, Pallas kernels for 22% -> 20%
where the time goes in v5:
time: 142 us
  waiting for transfers between devices  50.6 us (36%)
  starting transfers between devices  49.4 us (35%)
  Pallas kernels  32.9 us (23%)
  local copies, waits for them, and re-layouts  5.63 us (4%)
  other arithmetic  2.18 us (2%)
    ppermute x18, waiting for transfers between devices, swap_cube(): lax.ppermute(part, 'col', [(i, flip_col(i, order[step])) for i in range(1...  39.5 us
    ppermute x18, starting transfers between devices, swap_cube(): lax.ppermute(part, 'col', [(i, flip_col(i, order[step])) for i in range(1...  25.8 us
    ppermute x14, starting transfers between devices, swap_row(): lax.ppermute(value, 'row', [(i, flip_row(i, dims)) for i in range(8)])  22 us
    pallas_call x2, Pallas kernels, grads(): call(functools.partial(grads_kernel, mine=not into), 4, (1,), [whole(v.sh...  9.36 us
    pallas_call x4, Pallas kernels, project(): call(functools.partial(project_kernel, base=base, parts=parts), 1, (1,),...  8.4 us
    pallas_call x2, Pallas kernels, prepare(): call(functools.partial(prepare_kernel, kept=kept), 4, (width // step,), [...  7.44 us
    pallas_call x2, Pallas kernels, backward(): call(backward_kernel, 0, (width // step,), [whole(acts.shape), pl.BlockSp...  6.59 us
    ppermute x14, waiting for transfers between devices, swap_row(): lax.ppermute(value, 'row', [(i, flip_row(i, dims)) for i in range(8)])  5.92 us
  transfers between devices with their start and end apart: 38, of which 24 were waited for; matrix products, arithmetic and copies ran while one was open for 2% of the time, Pallas kernels for 20%

profile of v5, /device:TPU:0, one launch (start us, length us, event | category | flops | bytes accessed | tf_op | source)
XLA Modules:
  0.0 141.6 jit_solution(4553493530130243368)
XLA Ops:
  2.4 3.3 %collective-permute-start.3 = (bf16[96,1024]{1,0:T(8,128)(2,1)S(1)}, bf16[96,1024]{1,0:T(8,128)(2,1)S(1)}, u32[]{:S(2)}, u32[]{:S(2)}) collective-permute-start(bf16[96,1024]{1,0:T(8,128)(2,1)S(1)} %constant_dynamic-update-slice_fusion), channel_id=1, source_target_pairs={{0,32},{16,48},{32,0},{48,16},{64,96},{80,112},{96,64},{112,80},{1... | collective-permute-start | bytes 589832 | tf_op jit(solution)/shard_map/ppermute | solution.py:46
  5.7 3.0 %collective-permute-start.2 = (bf16[96,1024]{1,0:T(8,128)(2,1)S(1)}, bf16[96,1024]{1,0:T(8,128)(2,1)S(1)}, u32[]{:S(2)}, u32[]{:S(2)}) collective-permute-start(bf16[96,1024]{1,0:T(8,128)(2,1)S(1)} %constant_dynamic-update-slice_fusion), channel_id=1, source_target_pairs={{0,64},{16,80},{32,96},{48,112},{64,0},{80,16},{96,32},{112,48},{1... | collective-permute-start | bytes 589832 | tf_op jit(solution)/shard_map/ppermute | solution.py:46
  12.6 3.7 %shard_map.128 = (bf16[2,512,896]{2,1,0:T(8,128)(2,1)}, bf16[896,512]{1,0:T(8,128)(2,1)S(1)}) custom-call(s32[25]{0:T(128)S(1)} %dynamic-slice_bitcast_fusion.info, s32[4,14]{1,0:T(4,128)S(1)} %copy-done.1, s32[4,14]{1,0:T(4,128)S(1)} %copy-done.2, s32[14,4]{1,0:T(8,128)S(1)} %copy.17.dm, bf16[512,1792]{1,0:T(8,128)(2,1)} %g.2, bf16[512,1792]{1,0:T(8,128)(2,1)} %u.2, ...), custom_call_target="tpu_custom_call" | custom-call | bytes 5505024 | tf_op jit(solution)/shard_map/pallas_call | solution.py:123
  16.4 1.9 %collective-permute-start.6 = (bf16[96,1024]{1,0:T(8,128)(2,1)S(1)}, bf16[96,1024]{1,0:T(8,128)(2,1)S(1)}, u32[]{:S(2)}, u32[]{:S(2)}) collective-permute-start(bf16[96,1024]{1,0:T(8,128)(2,1)S(1)} %collective-permute-done.3), channel_id=1, source_target_pairs={{0,64},{16,80},{32,96},{48,112},{64,0},{80,16},{96,32},{112,48},{1... | collective-permute-start | bytes 589832 | tf_op jit(solution)/shard_map/ppermute | solution.py:46
  18.3 2.6 %collective-permute-start.5 = (bf16[96,1024]{1,0:T(8,128)(2,1)S(1)}, bf16[96,1024]{1,0:T(8,128)(2,1)S(1)}, u32[]{:S(2)}, u32[]{:S(2)}) collective-permute-start(bf16[96,1024]{1,0:T(8,128)(2,1)S(1)} %collective-permute-done.2), channel_id=1, source_target_pairs={{0,48},{16,32},{32,16},{48,0},{64,112},{80,96},{96,80},{112,64},{1... | collective-permute-start | bytes 589832 | tf_op jit(solution)/shard_map/ppermute | solution.py:46
  21.4 3.7 %shard_map.129 = (bf16[2,512,896]{2,1,0:T(8,128)(2,1)}, bf16[896,512]{1,0:T(8,128)(2,1)S(1)}) custom-call(s32[25]{0:T(128)S(1)} %dynamic-slice_bitcast_fusion.info, s32[4,14]{1,0:T(4,128)S(1)} %copy-done.1, s32[4,14]{1,0:T(4,128)S(1)} %copy-done.2, s32[14,4]{1,0:T(8,128)S(1)} %copy.17.dm, bf16[512,1792]{1,0:T(8,128)(2,1)} %g.2, bf16[512,1792]{1,0:T(8,128)(2,1)} %u.2, ...), custom_call_target="tpu_custom_call" | custom-call | bytes 5505024 | tf_op jit(solution)/shard_map/pallas_call | solution.py:123
  30.8 1.6 %shard_map.131 = bf16[384,896]{1,0:T(8,128)(2,1)S(1)} custom-call(s32[25]{0:T(128)S(1)} %dynamic-slice_bitcast_fusion.info, bf16[384,1024]{1,0:T(8,128)(2,1)S(1)} %pad_maximum_fusion.own_a, bf16[384,1024]{1,0:T(8,128)(2,1)S(1)} %constant_dynamic-update-slice_fusion.2.own_b, bf16[384,1024]{1,0:T(8,128)(2,1)S(1)} %collective-permute-done.7.oth_a, ...), custom_call_target="tpu_custom_call" | custom-call | flops 704643072 | bytes 4784128 | tf_op jit(solution)/shard_map/pallas_call | solution.py:180
  33.0 1.6 %shard_map.132 = bf16[384,896]{1,0:T(8,128)(2,1)S(1)} custom-call(s32[25]{0:T(128)S(1)} %dynamic-slice_bitcast_fusion.info, bf16[384,1024]{1,0:T(8,128)(2,1)S(1)} %pad_maximum_fusion.own_a, bf16[384,1024]{1,0:T(8,128)(2,1)S(1)} %constant_dynamic-update-slice_fusion.2.own_b, bf16[384,1024]{1,0:T(8,128)(2,1)S(1)} %collective-permute-done.7.oth_a, ...), custom_call_target="tpu_custom_call" | custom-call | flops 704643072 | bytes 4784128 | tf_op jit(solution)/shard_map/pallas_call | solution.py:180
  34.6 4.1 %collective-permute-start.14 = (bf16[384,896]{1,0:T(8,128)(2,1)S(1)}, bf16[384,896]{1,0:T(8,128)(2,1)S(1)}, u32[]{:S(2)}, u32[]{:S(2)}) collective-permute-start(bf16[384,896]{1,0:T(8,128)(2,1)S(1)} %shard_map.132), channel_id=1, source_target_pairs={{0,12},{1,13},{2,14},{3,15},{4,8},{5,9},{6,10},{7,11},{8,4},{9,5},... | collective-permute-start | bytes 2064392 | tf_op jit(solution)/shard_map/ppermute | solution.py:40
  40.5 3.5 %shard_map.130 = (f32[384,896]{1,0:T(8,128)S(1)}, f32[384,896]{1,0:T(8,128)S(1)}, f32[384,896]{1,0:T(8,128)S(1)}) custom-call(s32[25]{0:T(128)S(1)} %dynamic-slice_bitcast_fusion.info, bf16[384,1024]{1,0:T(8,128)(2,1)S(1)} %pad_maximum_fusion.own_a, bf16[384,1024]{1,0:T(8,128)(2,1)S(1)} %constant_dynamic-update-slice_fusion.2.own_b, ...), custom_call_target="tpu_custom_call" | custom-call | flops 2113929216 | bytes 11206656 | tf_op jit(solution)/shard_map/pallas_call | solution.py:180
  44.0 6.0 %collective-permute-done.11 = bf16[384,896]{1,0:T(8,128)(2,1)S(1)} collective-permute-done((bf16[384,896]{1,0:T(8,128)(2,1)S(1)}, bf16[384,896]{1,0:T(8,128)(2,1)S(1)}, u32[]{:S(2)}, u32[]{:S(2)}) %collective-permute-start.11) | collective-permute-done | bytes 688160 | tf_op jit(solution)/shard_map/ppermute | solution.py:40
  50.1 2.0 %collective-permute-start.12 = (bf16[192,896]{1,0:T(8,128)(2,1)S(1)}, bf16[192,896]{1,0:T(8,128)(2,1)S(1)}, u32[]{:S(2)}, u32[]{:S(2)}) collective-permute-start(bf16[192,896]{1,0:T(8,128)(2,1)S(1)} %slice.108), channel_id=1, source_target_pairs={{0,4},{1,5},{2,6},{3,7},{4,0},{5,1},{6,2},{7,3},{8,12},{9,13},{10,... | collective-permute-start | bytes 1032200 | tf_op jit(solution)/shard_map/ppermute | solution.py:40
  52.1 2.1 %collective-permute-done.14 = bf16[384,896]{1,0:T(8,128)(2,1)S(1)} collective-permute-done((bf16[384,896]{1,0:T(8,128)(2,1)S(1)}, bf16[384,896]{1,0:T(8,128)(2,1)S(1)}, u32[]{:S(2)}, u32[]{:S(2)}) %collective-permute-start.14) | collective-permute-done | bytes 688160 | tf_op jit(solution)/shard_map/ppermute | solution.py:40
  56.0 2.8 %collective-permute-done.17 = bf16[384,896]{1,0:T(8,128)(2,1)S(1)} collective-permute-done((bf16[384,896]{1,0:T(8,128)(2,1)S(1)}, bf16[384,896]{1,0:T(8,128)(2,1)S(1)}, u32[]{:S(2)}, u32[]{:S(2)}) %collective-permute-start.17) | collective-permute-done | bytes 688160 | tf_op jit(solution)/shard_map/ppermute | solution.py:40
  59.2 5.5 %collective-permute-done.12 = bf16[192,896]{1,0:T(8,128)(2,1)S(1)} collective-permute-done((bf16[192,896]{1,0:T(8,128)(2,1)S(1)}, bf16[192,896]{1,0:T(8,128)(2,1)S(1)}, u32[]{:S(2)}, u32[]{:S(2)}) %collective-permute-start.12) | collective-permute-done | bytes 344096 | tf_op jit(solution)/shard_map/ppermute | solution.py:40
  65.4 2.2 %collective-permute-done.18 = bf16[192,896]{1,0:T(8,128)(2,1)S(1)} collective-permute-done((bf16[192,896]{1,0:T(8,128)(2,1)S(1)}, bf16[192,896]{1,0:T(8,128)(2,1)S(1)}, u32[]{:S(2)}, u32[]{:S(2)}) %collective-permute-start.18) | collective-permute-done | bytes 344096 | tf_op jit(solution)/shard_map/ppermute | solution.py:40
  67.7 1.8 %collective-permute-start.19 = (bf16[96,896]{1,0:T(8,128)(2,1)S(1)}, bf16[96,896]{1,0:T(8,128)(2,1)S(1)}, u32[]{:S(2)}, u32[]{:S(2)}) collective-permute-start(bf16[96,896]{1,0:T(8,128)(2,1)S(1)} %slice.109), channel_id=1, source_target_pairs={{0,2},{1,3},{2,0},{3,1},{4,6},{5,7},{6,4},{7,5},{8,10},{9,11},{10,... | collective-permute-start | bytes 516104 | tf_op jit(solution)/shard_map/ppermute | solution.py:40
  69.5 2.1 %collective-permute-done.13 = bf16[96,896]{1,0:T(8,128)(2,1)S(1)} collective-permute-done((bf16[96,896]{1,0:T(8,128)(2,1)S(1)}, bf16[96,896]{1,0:T(8,128)(2,1)S(1)}, u32[]{:S(2)}, u32[]{:S(2)}) %collective-permute-start.13) | collective-permute-done | bytes 172064 | tf_op jit(solution)/shard_map/ppermute | solution.py:40
  71.5 1.8 %collective-permute-done.19 = bf16[96,896]{1,0:T(8,128)(2,1)S(1)} collective-permute-done((bf16[96,896]{1,0:T(8,128)(2,1)S(1)}, bf16[96,896]{1,0:T(8,128)(2,1)S(1)}, u32[]{:S(2)}, u32[]{:S(2)}) %collective-permute-start.19) | collective-permute-done | bytes 172064 | tf_op jit(solution)/shard_map/ppermute | solution.py:40
  75.3 2.7 %collective-permute-start.24 = (bf16[96,896]{1,0:T(8,128)(2,1)S(1)}, bf16[96,896]{1,0:T(8,128)(2,1)S(1)}, u32[]{:S(2)}, u32[]{:S(2)}) collective-permute-start(bf16[96,896]{1,0:T(8,128)(2,1)S(1)} %get-tuple-element.109), channel_id=1, source_target_pairs={{0,12},{1,13},{2,14},{3,15},{4,8},{5,9},{6,10},{7,11},{8,4},{9,5},... | collective-permute-start | bytes 516104 | tf_op jit(solution)/shard_map/ppermute | solution.py:40
  81.1 2.7 %collective-permute-start.21 = (bf16[192,896]{1,0:T(8,128)(2,1)S(1)}, bf16[192,896]{1,0:T(8,128)(2,1)S(1)}, u32[]{:S(2)}, u32[]{:S(2)}) collective-permute-start(bf16[192,896]{1,0:T(8,128)(2,1)S(1)} %pad_maximum_fusion.4), channel_id=1, source_target_pairs={{0,12},{1,13},{2,14},{3,15},{4,8},{5,9},{6,10},{7,11},{8,4},{9,5},... | collective-permute-start | bytes 1032200 | tf_op jit(solution)/shard_map/ppermute | solution.py:40
  86.6 2.6 %collective-permute-start.27 = (bf16[384,896]{1,0:T(8,128)(2,1)S(1)}, bf16[384,896]{1,0:T(8,128)(2,1)S(1)}, u32[]{:S(2)}, u32[]{:S(2)}) collective-permute-start(bf16[384,896]{1,0:T(8,128)(2,1)S(1)} %pad_maximum_fusion.2.refs_1_), channel_id=1, source_target_pairs={{0,12},{1,13},{2,14},{3,15},{4,8},{5,9},{6,10},{7,11},{8,4},{9,5},... | collective-permute-start | bytes 2064392 | tf_op jit(solution)/shard_map/ppermute | solution.py:40
  89.1 3.4 %collective-permute-done.21 = bf16[192,896]{1,0:T(8,128)(2,1)S(1)} collective-permute-done((bf16[192,896]{1,0:T(8,128)(2,1)S(1)}, bf16[192,896]{1,0:T(8,128)(2,1)S(1)}, u32[]{:S(2)}, u32[]{:S(2)}) %collective-permute-start.21) | collective-permute-done | bytes 344096 | tf_op jit(solution)/shard_map/ppermute | solution.py:40
  96.3 8.1 %collective-permute-done.27.refs_4_ = bf16[384,896]{1,0:T(8,128)(2,1)S(1)} collective-permute-done((bf16[384,896]{1,0:T(8,128)(2,1)S(1)}, bf16[384,896]{1,0:T(8,128)(2,1)S(1)}, u32[]{:S(2)}, u32[]{:S(2)}) %collective-permute-start.27) | collective-permute-done | bytes 688160 | tf_op jit(solution)/shard_map/ppermute | solution.py:40
  106.8 3.3 %shard_map.136 = f32[2,768,512]{2,1,0:T(8,128)S(1)} custom-call(bf16[768,2688]{1,0:T(8,128)(2,1)S(1)} %shard_map.134.acts, bf16[2,512,896]{2,1,0:T(8,128)(2,1)S(1)} %collective-permute-done.9.refs_1_.refs_3_.gu, bf16[896,512]{1,0:T(8,128)(2,1)S(1)} %collective-permute-done.10.refs_5_.refs_1_.d), custom_call_target="tpu_custom_call" | custom-call | flops 2113929216 | bytes 6881280 | tf_op jit(solution)/shard_map/pallas_call | solution.py:254
  110.2 3.3 %shard_map.135 = f32[2,768,512]{2,1,0:T(8,128)S(1)} custom-call(bf16[768,2688]{1,0:T(8,128)(2,1)S(1)} %shard_map.134.acts, bf16[2,512,896]{2,1,0:T(8,128)(2,1)S(1)} %copy-done, bf16[896,512]{1,0:T(8,128)(2,1)S(1)} %get-tuple-element.71.refs_4_.refs_0_.d), custom_call_target="tpu_custom_call" | custom-call | flops 2113929216 | bytes 6881280 | tf_op jit(solution)/shard_map/pallas_call | solution.py:254
  113.5 2.3 %collective-permute-done.29 = f32[2,768,512]{2,1,0:T(8,128)S(1)} collective-permute-done((f32[2,768,512]{2,1,0:T(8,128)S(1)}, f32[2,768,512]{2,1,0:T(8,128)S(1)}, u32[]{:S(2)}, u32[]{:S(2)}) %collective-permute-start.29) | collective-permute-done | bytes 3145760 | tf_op jit(solution)/shard_map/ppermute | solution.py:35
  118.9 2.3 %collective-permute-start.33 = (bf16[2,96,512]{2,1,0:T(8,128)(2,1)S(1)}, bf16[2,96,512]{2,1,0:T(8,128)(2,1)S(1)}, u32[]{:S(2)}, u32[]{:S(2)}) collective-permute-start(bf16[2,96,512]{2,1,0:T(8,128)(2,1)S(1)} %get-tuple-element.81), channel_id=1, source_target_pairs={{0,64},{16,80},{32,96},{48,112},{64,0},{80,16},{96,32},{112,48},{1... | collective-permute-start | bytes 589832 | tf_op jit(solution)/shard_map/ppermute | solution.py:46
  121.1 4.7 %shard_map.138 = (bf16[512,1792]{1,0:T(8,128)(2,1)}, bf16[512,1792]{1,0:T(8,128)(2,1)}, bf16[1792,512]{1,0:T(8,128)(2,1)}) custom-call(s32[25]{0:T(128)S(1)} %dynamic-slice_bitcast_fusion.info, s32[4,14]{1,0:T(4,128)S(1)} %copy-done.1, s32[4,14]{1,0:T(4,128)S(1)} %copy-done.2, s32[14,4]{1,0:T(8,128)S(1)} %copy.17.dm, ...), custom_call_target="tpu_custom_call" | custom-call | flops 2113929216 | bytes 6881280 | tf_op jit(solution)/shard_map/pallas_call | solution.py:320
  127.4 2.1 %collective-permute-start.35 = (f32[2,96,512]{2,1,0:T(8,128)S(1)}, f32[2,96,512]{2,1,0:T(8,128)S(1)}, u32[]{:S(2)}, u32[]{:S(2)}) collective-permute-start(f32[2,96,512]{2,1,0:T(8,128)S(1)} %get-tuple-element.95), channel_id=1, source_target_pairs={{0,64},{16,80},{32,96},{48,112},{64,0},{80,16},{96,32},{112,48},{1... | collective-permute-start | bytes 1179656 | tf_op jit(solution)/shard_map/ppermute | solution.py:46
  129.5 2.2 %collective-permute-start.34 = (bf16[2,96,512]{2,1,0:T(8,128)(2,1)S(1)}, bf16[2,96,512]{2,1,0:T(8,128)(2,1)S(1)}, u32[]{:S(2)}, u32[]{:S(2)}) collective-permute-start(bf16[2,96,512]{2,1,0:T(8,128)(2,1)S(1)} %get-tuple-element.94), channel_id=1, source_target_pairs={{0,32},{16,48},{32,0},{48,16},{64,96},{80,112},{96,64},{112,80},{1... | collective-permute-start | bytes 589832 | tf_op jit(solution)/shard_map/ppermute | solution.py:46
  133.6 4.7 %shard_map.139 = (bf16[512,1792]{1,0:T(8,128)(2,1)}, bf16[512,1792]{1,0:T(8,128)(2,1)}, bf16[1792,512]{1,0:T(8,128)(2,1)}) custom-call(s32[25]{0:T(128)S(1)} %dynamic-slice_bitcast_fusion.info, s32[4,14]{1,0:T(4,128)S(1)} %copy-done.1, s32[4,14]{1,0:T(4,128)S(1)} %copy-done.2, ...), custom_call_target="tpu_custom_call", output_to_operand_aliasing={{0}: (7, {}), {1}: (8, {}), {2}: (9, {})} | custom-call | flops 2113929216 | bytes 6881280 | tf_op jit(solution)/shard_map/pallas_call | solution.py:320
  (95 shorter events, 40.8 us)
Async XLA Ops:
  2.4 13.9 %collective-permute-start.3 = (bf16[96,1024]{1,0:T(8,128)(2,1)S(1)}, bf16[96,1024]{1,0:T(8,128)(2,1)S(1)}, u32[]{:S(2)}, u32[]{:S(2)}) collective-permute-start(bf16[96,1024]{1,0:T(8,128)(2,1)S(1)} %constant_dynamic-update-slice_fusion), channel_id=1, source_target_pairs={{0,32},{16,48},{32,0},{48,16},{64,96},{80,112},{96,64},{112,80},{1... | collective-permute-start | bytes 589832 | tf_op jit(solution)/shard_map/ppermute | solution.py:46
  5.7 10.6 %collective-permute-start.2 = (bf16[96,1024]{1,0:T(8,128)(2,1)S(1)}, bf16[96,1024]{1,0:T(8,128)(2,1)S(1)}, u32[]{:S(2)}, u32[]{:S(2)}) collective-permute-start(bf16[96,1024]{1,0:T(8,128)(2,1)S(1)} %constant_dynamic-update-slice_fusion), channel_id=1, source_target_pairs={{0,64},{16,80},{32,96},{48,112},{64,0},{80,16},{96,32},{112,48},{1... | collective-permute-start | bytes 589832 | tf_op jit(solution)/shard_map/ppermute | solution.py:46
  8.7 7.6 %collective-permute-start.1 = (bf16[96,1024]{1,0:T(8,128)(2,1)S(1)}, bf16[96,1024]{1,0:T(8,128)(2,1)S(1)}, u32[]{:S(2)}, u32[]{:S(2)}) collective-permute-start(bf16[96,1024]{1,0:T(8,128)(2,1)S(1)} %constant_dynamic-update-slice_fusion), channel_id=1, source_target_pairs={{0,48},{16,32},{32,16},{48,0},{64,112},{80,96},{96,80},{112,64},{1... | collective-permute-start | bytes 589832 | tf_op jit(solution)/shard_map/ppermute | solution.py:46
  9.8 6.6 %collective-permute-start = (bf16[96,1024]{1,0:T(8,128)(2,1)S(1)}, bf16[96,1024]{1,0:T(8,128)(2,1)S(1)}, u32[]{:S(2)}, u32[]{:S(2)}) collective-permute-start(bf16[96,1024]{1,0:T(8,128)(2,1)S(1)} %constant_dynamic-update-slice_fusion), channel_id=1, source_target_pairs={{0,16},{16,0},{32,48},{48,32},{64,80},{80,64},{96,112},{112,96},{1... | collective-permute-start | bytes 589832 | tf_op jit(solution)/shard_map/ppermute | solution.py:46
  16.4 8.8 %collective-permute-start.6 = (bf16[96,1024]{1,0:T(8,128)(2,1)S(1)}, bf16[96,1024]{1,0:T(8,128)(2,1)S(1)}, u32[]{:S(2)}, u32[]{:S(2)}) collective-permute-start(bf16[96,1024]{1,0:T(8,128)(2,1)S(1)} %collective-permute-done.3), channel_id=1, source_target_pairs={{0,64},{16,80},{32,96},{48,112},{64,0},{80,16},{96,32},{112,48},{1... | collective-permute-start | bytes 589832 | tf_op jit(solution)/shard_map/ppermute | solution.py:46
  18.3 7.4 %collective-permute-start.5 = (bf16[96,1024]{1,0:T(8,128)(2,1)S(1)}, bf16[96,1024]{1,0:T(8,128)(2,1)S(1)}, u32[]{:S(2)}, u32[]{:S(2)}) collective-permute-start(bf16[96,1024]{1,0:T(8,128)(2,1)S(1)} %collective-permute-done.2), channel_id=1, source_target_pairs={{0,48},{16,32},{32,16},{48,0},{64,112},{80,96},{96,80},{112,64},{1... | collective-permute-start | bytes 589832 | tf_op jit(solution)/shard_map/ppermute | solution.py:46
  20.9 6.3 %collective-permute-start.4 = (bf16[96,1024]{1,0:T(8,128)(2,1)S(1)}, bf16[96,1024]{1,0:T(8,128)(2,1)S(1)}, u32[]{:S(2)}, u32[]{:S(2)}) collective-permute-start(bf16[96,1024]{1,0:T(8,128)(2,1)S(1)} %collective-permute-done.2), channel_id=1, source_target_pairs={{0,16},{16,0},{32,48},{48,32},{64,80},{80,64},{96,112},{112,96},{1... | collective-permute-start | bytes 589832 | tf_op jit(solution)/shard_map/ppermute | solution.py:46
  20.9 12.1 %collective-permute-start.9 = (bf16[2,512,896]{2,1,0:T(8,128)(2,1)}, bf16[2,512,896]{2,1,0:T(8,128)(2,1)S(1)}, u32[]{:S(2)}, u32[]{:S(2)}) collective-permute-start(bf16[2,512,896]{2,1,0:T(8,128)(2,1)} %get-tuple-element.70), channel_id=1, source_target_pairs={{0,1},{1,0},{2,3},{3,2},{4,5},{5,4},{6,7},{7,6},{8,9},{9,8},{10,11... | collective-permute-start | bytes 5505032 | tf_op jit(solution)/shard_map/ppermute | solution.py:35
  20.9 7.1 %collective-permute-start.10 = (bf16[896,512]{1,0:T(8,128)(2,1)S(1)}, bf16[896,512]{1,0:T(8,128)(2,1)S(1)}, u32[]{:S(2)}, u32[]{:S(2)}) collective-permute-start(bf16[896,512]{1,0:T(8,128)(2,1)S(1)} %get-tuple-element.72), channel_id=1, source_target_pairs={{0,1},{1,0},{2,3},{3,2},{4,5},{5,4},{6,7},{7,6},{8,9},{9,8},{10,11... | collective-permute-start | bytes 2752520 | tf_op jit(solution)/shard_map/ppermute | solution.py:35
  32.4 17.6 %collective-permute-start.11 = (bf16[384,896]{1,0:T(8,128)(2,1)S(1)}, bf16[384,896]{1,0:T(8,128)(2,1)S(1)}, u32[]{:S(2)}, u32[]{:S(2)}) collective-permute-start(bf16[384,896]{1,0:T(8,128)(2,1)S(1)} %shard_map.131), channel_id=1, source_target_pairs={{0,2},{1,3},{2,0},{3,1},{4,6},{5,7},{6,4},{7,5},{8,10},{9,11},{10,... | collective-permute-start | bytes 2064392 | tf_op jit(solution)/shard_map/ppermute | solution.py:40
  34.6 19.6 %collective-permute-start.14 = (bf16[384,896]{1,0:T(8,128)(2,1)S(1)}, bf16[384,896]{1,0:T(8,128)(2,1)S(1)}, u32[]{:S(2)}, u32[]{:S(2)}) collective-permute-start(bf16[384,896]{1,0:T(8,128)(2,1)S(1)} %shard_map.132), channel_id=1, source_target_pairs={{0,12},{1,13},{2,14},{3,15},{4,8},{5,9},{6,10},{7,11},{8,4},{9,5},... | collective-permute-start | bytes 2064392 | tf_op jit(solution)/shard_map/ppermute | solution.py:40
  40.4 18.4 %collective-permute-start.17 = (bf16[384,896]{1,0:T(8,128)(2,1)S(1)}, bf16[384,896]{1,0:T(8,128)(2,1)S(1)}, u32[]{:S(2)}, u32[]{:S(2)}) collective-permute-start(bf16[384,896]{1,0:T(8,128)(2,1)S(1)} %shard_map.133), channel_id=1, source_target_pairs={{0,4},{1,5},{2,6},{3,7},{4,0},{5,1},{6,2},{7,3},{8,12},{9,13},{10,... | collective-permute-start | bytes 2064392 | tf_op jit(solution)/shard_map/ppermute | solution.py:40
  50.1 14.6 %collective-permute-start.12 = (bf16[192,896]{1,0:T(8,128)(2,1)S(1)}, bf16[192,896]{1,0:T(8,128)(2,1)S(1)}, u32[]{:S(2)}, u32[]{:S(2)}) collective-permute-start(bf16[192,896]{1,0:T(8,128)(2,1)S(1)} %slice.108), channel_id=1, source_target_pairs={{0,4},{1,5},{2,6},{3,7},{4,0},{5,1},{6,2},{7,3},{8,12},{9,13},{10,... | collective-permute-start | bytes 1032200 | tf_op jit(solution)/shard_map/ppermute | solution.py:40
  54.4 10.8 %collective-permute-start.15 = (bf16[192,896]{1,0:T(8,128)(2,1)S(1)}, bf16[192,896]{1,0:T(8,128)(2,1)S(1)}, u32[]{:S(2)}, u32[]{:S(2)}) collective-permute-start(bf16[192,896]{1,0:T(8,128)(2,1)S(1)} %slice.107), channel_id=1, source_target_pairs={{0,2},{1,3},{2,0},{3,1},{4,6},{5,7},{6,4},{7,5},{8,10},{9,11},{10,... | collective-permute-start | bytes 1032200 | tf_op jit(solution)/shard_map/ppermute | solution.py:40
  59.0 8.6 %collective-permute-start.18 = (bf16[192,896]{1,0:T(8,128)(2,1)S(1)}, bf16[192,896]{1,0:T(8,128)(2,1)S(1)}, u32[]{:S(2)}, u32[]{:S(2)}) collective-permute-start(bf16[192,896]{1,0:T(8,128)(2,1)S(1)} %slice.106), channel_id=1, source_target_pairs={{0,12},{1,13},{2,14},{3,15},{4,8},{5,9},{6,10},{7,11},{8,4},{9,5},... | collective-permute-start | bytes 1032200 | tf_op jit(solution)/shard_map/ppermute | solution.py:40
  64.8 6.7 %collective-permute-start.13 = (bf16[96,896]{1,0:T(8,128)(2,1)S(1)}, bf16[96,896]{1,0:T(8,128)(2,1)S(1)}, u32[]{:S(2)}, u32[]{:S(2)}) collective-permute-start(bf16[96,896]{1,0:T(8,128)(2,1)S(1)} %slice.111), channel_id=1, source_target_pairs={{0,12},{1,13},{2,14},{3,15},{4,8},{5,9},{6,10},{7,11},{8,4},{9,5},... | collective-permute-start | bytes 516104 | tf_op jit(solution)/shard_map/ppermute | solution.py:40
  73.7 7.3 %collective-permute-start.20 = (bf16[96,896]{1,0:T(8,128)(2,1)S(1)}, bf16[96,896]{1,0:T(8,128)(2,1)S(1)}, u32[]{:S(2)}, u32[]{:S(2)}) collective-permute-start(bf16[96,896]{1,0:T(8,128)(2,1)S(1)} %get-tuple-element.110), channel_id=1, source_target_pairs={{0,2},{1,3},{2,0},{3,1},{4,6},{5,7},{6,4},{7,5},{8,10},{9,11},{10,... | collective-permute-start | bytes 516104 | tf_op jit(solution)/shard_map/ppermute | solution.py:40
  75.3 8.5 %collective-permute-start.24 = (bf16[96,896]{1,0:T(8,128)(2,1)S(1)}, bf16[96,896]{1,0:T(8,128)(2,1)S(1)}, u32[]{:S(2)}, u32[]{:S(2)}) collective-permute-start(bf16[96,896]{1,0:T(8,128)(2,1)S(1)} %get-tuple-element.109), channel_id=1, source_target_pairs={{0,12},{1,13},{2,14},{3,15},{4,8},{5,9},{6,10},{7,11},{8,4},{9,5},... | collective-permute-start | bytes 516104 | tf_op jit(solution)/shard_map/ppermute | solution.py:40
  79.2 7.3 %collective-permute-start.23 = (bf16[192,896]{1,0:T(8,128)(2,1)S(1)}, bf16[192,896]{1,0:T(8,128)(2,1)S(1)}, u32[]{:S(2)}, u32[]{:S(2)}) collective-permute-start(bf16[192,896]{1,0:T(8,128)(2,1)S(1)} %pad_maximum_fusion.5), channel_id=1, source_target_pairs={{0,2},{1,3},{2,0},{3,1},{4,6},{5,7},{6,4},{7,5},{8,10},{9,11},{10,... | collective-permute-start | bytes 1032200 | tf_op jit(solution)/shard_map/ppermute | solution.py:40
  81.1 11.5 %collective-permute-start.21 = (bf16[192,896]{1,0:T(8,128)(2,1)S(1)}, bf16[192,896]{1,0:T(8,128)(2,1)S(1)}, u32[]{:S(2)}, u32[]{:S(2)}) collective-permute-start(bf16[192,896]{1,0:T(8,128)(2,1)S(1)} %pad_maximum_fusion.4), channel_id=1, source_target_pairs={{0,12},{1,13},{2,14},{3,15},{4,8},{5,9},{6,10},{7,11},{8,4},{9,5},... | collective-permute-start | bytes 1032200 | tf_op jit(solution)/shard_map/ppermute | solution.py:40
  83.8 11.0 %collective-permute-start.25 = (bf16[192,896]{1,0:T(8,128)(2,1)S(1)}, bf16[192,896]{1,0:T(8,128)(2,1)S(1)}, u32[]{:S(2)}, u32[]{:S(2)}) collective-permute-start(bf16[192,896]{1,0:T(8,128)(2,1)S(1)} %pad_maximum_fusion.6), channel_id=1, source_target_pairs={{0,4},{1,5},{2,6},{3,7},{4,0},{5,1},{6,2},{7,3},{8,12},{9,13},{10,... | collective-permute-start | bytes 1032200 | tf_op jit(solution)/shard_map/ppermute | solution.py:40
  86.6 17.8 %collective-permute-start.27 = (bf16[384,896]{1,0:T(8,128)(2,1)S(1)}, bf16[384,896]{1,0:T(8,128)(2,1)S(1)}, u32[]{:S(2)}, u32[]{:S(2)}) collective-permute-start(bf16[384,896]{1,0:T(8,128)(2,1)S(1)} %pad_maximum_fusion.2.refs_1_), channel_id=1, source_target_pairs={{0,12},{1,13},{2,14},{3,15},{4,8},{5,9},{6,10},{7,11},{8,4},{9,5},... | collective-permute-start | bytes 2064392 | tf_op jit(solution)/shard_map/ppermute | solution.py:40
  92.6 13.2 %collective-permute-start.26 = (bf16[384,896]{1,0:T(8,128)(2,1)S(1)}, bf16[384,896]{1,0:T(8,128)(2,1)S(1)}, u32[]{:S(2)}, u32[]{:S(2)}) collective-permute-start(bf16[384,896]{1,0:T(8,128)(2,1)S(1)} %pad_maximum_fusion.1.refs_0_), channel_id=1, source_target_pairs={{0,4},{1,5},{2,6},{3,7},{4,0},{5,1},{6,2},{7,3},{8,12},{9,13},{10,... | collective-permute-start | bytes 2064392 | tf_op jit(solution)/shard_map/ppermute | solution.py:40
  94.9 11.0 %collective-permute-start.28 = (bf16[384,896]{1,0:T(8,128)(2,1)S(1)}, bf16[384,896]{1,0:T(8,128)(2,1)S(1)}, u32[]{:S(2)}, u32[]{:S(2)}) collective-permute-start(bf16[384,896]{1,0:T(8,128)(2,1)S(1)} %pad_maximum_fusion.3.refs_2_), channel_id=1, source_target_pairs={{0,2},{1,3},{2,0},{3,1},{4,6},{5,7},{6,4},{7,5},{8,10},{9,11},{10,... | collective-permute-start | bytes 2064392 | tf_op jit(solution)/shard_map/ppermute | solution.py:40
  116.7 10.7 %collective-permute-start.30 = (bf16[768,2688]{1,0:T(8,128)(2,1)S(1)}, bf16[768,2688]{1,0:T(8,128)(2,1)S(1)}, u32[]{:S(2)}, u32[]{:S(2)}) collective-permute-start(bf16[768,2688]{1,0:T(8,128)(2,1)S(1)} %shard_map.134.acts), channel_id=1, source_target_pairs={{0,1},{1,0},{2,3},{3,2},{4,5},{5,4},{6,7},{7,6},{8,9},{9,8},{10,11... | collective-permute-start | bytes 12386312 | tf_op jit(solution)/shard_map/ppermute | solution.py:35
  117.2 8.6 %collective-permute-start.31 = (bf16[2,96,512]{2,1,0:T(8,128)(2,1)S(1)}, bf16[2,96,512]{2,1,0:T(8,128)(2,1)S(1)}, u32[]{:S(2)}, u32[]{:S(2)}) collective-permute-start(bf16[2,96,512]{2,1,0:T(8,128)(2,1)S(1)} %get-tuple-element.79), channel_id=1, source_target_pairs={{0,16},{16,0},{32,48},{48,32},{64,80},{80,64},{96,112},{112,96},{1... | collective-permute-start | bytes 589832 | tf_op jit(solution)/shard_map/ppermute | solution.py:46
  117.5 8.3 %collective-permute-start.32 = (bf16[2,96,512]{2,1,0:T(8,128)(2,1)S(1)}, bf16[2,96,512]{2,1,0:T(8,128)(2,1)S(1)}, u32[]{:S(2)}, u32[]{:S(2)}) collective-permute-start(bf16[2,96,512]{2,1,0:T(8,128)(2,1)S(1)} %get-tuple-element.80), channel_id=1, source_target_pairs={{0,48},{16,32},{32,16},{48,0},{64,112},{80,96},{96,80},{112,64},{1... | collective-permute-start | bytes 589832 | tf_op jit(solution)/shard_map/ppermute | solution.py:46
  118.9 8.4 %collective-permute-start.33 = (bf16[2,96,512]{2,1,0:T(8,128)(2,1)S(1)}, bf16[2,96,512]{2,1,0:T(8,128)(2,1)S(1)}, u32[]{:S(2)}, u32[]{:S(2)}) collective-permute-start(bf16[2,96,512]{2,1,0:T(8,128)(2,1)S(1)} %get-tuple-element.81), channel_id=1, source_target_pairs={{0,64},{16,80},{32,96},{48,112},{64,0},{80,16},{96,32},{112,48},{1... | collective-permute-start | bytes 589832 | tf_op jit(solution)/shard_map/ppermute | solution.py:46
  127.4 13.3 %collective-permute-start.35 = (f32[2,96,512]{2,1,0:T(8,128)S(1)}, f32[2,96,512]{2,1,0:T(8,128)S(1)}, u32[]{:S(2)}, u32[]{:S(2)}) collective-permute-start(f32[2,96,512]{2,1,0:T(8,128)S(1)} %get-tuple-element.95), channel_id=1, source_target_pairs={{0,64},{16,80},{32,96},{48,112},{64,0},{80,16},{96,32},{112,48},{1... | collective-permute-start | bytes 1179656 | tf_op jit(solution)/shard_map/ppermute | solution.py:46
  129.5 9.2 %collective-permute-start.34 = (bf16[2,96,512]{2,1,0:T(8,128)(2,1)S(1)}, bf16[2,96,512]{2,1,0:T(8,128)(2,1)S(1)}, u32[]{:S(2)}, u32[]{:S(2)}) collective-permute-start(bf16[2,96,512]{2,1,0:T(8,128)(2,1)S(1)} %get-tuple-element.94), channel_id=1, source_target_pairs={{0,32},{16,48},{32,0},{48,16},{64,96},{80,112},{96,64},{112,80},{1... | collective-permute-start | bytes 589832 | tf_op jit(solution)/shard_map/ppermute | solution.py:46
  131.7 8.4 %collective-permute-start.36 = (bf16[2,96,512]{2,1,0:T(8,128)(2,1)S(1)}, bf16[2,96,512]{2,1,0:T(8,128)(2,1)S(1)}, u32[]{:S(2)}, u32[]{:S(2)}) collective-permute-start(bf16[2,96,512]{2,1,0:T(8,128)(2,1)S(1)} %get-tuple-element.96), channel_id=1, source_target_pairs={{0,16},{16,0},{32,48},{48,32},{64,80},{80,64},{96,112},{112,96},{1... | collective-permute-start | bytes 589832 | tf_op jit(solution)/shard_map/ppermute | solution.py:46
  132.5 8.2 %collective-permute-start.37 = (bf16[2,96,512]{2,1,0:T(8,128)(2,1)S(1)}, bf16[2,96,512]{2,1,0:T(8,128)(2,1)S(1)}, u32[]{:S(2)}, u32[]{:S(2)}) collective-permute-start(bf16[2,96,512]{2,1,0:T(8,128)(2,1)S(1)} %get-tuple-element.97), channel_id=1, source_target_pairs={{0,48},{16,32},{32,16},{48,0},{64,112},{80,96},{96,80},{112,64},{1... | collective-permute-start | bytes 589832 | tf_op jit(solution)/shard_map/ppermute | solution.py:46
  (9 other events, 35.7 us)
